TPU v7x, 32 devices: a whole 2x2x4 slice. The times are simulated.
32 devices in a mesh: rep: 2 (over core), shard: 16 (over z, y, x).
Axes of the slice: x: 2, y: 2, z: 4, core: 2. Of those that a mesh axis runs over, the one named last changes fastest.
Arguments:
- noisy: float32 [32, 4, 32, 32], P(('rep', 'shard')), may hold values from -6 to 6
- timesteps: int32 [32], P(('rep', 'shard')), may hold values from 0 to 999
- labels: int32 [32], P(('rep', 'shard')), may hold values from 0 to 999
- noise: float32 [32, 4, 32, 32], P(('rep', 'shard')), may hold values from -12 to 12
- block_in: float32 [1, 1024, 14336], P(None, 'shard'), may hold values from -3 to 3
- block_in_first: float32 [1, 1024, 14336], P(None, 'shard'), may hold values from -4.5776367e-05 to 4.5776367e-05
- block_in_second: float32 [1, 1024, 14336], P(None, 'shard'), may hold values from 8.569345e-12 to 3.427738e-11
- block_out: float32 [1, 4096, 1024], P(None, 'shard'), may hold values from -0.09375 to 0.09375
- block_out_first: float32 [1, 4096, 1024], P(None, 'shard'), may hold values from -4.5776367e-05 to 4.5776367e-05
- block_out_second: float32 [1, 4096, 1024], P(None, 'shard'), may hold values from 8.569345e-12 to 3.427738e-11
- entry_table: float32 [1272, 1024], P(None, 'shard'), may hold values from -1.5 to 1.5
- entry_first: float32 [1272, 1024], P(None, 'shard'), may hold values from -0.0014648438 to 0.0014648438
- entry_second: float32 [1272, 1024], P(None, 'shard'), may hold values from 1.071168e-08 to 4.284672e-08
- exit_proj: float32 [1024, 3088], P('shard'), may hold values from -0.1875 to 0.1875
- exit_first: float32 [1024, 3088], P('shard'), may hold values from -0.0014648438 to 0.0014648438
- exit_second: float32 [1024, 3088], P('shard'), may hold values from 1.071168e-08 to 4.284672e-08
Outputs:
- loss: float32 [], replicated
- grad_norm: float32 [], replicated
- block_in_new: float32 [1, 1024, 14336], P(None, 'shard')
- block_in_first_new: float32 [1, 1024, 14336], P(None, 'shard')
- block_in_second_new: float32 [1, 1024, 14336], P(None, 'shard')
- block_in_low: bfloat16 [1, 1024, 14336], P(None, 'shard')
- block_out_new: float32 [1, 4096, 1024], P(None, 'shard')
- block_out_first_new: float32 [1, 4096, 1024], P(None, 'shard')
- block_out_second_new: float32 [1, 4096, 1024], P(None, 'shard')
- block_out_low: bfloat16 [1, 4096, 1024], P(None, 'shard')
- entry_new: float32 [1272, 1024], P(None, 'shard')
- entry_first_new: float32 [1272, 1024], P(None, 'shard')
- entry_second_new: float32 [1272, 1024], P(None, 'shard')
- entry_low: bfloat16 [1272, 1024], P(None, 'shard')
- exit_new: float32 [1024, 3088], P('shard')
- exit_first_new: float32 [1024, 3088], P('shard')
- exit_second_new: float32 [1024, 3088], P('shard')
- exit_low: bfloat16 [1024, 3088], P('shard')
All inputs are finite; a program needn't handle non-finite values.
Results may differ from a plain program's by a relative error of at most 0.017.
Values may be sent and summed in bfloat16 or wider, within the bound.
A program may use at most 384 MiB of HBM per device.

v0:
```python
import jax
import jax.numpy as jnp
from jax import lax
from jax.sharding import PartitionSpec as P

D = 1024
HEADS = 16
PATCH = 2
NCLS = 1000
FREQ = 256
STEP = 10
PDIM = 16


clip_limit = 0.5
rate_main = 0.02
rate_edge = 0.1
decay_rate = 0.01
adam_eps = 1e-08
highest = lax.Precision.HIGHEST


def lowered(value):
    return value.astype(jnp.bfloat16)


def product(left, right):
    return jnp.dot(left, right, preferred_element_type=jnp.float32)


def product_tn(left, right):
    return lax.dot_general(
        left, right, (((0,), (0,)), ((), ())), preferred_element_type=jnp.float32
    )


def product_nt(left, right):
    return lax.dot_general(
        left, right, (((1,), (1,)), ((), ())), preferred_element_type=jnp.float32
    )


def patchify(image, patch):
    batch, chans, height, width = image.shape
    grid = height // patch
    parts = image.reshape(batch, chans, grid, patch, grid, patch)
    parts = parts.transpose(0, 2, 4, 3, 5, 1)
    return parts.reshape(batch, grid * grid, patch * patch * chans)


def position_table(grid, width):
    quarter = width // 4
    omega = 1.0 / 10000.0 ** (jnp.arange(quarter, dtype=jnp.float32) / quarter)
    index = jnp.arange(grid * grid)
    row_pos = (index // grid).astype(jnp.float32)[:, None] * omega[None, :]
    col_pos = (index % grid).astype(jnp.float32)[:, None] * omega[None, :]
    return jnp.concatenate(
        [jnp.sin(col_pos), jnp.cos(col_pos), jnp.sin(row_pos), jnp.cos(row_pos)], axis=1
    )


def time_features(steps, size):
    half = size // 2
    freqs = jnp.exp(-jnp.log(10000.0) * jnp.arange(half, dtype=jnp.float32) / half)
    angles = steps.astype(jnp.float32)[:, None] * freqs[None, :]
    return jnp.concatenate([jnp.cos(angles), jnp.sin(angles)], axis=1)


def modulate(x, shift, scale):
    centered = x - jnp.mean(x, axis=-1, keepdims=True)
    var = jnp.mean(centered * centered, axis=-1, keepdims=True)
    normed = centered * lax.rsqrt(var + 1e-06)
    return normed * (1.0 + scale[:, None, :]) + shift[:, None, :]


def gelu_tanh(value):
    return jax.nn.gelu(value, approximate=True)


def adam_step(weight, first, second, grad, factor, rate):
    clipped = grad * factor
    first_new = 0.5 * first + 0.5 * clipped
    second_new = 0.5 * second + 0.5 * clipped * clipped
    corr = 1.0 - 0.5**STEP
    update = first_new / corr / (jnp.sqrt(second_new / corr) + adam_eps) + decay_rate * weight
    weight_new = weight - rate * update
    return (weight_new, first_new, second_new, weight_new.astype(jnp.bfloat16))


def layer_parts(x, cond_low, w_in, w_out):
    width = x.shape[-1]
    batch, seq = (x.shape[0], x.shape[1])
    size = width // HEADS
    mod = product(cond_low, w_in[:, : 6 * width])
    shift_a, scale_a, gate_a, shift_b, scale_b, gate_b = jnp.split(mod, 6, axis=-1)
    attn_in = lowered(modulate(x, shift_a, scale_a))
    qkv = lowered(
        jnp.einsum(
            "bsd,de->bse",
            attn_in,
            w_in[:, 6 * width : 9 * width],
            preferred_element_type=jnp.float32,
        )
    )
    query = qkv[..., :width].reshape(batch, seq, HEADS, size)
    keys = qkv[..., width : 2 * width].reshape(batch, seq, HEADS, size)
    values = qkv[..., 2 * width :].reshape(batch, seq, HEADS, size)
    scores = jnp.einsum(
        "bqhd,bkhd->bhqk", query, keys, preferred_element_type=jnp.float32
    ) * size ** (-0.5)
    weights = jax.nn.softmax(scores, axis=-1)
    weights_low = lowered(weights)
    mixed = lowered(
        jnp.einsum("bhqk,bkhd->bqhd", weights_low, values, preferred_element_type=jnp.float32)
    ).reshape(batch, seq, width)
    attn_out = jnp.einsum(
        "bsd,de->bse", mixed, w_in[:, 9 * width : 10 * width], preferred_element_type=jnp.float32
    )
    resid = x + gate_a[:, None, :] * attn_out
    mlp_in = lowered(modulate(resid, shift_b, scale_b))
    hidden = jnp.einsum(
        "bsd,df->bsf", mlp_in, w_in[:, 10 * width :], preferred_element_type=jnp.float32
    )
    active = lowered(gelu_tanh(hidden))
    mlp_out = jnp.einsum("bsf,fd->bsd", active, w_out, preferred_element_type=jnp.float32)
    result = resid + gate_b[:, None, :] * mlp_out
    return dict(
        mods=(shift_a, scale_a, gate_a, shift_b, scale_b, gate_b),
        attn_in=attn_in,
        query=query,
        keys=keys,
        values=values,
        weights=weights,
        weights_low=weights_low,
        mixed=mixed,
        attn_out=attn_out,
        resid=resid,
        mlp_in=mlp_in,
        hidden=hidden,
        active=active,
        mlp_out=mlp_out,
        result=result,
    )


def layer_back(x, cond_low, w_in, w_out, parts, grad_out, grad_cond):
    width = x.shape[-1]
    batch, seq = (x.shape[0], x.shape[1])
    size = width // HEADS
    shift_a, scale_a, gate_a, shift_b, scale_b, gate_b = parts["mods"]
    d_gate_b = jnp.sum(grad_out * parts["mlp_out"], axis=1)
    d_mlp_out = lowered(grad_out * gate_b[:, None, :])
    g_fc2 = jnp.einsum(
        "bsf,bsd->fd", parts["active"], d_mlp_out, preferred_element_type=jnp.float32
    )
    d_active = jnp.einsum("bsd,fd->bsf", d_mlp_out, w_out, preferred_element_type=jnp.float32)
    _, gelu_pull = jax.vjp(gelu_tanh, parts["hidden"])
    d_hidden = lowered(gelu_pull(d_active)[0])
    g_fc1 = jnp.einsum("bsd,bsf->df", parts["mlp_in"], d_hidden, preferred_element_type=jnp.float32)
    d_mlp_in = jnp.einsum(
        "bsf,df->bsd", d_hidden, w_in[:, 10 * width :], preferred_element_type=jnp.float32
    )
    _, norm_pull = jax.vjp(modulate, parts["resid"], shift_b, scale_b)
    d_resid, d_shift_b, d_scale_b = norm_pull(d_mlp_in)
    d_resid = d_resid + grad_out
    d_gate_a = jnp.sum(d_resid * parts["attn_out"], axis=1)
    d_attn_out = lowered(d_resid * gate_a[:, None, :])
    g_proj = jnp.einsum(
        "bsd,bse->de", parts["mixed"], d_attn_out, preferred_element_type=jnp.float32
    )
    d_mixed = lowered(
        jnp.einsum(
            "bse,de->bsd",
            d_attn_out,
            w_in[:, 9 * width : 10 * width],
            preferred_element_type=jnp.float32,
        )
    ).reshape(batch, seq, HEADS, size)
    d_probs = jnp.einsum(
        "bqhd,bkhd->bhqk", d_mixed, parts["values"], preferred_element_type=jnp.float32
    )
    d_values = jnp.einsum(
        "bhqk,bqhd->bkhd", parts["weights_low"], d_mixed, preferred_element_type=jnp.float32
    )
    weights = parts["weights"]
    d_scores = weights * (d_probs - jnp.sum(d_probs * weights, axis=-1, keepdims=True))
    d_scaled = lowered(d_scores * size ** (-0.5))
    d_query = jnp.einsum(
        "bhqk,bkhd->bqhd", d_scaled, parts["keys"], preferred_element_type=jnp.float32
    )
    d_keys = jnp.einsum(
        "bhqk,bqhd->bkhd", d_scaled, parts["query"], preferred_element_type=jnp.float32
    )
    d_qkv = lowered(
        jnp.concatenate(
            [
                d_query.reshape(batch, seq, width),
                d_keys.reshape(batch, seq, width),
                d_values.reshape(batch, seq, width),
            ],
            axis=-1,
        )
    )
    g_qkv = jnp.einsum("bsd,bse->de", parts["attn_in"], d_qkv, preferred_element_type=jnp.float32)
    d_attn_in = jnp.einsum(
        "bse,de->bsd", d_qkv, w_in[:, 6 * width : 9 * width], preferred_element_type=jnp.float32
    )
    _, first_pull = jax.vjp(modulate, x, shift_a, scale_a)
    d_x, d_shift_a, d_scale_a = first_pull(d_attn_in)
    d_x = d_x + d_resid
    d_mod = lowered(
        jnp.concatenate([d_shift_a, d_scale_a, d_gate_a, d_shift_b, d_scale_b, d_gate_b], axis=-1)
    )
    g_mod = product_tn(cond_low, d_mod)
    grad_cond = grad_cond + product_nt(d_mod, w_in[:, : 6 * width])
    g_in = jnp.concatenate([g_mod, g_qkv, g_proj, g_fc1], axis=1)
    return (d_x, grad_cond, g_in, g_fc2)


def local(
    noisy,
    timesteps,
    labels,
    noise,
    block_in,
    block_in_first,
    block_in_second,
    block_out,
    block_out_first,
    block_out_second,
    entry_table,
    entry_first,
    entry_second,
    exit_proj,
    exit_first,
    exit_second,
):
    layers = block_in.shape[0]
    entry_all, exit_all = (
        lax.all_gather(lowered(entry_table), "shard", axis=1, tiled=True),
        lax.all_gather(lowered(exit_proj), "shard", axis=0, tiled=True),
    )
    w_patch = entry_all[:PDIM]
    w_label = entry_all[PDIM : PDIM + NCLS]
    w_time = entry_all[PDIM + NCLS :]
    w_time2 = exit_all[:, :D]
    w_final = exit_all[:, D : 3 * D]
    w_output = exit_all[:, 3 * D :]
    patches = lowered(patchify(noisy, PATCH))
    target = patchify(noise, PATCH)
    seq = patches.shape[1]
    x = (
        jnp.einsum("bsp,pd->bsd", patches, w_patch, preferred_element_type=jnp.float32)
        + position_table(noisy.shape[-1] // PATCH, D)[None]
    )
    femb = lowered(time_features(timesteps, FREQ))
    t_hidden = product(femb, w_time)
    t_act = lowered(jax.nn.silu(t_hidden))
    temb = product(t_act, w_time2)
    onehot = (labels[:, None] == jnp.arange(NCLS)[None, :]).astype(jnp.float32)
    cond = temb + jnp.dot(onehot, w_label.astype(jnp.float32), precision=highest)
    cond_low = lowered(jax.nn.silu(cond))
    layer = 0
    w_in_all = lax.all_gather(lowered(block_in[layer]), "shard", axis=0, tiled=True)
    w_out_all = lax.all_gather(lowered(block_out[layer]), "shard", axis=0, tiled=True)
    inputs = [x]
    parts = layer_parts(x, cond_low, w_in_all, w_out_all)
    saved = [parts]
    x = parts["result"]
    final_mod = product(cond_low, w_final)
    shift_f, scale_f = jnp.split(final_mod, 2, axis=-1)
    final_in = lowered(modulate(x, shift_f, scale_f))
    pred = jnp.einsum("bsd,dp->bsp", final_in, w_output, preferred_element_type=jnp.float32)
    error = pred - target
    loss_part = jnp.sum(error * error) / (seq * PDIM)
    d_pred = lowered(2.0 * error / (seq * PDIM))
    g_output = jnp.einsum("bsd,bsp->dp", final_in, d_pred, preferred_element_type=jnp.float32)
    d_final_in = jnp.einsum("bsp,dp->bsd", d_pred, w_output, preferred_element_type=jnp.float32)
    _, final_pull = jax.vjp(modulate, x, shift_f, scale_f)
    d_x, d_shift_f, d_scale_f = final_pull(d_final_in)
    d_fmod = lowered(jnp.concatenate([d_shift_f, d_scale_f], axis=-1))
    g_final = product_tn(cond_low, d_fmod)
    grad_cond = product_nt(d_fmod, w_final)
    shards_in = [None] * layers
    shards_out = [None] * layers
    for layer in reversed(range(layers)):
        w_in_all, w_out_all = (
            lax.all_gather(lowered(block_in[layer]), "shard", axis=0, tiled=True),
            lax.all_gather(lowered(block_out[layer]), "shard", axis=0, tiled=True),
        )
        d_x, grad_cond, g_in, g_fc2 = layer_back(
            inputs[layer], cond_low, w_in_all, w_out_all, saved[layer], d_x, grad_cond
        )
        shards_in[layer], shards_out[layer] = (
            lax.psum_scatter(g_in, "shard", scatter_dimension=0, tiled=True),
            lax.psum_scatter(g_fc2, "shard", scatter_dimension=0, tiled=True),
        )
    _, silu_pull = jax.vjp(jax.nn.silu, cond)
    d_cond = silu_pull(grad_cond)[0]
    g_label = jnp.dot(onehot.T, d_cond, precision=highest)
    d_temb = lowered(d_cond)
    g_time2 = product_tn(t_act, d_temb)
    d_tact = product_nt(d_temb, w_time2)
    _, time_pull = jax.vjp(jax.nn.silu, t_hidden)
    d_thidden = lowered(time_pull(d_tact)[0])
    g_time = product_tn(femb, d_thidden)
    g_patch = jnp.einsum("bsp,bsd->pd", patches, lowered(d_x), preferred_element_type=jnp.float32)
    g_entry = jnp.concatenate([g_patch, g_label, g_time], axis=0)
    g_exit = jnp.concatenate([g_time2, g_final, g_output], axis=1)
    share_entry, share_exit = (
        lax.psum_scatter(g_entry, "shard", scatter_dimension=1, tiled=True),
        lax.psum_scatter(g_exit, "shard", scatter_dimension=0, tiled=True),
    )
    grads = (
        lax.psum(jnp.stack(shards_in).astype(jnp.bfloat16), "rep").astype(jnp.float32),
        lax.psum(jnp.stack(shards_out).astype(jnp.bfloat16), "rep").astype(jnp.float32),
        lax.psum(share_entry.astype(jnp.bfloat16), "rep").astype(jnp.float32),
        lax.psum(share_exit.astype(jnp.bfloat16), "rep").astype(jnp.float32),
    )
    squares = (
        jnp.sum(grads[0] * grads[0])
        + jnp.sum(grads[1] * grads[1])
        + jnp.sum(grads[2] * grads[2])
        + jnp.sum(grads[3] * grads[3])
    )
    loss = lax.psum(loss_part, ("rep", "shard"))
    norm_sq = lax.psum(squares, "shard")
    grad_norm = jnp.sqrt(norm_sq)
    factor = clip_limit / jnp.maximum(grad_norm, clip_limit)
    bi_w, bi_m, bi_v, bi_l = adam_step(
        block_in, block_in_first, block_in_second, grads[0], factor, rate_main
    )
    bo_w, bo_m, bo_v, bo_l = adam_step(
        block_out, block_out_first, block_out_second, grads[1], factor, rate_main
    )
    en_w, en_m, en_v, en_l = adam_step(
        entry_table, entry_first, entry_second, grads[2], factor, rate_edge
    )
    ex_w, ex_m, ex_v, ex_l = adam_step(
        exit_proj, exit_first, exit_second, grads[3], factor, rate_main
    )
    return (
        loss,
        grad_norm,
        bi_w,
        bi_m,
        bi_v,
        bi_l,
        bo_w,
        bo_m,
        bo_v,
        bo_l,
        en_w,
        en_m,
        en_v,
        en_l,
        ex_w,
        ex_m,
        ex_v,
        ex_l,
    )


def solution(mesh):
    in_specs = (
        P(("rep", "shard"), None, None, None),
        P(("rep", "shard")),
        P(("rep", "shard")),
        P(("rep", "shard"), None, None, None),
        P(None, "shard", None),
        P(None, "shard", None),
        P(None, "shard", None),
        P(None, "shard", None),
        P(None, "shard", None),
        P(None, "shard", None),
        P(None, "shard"),
        P(None, "shard"),
        P(None, "shard"),
        P("shard", None),
        P("shard", None),
        P("shard", None),
    )
    out_specs = (
        P(),
        P(),
        P(None, "shard", None),
        P(None, "shard", None),
        P(None, "shard", None),
        P(None, "shard", None),
        P(None, "shard", None),
        P(None, "shard", None),
        P(None, "shard", None),
        P(None, "shard", None),
        P(None, "shard"),
        P(None, "shard"),
        P(None, "shard"),
        P(None, "shard"),
        P("shard", None),
        P("shard", None),
        P("shard", None),
        P("shard", None),
    )
    return jax.shard_map(local, mesh=mesh, in_specs=in_specs, out_specs=out_specs, check_vma=False)
```

profile of v0, /device:TPU:0, one launch (start us, length us, event | category | flops | bytes accessed | tf_op | source)
XLA Modules:
  0.0 2781.3 jit_solution(10314342144201459114)
XLA Ops:
  20.8 57.2 %all-gather.7.cloned.1.call-done = bf16[1272,1024]{0,1:T(8,128)(2,1)} async-done(((bf16[1272,64]{0,1:T(8,128)(2,1)}), bf16[1272,1024]{0,1:T(8,128)(2,1)}) %all-gather.7.cloned.1.call-update) | async-done | bytes 2605072 | tf_op jit(solution)/shard_map/all_gather | solution.py:240
  83.7 93.3 %all-gather.9.cloned.1.call-done = bf16[1024,3088]{1,0:T(8,128)(2,1)} async-done(((bf16[64,3088]{1,0:T(8,128)(2,1)}), bf16[1024,3088]{1,0:T(8,128)(2,1)}) %all-gather.9.cloned.1.call-update) | async-done | bytes 6324240 | tf_op jit(solution)/shard_map/all_gather | solution.py:241
  181.8 307.9 %all-gather.11.cloned.1.call-done = bf16[1,1024,14336]{2,1,0:T(8,128)(2,1)} async-done(((bf16[1,64,14336]{2,1,0:T(8,128)(2,1)}), bf16[1,1024,14336]{2,1,0:T(8,128)(2,1)}) %all-gather.11.cloned.1.call-update) | async-done | bytes 29360144 | tf_op jit(solution)/shard_map/all_gather | solution.py:264
  489.7 6.1 fusion.4
  512.0 7.8 fusion.12
  519.8 84.2 %all-gather.13.cloned.1.call-done = bf16[1,4096,1024]{2,1,0:T(8,128)(2,1)} async-done(((bf16[1,256,1024]{2,1,0:T(8,128)(2,1)}), bf16[1,4096,1024]{2,1,0:T(8,128)(2,1)}) %all-gather.13.cloned.1.call-update) | async-done | bytes 8388624 | tf_op jit(solution)/shard_map/all_gather | solution.py:265
  604.0 7.5 fusion.134
  616.2 8.5 fusion.24
  643.2 8.7 fusion.64
  652.0 8.7 fusion.67
  666.6 6.9 fusion.2
  680.2 7.0 concatenate.59
  694.8 11.2 fusion.116
  710.2 6.6 fusion.79
  716.7 8.2 fusion.117
  725.0 11.6 broadcast_multiply_fusion
  736.6 38.6 %pad_maximum_fusion = f32[1024,14336]{1,0:T(8,128)} fusion(f32[1024,4096]{1,0:T(8,128)} %fusion.117, f32[1024,1024]{1,0:T(8,128)} %fusion.91, f32[1024,3072]{1,0:T(8,128)} %fusion.79, f32[1024,6144]{1,0:T(8,128)} %broadcast_multiply_fusion), kind=kLoop, calls=%fused_computation.2 | loop fusion | flops 44040192 | bytes 117440512 | tf_op jit(solution)/shard_map/concatenate | solution.py:216
  775.3 25.8 reduce-scatter.9.cloned.1.call-done
  802.7 274.1 %reduce-scatter.11.cloned.1.call-done = f32[64,3088]{1,0:T(8,128)} async-done(((f32[1024,3088]{1,0:T(8,128)}), f32[64,3088]{1,0:T(8,128)}) %reduce-scatter.11.cloned.1.call-update) | async-done | bytes 790544 | tf_op jit(solution)/shard_map/reduce_scatter | solution.py:312
  1078.8 351.7 %reduce-scatter.7.cloned.1.call-done = f32[256,1024]{1,0:T(8,128)} async-done(((f32[4096,1024]{1,0:T(8,128)}), f32[256,1024]{1,0:T(8,128)}) %reduce-scatter.7.cloned.1.call-update) | async-done | bytes 1048592 | tf_op jit(solution)/shard_map/reduce_scatter | solution.py:296
  1432.6 1197.2 %reduce-scatter.5.cloned.1.call-done = f32[64,14336]{1,0:T(8,128)} async-done(((f32[1024,14336]{1,0:T(8,128)}), f32[64,14336]{1,0:T(8,128)}) %reduce-scatter.5.cloned.1.call-update) | async-done | bytes 3670032 | tf_op jit(solution)/shard_map/reduce_scatter | solution.py:295
  2634.0 29.1 %all-reduce.3.cloned.1.call-done = (bf16[1,64,14336]{2,1,0:T(8,128)(2,1)}, bf16[1,256,1024]{2,1,0:T(8,128)(2,1)}, bf16[1272,64]{0,1:T(8,128)(2,1)}, bf16[64,3088]{1,0:T(8,128)(2,1)}) async-done(((bf16[1,64,14336]{2,1,0:T(8,128)(2,1)}, bf16[1,256,1024]{2,1,0:T(8,128)(2,1)}, bf16[1272,64]{0,1:T(8,128)(2,1)}, bf16[64,3088]{1,0:T(8,128)(2,1)}), (bf16[1,64,14336]{2,1,0:T(8,128)(2,1)}, ...) | async-done | bytes 2917392 | tf_op jit(solution)/shard_map/psum | solution.py:315
  2674.2 40.6 %psum.42 = f32[]{:T(128)} all-reduce(f32[]{:T(128)S(6)} %div.178), channel_id=1, replica_groups=mesh['rep'=2,'shard'=16] {'rep','shard'}, use_global_device_ids=true, to_apply=%region_9.10 | all-reduce | flops 1 | bytes 8 | tf_op jit(solution)/shard_map/psum | solution.py:326
  2714.8 41.5 %psum.47 = f32[]{:T(128)} all-reduce(f32[]{:T(128)S(6)} %add.294), channel_id=1, replica_groups=mesh['rep'=2,'shard'=16] {'shard'}, use_global_device_ids=true, to_apply=%region_37.38 | all-reduce | flops 1 | bytes 8 | tf_op jit(solution)/shard_map/psum | solution.py:327
  (182 shorter events, 119.8 us)
Async XLA Ops:
  7.2 70.8 %all-gather.7.cloned.1.call-start = ((), (), s32[]{:S(2)}) async-start(), calls=%async_computation.4 | async-start | bytes 2785280 | tf_op jit(solution)/shard_map/all_gather | solution.py:240
  8.9 168.0 %all-gather.9.cloned.1.call-start = ((), (), s32[]{:S(2)}) async-start(), calls=%async_computation.5 | async-start | bytes 6963200 | tf_op jit(solution)/shard_map/all_gather | solution.py:241
  11.0 6.9 copy-start.26
  11.0 478.7 %all-gather.11.cloned.1.call-start = ((), (), s32[]{:S(2)}) async-start(), calls=%async_computation.10 | async-start | bytes 31195136 | tf_op jit(solution)/shard_map/all_gather | solution.py:264
  14.6 589.4 %all-gather.13.cloned.1.call-start = ((), (), s32[]{:S(2)}) async-start(), calls=%async_computation.11 | async-start | bytes 8912896 | tf_op jit(solution)/shard_map/all_gather | solution.py:265
  15.5 785.6 %reduce-scatter.9.cloned.1.call-start = ((), (), s32[]{:S(2)}) async-start(), calls=%async_computation.8 | async-start | bytes 5570560 | tf_op jit(solution)/shard_map/reduce_scatter | solution.py:311
  500.8 6.8 copy-start.23
  612.0 12.7 copy-start.4
  616.1 14.9 copy-start.1
  666.1 7.4 slice-start
  666.6 6.9 slice-start.1
  687.3 389.5 %reduce-scatter.11.cloned.1.call-start = ((), (), s32[]{:S(2)}) async-start(), calls=%async_computation.9 | async-start | bytes 13926400 | tf_op jit(solution)/shard_map/reduce_scatter | solution.py:312
  694.7 735.7 %reduce-scatter.7.cloned.1.call-start = ((), (), s32[]{:S(2)}) async-start(), calls=%async_computation.7 | async-start | bytes 17825792 | tf_op jit(solution)/shard_map/reduce_scatter | solution.py:296
  706.0 1923.8 %reduce-scatter.5.cloned.1.call-start = ((), (), s32[]{:S(2)}) async-start(), calls=%async_computation.6 | async-start | bytes 62390272 | tf_op jit(solution)/shard_map/reduce_scatter | solution.py:295
  710.2 6.6 copy-start.17
  775.3 1887.8 %all-reduce.3.cloned.1.call-start = ((), (), s32[]{:S(2)}) async-start(), calls=%async_computation.12 | async-start | bytes 5865472 | tf_op jit(solution)/shard_map/psum | solution.py:315
  2633.2 123.8 %copy-start.19 = (f32[1272,64]{0,1:T(8,128)S(1)}, f32[1272,64]{0,1:T(8,128)}, u32[]{:S(2)}) copy-start(f32[1272,64]{0,1:T(8,128)} %param.26) | copy-start | bytes 976900
  2633.2 123.8 %copy-start.25 = (f32[1272,64]{0,1:T(8,128)S(1)}, f32[1272,64]{0,1:T(8,128)}, u32[]{:S(2)}) copy-start(f32[1272,64]{0,1:T(8,128)} %param.27) | copy-start | bytes 976900
  2633.2 126.1 %copy-start.10 = (f32[64,3088]{1,0:T(8,128)S(1)}, f32[64,3088]{1,0:T(8,128)}, u32[]{:S(2)}) copy-start(f32[64,3088]{1,0:T(8,128)} %param.29) | copy-start | bytes 2371588
  2663.1 96.2 %copy-start.18 = (bf16[64,3088]{1,0:T(8,128)(2,1)S(1)}, bf16[64,3088]{1,0:T(8,128)(2,1)}, u32[]{:S(2)}) copy-start(bf16[64,3088]{1,0:T(8,128)(2,1)} %get-tuple-element.30) | copy-start | bytes 1185796
  2671.5 91.4 %copy-start.7 = (f32[1,256,1024]{2,1,0:T(8,128)S(1)}, f32[1,256,1024]{2,1,0:T(8,128)}, u32[]{:S(2)}) copy-start(f32[1,256,1024]{2,1,0:T(8,128)} %param.23) | copy-start | bytes 3145732
  2671.5 91.4 %copy-start.15 = (bf16[1,256,1024]{2,1,0:T(8,128)(2,1)S(1)}, bf16[1,256,1024]{2,1,0:T(8,128)(2,1)}, u32[]{:S(2)}) copy-start(bf16[1,256,1024]{2,1,0:T(8,128)(2,1)} %get-tuple-element.28) | copy-start | bytes 1572868
  2759.3 7.9 copy-start.8
  2759.3 7.9 copy-start.9
  (15 other events, 70.0 us)
Sparse Core Ops, SparseCore 0:
  11.3 66.6 all-gather.6
  81.3 95.6 all-gather.8
  180.3 309.4 all-gather.10
  492.9 111.0 all-gather.12
  687.4 113.6 reduce-scatter.8
  803.3 273.5 reduce-scatter.10
  1079.1 351.3 reduce-scatter.6
  1432.8 1196.8 reduce-scatter.4
  2634.0 28.9 all-reduce.2
where the time goes:
time: 2790 us; the launch traced here: 2780 us
  waiting for transfers between devices  2420 us (87%)
  matrix products  137 us (5%)
  other arithmetic  106 us (4%)
  blocking collectives  82 us (3%)
    reduce_scatter x1, waiting for transfers between devices, local(): lax.psum_scatter(g_in, 'shard', scatter_dimension=0, tiled=True)  1200 us
    reduce_scatter x1, waiting for transfers between devices, local(): lax.psum_scatter(g_fc2, 'shard', scatter_dimension=0, tiled=True)  352 us
    all_gather x1, waiting for transfers between devices, local(): lax.all_gather(lowered(block_in[layer]), 'shard', axis=0, tiled=True)  308 us
    reduce_scatter x1, waiting for transfers between devices, local(): lax.psum_scatter(g_exit, 'shard', scatter_dimension=0, tiled=True)  274 us
    all_gather x1, waiting for transfers between devices, local(): lax.all_gather(lowered(exit_proj), 'shard', axis=0, tiled=True)  93.3 us
    all_gather x1, waiting for transfers between devices, local(): lax.all_gather(lowered(block_out[layer]), 'shard', axis=0, tiled=True)  84.2 us
    all_gather x1, waiting for transfers between devices, local(): lax.all_gather(lowered(entry_table), 'shard', axis=1, tiled=True)  57.2 us
  transfers between devices with their start and end apart: 9, of which 9 were waited for; matrix products, arithmetic and copies ran while one was open for 5% of the time, Pallas kernels for 0%

commit v1 on v0

--- a/solution.py
+++ b/solution.py
@@ -1,6 +1,8 @@
 import jax
 import jax.numpy as jnp
 from jax import lax
+from jax.experimental import pallas as pl
+from jax.experimental.pallas import tpu as pltpu
 from jax.sharding import PartitionSpec as P
 
 D = 1024
@@ -361,7 +363,915 @@
     )
 
 
+BF = jnp.bfloat16
+F32 = jnp.float32
+MESH = pl.DeviceIdType.MESH
+TOK = 256
+LANES = 128
+CHUNKS = 12
+ORDER = (8, 9, 10, 11, 4, 5, 6, 7, 3, 0, 1, 2)
+
+
+def dot_nn(left, right):
+    return lax.dot_general(left, right, (((1,), (0,)), ((), ())), preferred_element_type=F32)
+
+
+def dot_nt(left, right):
+    return lax.dot_general(left, right, (((1,), (1,)), ((), ())), preferred_element_type=F32)
+
+
+def dot_tn(left, right):
+    return lax.dot_general(left, right, (((0,), (0,)), ((), ())), preferred_element_type=F32)
+
+
+def sigmoid(value):
+    return 1.0 / (1.0 + jnp.exp(-value))
+
+
+def silu_slope(value):
+    gate = sigmoid(value)
+    return gate * (1.0 + value * (1.0 - gate))
+
+
+def normed(x):
+    centered = x - jnp.mean(x, axis=-1, keepdims=True)
+    var = jnp.mean(centered * centered, axis=-1, keepdims=True)
+    inv = lax.rsqrt(var + 1e-06)
+    return centered * inv, inv
+
+
+def normed_back(d_normed, x_normed, inv):
+    mean_d = jnp.mean(d_normed, axis=-1, keepdims=True)
+    mean_dx = jnp.mean(d_normed * x_normed, axis=-1, keepdims=True)
+    return inv * (d_normed - mean_d - x_normed * mean_dx)
+
+
+def fold(value):
+    rows, cols = value.shape
+    return jnp.sum(value.reshape(rows // 8, 8, cols), axis=0)
+
+
+def rows_at(i, size):
+    return pl.ds(pl.multiple_of(i * size, size), size)
+
+
+def step_kernel(
+    msg, pt, pos, bi, bo, ent_in, ex_in,
+    g_in, g_out, ENT, EX, stats,
+    W, WP, G, R1, R2, R3, FIN,
+    ATI, QKV, MIX, MLI, ACT, GD, DMO, DAO, DMX, DMS,
+    X0, AO, RSD, MO, X1, SND, RCV,
+    WMOD, E1, E2S, E2R, E3S, E3R, DMB, DMF, B2S, B2R, DTA, CP, CND,
+    B3S, B3R, B3D, NSS, NSR, NSD, MODS, DACC, WPT, WLT, GLP, SQ, LOSS,
+    st_sem, peer_s, peer_r, zs, zr, bs, br, as_, ar,
+    s1s, s1r, s2s, s2r, s3s, s3r, d_s, d_r, f_l, f_s, f_r,
+    cred_a, cred_b, cred_z,
+):
+    c = lax.axis_index("rep")
+    s = lax.axis_index("shard")
+    o = 1 - c
+    x = s % 2
+    y = (s // 2) % 2
+    z = s // 4
+    a_me = y * o + x * c
+    b_me = x * o + y * c
+
+    def yx(a, b):
+        return a * o + b * c, b * o + a * c
+
+    def dev(core, chip):
+        return {"rep": core, "shard": chip}
+
+    def chip_of(zz, yy, xx):
+        return zz * 4 + yy * 2 + xx
+
+    nb_a = dev(c, chip_of(z, *yx(1 - a_me, b_me)))
+    nb_b = dev(c, chip_of(z, *yx(a_me, 1 - b_me)))
+    twin = dev(o, s)
+
+    def remote(src, dst, ss, rs, to):
+        return pltpu.make_async_remote_copy(
+            src_ref=src, dst_ref=dst, send_sem=ss, recv_sem=rs, device_id=to, device_id_type=MESH
+        )
+
+    pieces = []
+    for j in range(4):
+        pieces.append((bi.at[:, pl.ds(pl.multiple_of(6144 + 1024 * j + c * 512, 512), 512)], FIN.at[j]))
+    for j in range(16):
+        pieces.append((
+            bi.at[:, pl.ds(pl.multiple_of(10240 + 256 * j + c * 128, 128), 128)],
+            FIN.at[4 + j // 4, :, pl.ds((j % 4) * 128, 128)],
+        ))
+    for ch in range(2):
+        for rh in range(2):
+            pieces.append((
+                bo.at[pl.ds(pl.multiple_of(c * 128 + rh * 64, 64), 64), pl.ds(ch * 512, 512)],
+                FIN.at[8 + 2 * ch + rh],
+            ))
+    pieces.append((ent_in, ENT))
+    pieces.append((ex_in, EX))
+    pieces.append((bi.at[:, pl.ds(0, 6144)], WMOD))
+    local = [pltpu.make_async_copy(p, q, st_sem.at[i]) for i, (p, q) in enumerate(pieces)]
+    for i in (24, 25, 0, 1, 2, 3, *range(4, 24), 26):
+        local[i].start()
+
+    barrier = pltpu.get_barrier_semaphore()
+
+    @pl.loop(1, 16)
+    def _(k):
+        pl.semaphore_signal(barrier, 1, device_id=dev(c, (s + k) % 16), device_id_type=MESH)
+
+    pl.semaphore_signal(barrier, 1, device_id=twin, device_id_type=MESH)
+    pl.semaphore_wait(barrier, 16)
+
+    def peers_copy(e, k, src_of, dst):
+        peer = (s + k) % 16
+        return remote(src_of(peer), dst.at[s], peer_s.at[e, k], peer_r.at[e, s], dev(c, peer))
+
+    def peers_send(e, src_of, dst):
+        @pl.loop(1, 16)
+        def _(k):
+            peers_copy(e, k, src_of, dst).start()
+
+    def peers_wait(e, src_of, dst):
+        @pl.loop(1, 16)
+        def _(k):
+            frm = (s + k) % 16
+            remote(src_of(frm), dst.at[frm], peer_s.at[e, k], peer_r.at[e, frm], dev(c, frm)).wait_recv()
+
+        @pl.loop(1, 16)
+        def _(k):
+            peers_copy(e, k, src_of, dst).wait_send()
+
+    def twin_copy(i, src, dst):
+        return remote(src, dst, d_s.at[i], d_r.at[i], twin)
+
+    def z_copy(k, dz):
+        peer = (z + dz) % 4
+        return remote(W.at[k, z, y, x], W.at[k, z, y, x], zs.at[k * 3 + dz - 1], zr.at[k * 4 + z], dev(c, chip_of(peer, y, x)))
+
+    def z_wait(k):
+        for dz in range(1, 4):
+            frm = (z + dz) % 4
+            remote(W.at[k, frm, y, x], W.at[k, frm, y, x], zs.at[k * 3 + dz - 1], zr.at[k * 4 + frm], dev(c, chip_of(frm, y, x))).wait_recv()
+
+    def b_copy(k):
+        return remote(W.at[k, :, y, x], W.at[k, :, y, x], bs.at[k], br.at[k], nb_b)
+
+    def a_copy(k, i):
+        yy, xx = yx(a_me, b_me if i == 0 else 1 - b_me)
+        return remote(W.at[k, :, yy, xx], W.at[k, :, yy, xx], as_.at[k * 2 + i], ar.at[k * 2 + i], nb_a)
+
+    def pump_b(k):
+        z_wait(k)
+        b_copy(k).start()
+        a_copy(k, 0).start()
+
+    def pump_a(k):
+        b_copy(k).wait_recv()
+        a_copy(k, 1).start()
+
+    def need(k):
+        a_copy(k, 0).wait_recv()
+        a_copy(k, 1).wait_recv()
+
+    E1[c, s] = msg[...]
+    peers_send(0, lambda p: msg, E1.at[c])
+
+    for k in range(CHUNKS):
+        if k < 4:
+            local[k].wait()
+            W[k, z, y, x] = FIN[k].astype(BF)
+        elif k < 8:
+            if k == 4:
+                for i in range(4, 20):
+                    local[i].wait()
+            rh, half = (k - 4) // 2, (k - 4) % 2
+            for q in range(4):
+                j = half * 8 + 2 * q
+                pair = FIN[4 + j // 4, :, (j % 4) * 128 : (j % 4) * 128 + 256]
+                piece = jnp.concatenate(
+                    [pair[:, rh * 64 : rh * 64 + 64], pair[:, 128 + rh * 64 : 128 + rh * 64 + 64]], axis=1
+                )
+                W[k, z, y, x, :, q * 128 : q * 128 + 128] = piece.astype(BF)
+        else:
+            local[20 + k - 8].wait()
+            W[k, z, y, x] = FIN[k].astype(BF)
+        for dz in range(1, 4):
+            z_copy(k, dz).start()
+
+    local[24].wait()
+    local[25].wait()
+    peers_wait(0, lambda p: msg, E1.at[c])
+    t_hidden = dot_nn(E1[c, :, 0, :].astype(BF), ENT[1016:1144, :].astype(BF)) + dot_nn(
+        E1[c, :, 1, :].astype(BF), ENT[1144:1272, :].astype(BF)
+    )
+    CND[0] = t_hidden
+    t_act = (t_hidden * sigmoid(t_hidden)).astype(BF)
+    CP[c, 1, :, 0:64] = t_act.astype(F32)
+    for q in range(8):
+        E2S[q] = dot_nn(t_act, EX[:, q * 128 : q * 128 + 128].astype(BF))
+    E2R[s] = E2S[s // 2]
+    peers_send(1, lambda p: E2S.at[p // 2], E2R)
+    for q in range(8):
+        even = E1[c, 2 * q, 8:24, :]
+        odd = E1[c, 2 * q + 1, 8:24, :]
+        WPT[:, q * 128 : q * 128 + 128] = jnp.concatenate([even[:, :64], odd[:, :64]], axis=1)
+        WLT[:, q * 128 : q * 128 + 128] = jnp.concatenate([even[:, 64:], odd[:, 64:]], axis=1)
+    pump_b(0)
+    hot = (
+        E1[c, :, 2, 0:1].astype(jnp.int32) == lax.broadcasted_iota(jnp.int32, (16, 1024), 1)
+    ).astype(F32).astype(BF)
+    w_class = dot_nn(hot, ENT[16:1040, :].astype(BF))
+    peers_wait(1, lambda p: E2S.at[p // 2], E2R)
+    temb = jnp.sum(E2R[...], axis=0)
+    cond = jnp.where(x == 0, temb[:, :64], temb[:, 64:]) + w_class
+    CND[1] = cond
+    cond_low = (cond * sigmoid(cond)).astype(BF)
+    CP[c, 0, :, 0:64] = cond_low.astype(F32)
+    local[26].wait()
+    for k in range(8):
+        w_k = WMOD[:, k * 1024 : k * 1024 + 1024] if k < 6 else EX[:, (k - 5) * 1024 : (k - 4) * 1024]
+        E3S[:, k, :] = dot_nn(cond_low, w_k.astype(BF))
+    E3R[s] = E3S[s]
+    peers_send(2, lambda p: E3S.at[p], E3R)
+    pump_b(1)
+    pump_a(0)
+
+    for n in range(4):
+        cols = slice(n * 256, n * 256 + 256)
+        X0[:, cols] = dot_nn(pt[0].astype(BF), WPT[:, cols].astype(BF))
+
+    @pl.loop(0, 16)
+    def _(i):
+        X0[rows_at(i, 16), 0:512] += pos[...]
+        X0[rows_at(i, 16), 512:1024] += jnp.broadcast_to(pos[pl.ds(i, 1), :], (16, 512))
+
+    DACC[...] = jnp.zeros_like(DACC)
+    peers_wait(2, lambda p: E3S.at[p], E3R)
+    MODS[...] = jnp.sum(E3R[...], axis=0)
+
+    def mod_row(k):
+        return MODS[k : k + 1, :]
+
+    def modulated(src, dst, shift, scale):
+        @pl.loop(0, TOK // 32)
+        def _(i):
+            r = rows_at(i, 32)
+            hat, _ = normed(src[r, :])
+            dst[c, r, :] = (hat * (1.0 + mod_row(scale)) + mod_row(shift)).astype(BF)
+
+    modulated(X0, ATI, 0, 1)
+    twin_copy(0, ATI.at[c], ATI.at[c]).start()
+    pump_b(2)
+    pump_a(1)
+    pump_b(3)
+    pump_a(2)
+    twin_copy(0, ATI.at[o], ATI.at[o]).wait_recv()
+
+    def w_cols(k, n):
+        return W[k, :, :, :, :, rows_at(n, 256)].reshape(1024, 256)
+
+    for j in range(3):
+        need(j)
+
+        @pl.loop(0, 4)
+        def _(t):
+            lat, n = t // 2, t % 2
+            QKV[j, lat, :, rows_at(n, 256)] = dot_nn(ATI[lat], w_cols(j, n)).astype(BF)
+
+        pump_b(4 + j)
+        pump_a(3 + j)
+
+    lane = lax.broadcasted_iota(jnp.int32, (1, LANES), 1)
+    first = lane < 64
+    masks = (first.astype(F32).astype(BF), 1.0 - first.astype(F32).astype(BF))
+
+    def probs_of(q, k):
+        score = dot_nt(q, k) * 0.125
+        e = jnp.exp(score - jnp.max(score, axis=-1, keepdims=True))
+        return e / jnp.sum(e, axis=-1, keepdims=True)
+
+    @pl.loop(0, 8)
+    def _(t):
+        lat, cols = t // 4, rows_at(t % 4, 128)
+        q, k, v = QKV[0, lat, :, cols], QKV[1, lat, :, cols], QKV[2, lat, :, cols]
+        outs = [dot_nn(probs_of(q * m, k).astype(BF), v) for m in masks]
+        MIX[c, lat, :, cols] = jnp.where(first, outs[0], outs[1]).astype(BF)
+
+    twin_copy(1, MIX.at[c], MIX.at[c]).start()
+    need(3)
+    twin_copy(2, W.at[3], WP).start()
+    pump_b(7)
+    pump_a(6)
+    pump_b(8)
+    pump_a(7)
+    twin_copy(1, MIX.at[o], MIX.at[o]).wait_recv()
+    twin_copy(2, W.at[3], WP).wait_recv()
+
+    def proj(own):
+        def cols(n):
+            return pl.ds(pl.multiple_of((c if own else o) * 512 + n * 256, 256), 256)
+
+        @pl.loop(0, 2)
+        def _(n):
+            ref = W.at[3] if own else WP
+            total = 0.0
+            for hh in range(2):
+                w_half = ref[2 * hh : 2 * hh + 2, :, :, :, rows_at(n, 256)].reshape(512, 256)
+                total += dot_nn(MIX[hh, c], w_half)
+            AO[:, cols(n)] = total
+
+    proj(True)
+    proj(False)
+
+    @pl.loop(0, TOK // 32)
+    def _(i):
+        r = rows_at(i, 32)
+        RSD[r, :] = X0[r, :] + mod_row(2) * AO[r, :]
+
+    modulated(RSD, MLI, 3, 4)
+    twin_copy(3, MLI.at[c], MLI.at[c]).start()
+    pump_b(9)
+    pump_a(8)
+    twin_copy(3, MLI.at[o], MLI.at[o]).wait_recv()
+    for j in range(4):
+        need(4 + j)
+
+        @pl.loop(0, 4)
+        def _(t):
+            lat, n = t // 2, t % 2
+            hidden = dot_nn(MLI[lat], w_cols(4 + j, n))
+            cols = pl.ds(pl.multiple_of(j * 512 + n * 256, 256), 256)
+            square = hidden * hidden
+            t_in = 0.7978845608028654 * hidden * (1.0 + 0.044715 * square)
+            t_out = jnp.tanh(t_in)
+            half = 0.5 * (1.0 + t_out)
+            ACT[lat, :, cols] = (hidden * half).astype(BF)
+            slope = half + 0.5 * hidden * (1.0 - t_out * t_out) * (
+                0.7978845608028654 * (1.0 + 3.0 * 0.044715 * square)
+            )
+            GD[lat, :, cols] = slope.astype(BF)
+
+        if j < 2:
+            pump_b(10 + j)
+            pump_a(9 + j)
+        if j == 2:
+            pump_a(11)
+
+    for ch in range(2):
+        need(8 + 2 * ch)
+        need(9 + 2 * ch)
+
+        def mlp_tile(lat, n):
+            total = 0.0
+            for rh in range(2):
+                total += dot_nn(ACT[lat, :, rh * 1024 : rh * 1024 + 1024], w_cols(8 + 2 * ch + rh, n))
+            return total
+
+        @pl.loop(0, 2)
+        def _(n):
+            SND[ch, :, rows_at(n, 256)] = mlp_tile(o, n)
+
+        twin_copy(4 + ch, SND.at[ch], RCV.at[ch]).start()
+
+        @pl.loop(0, 2)
+        def _(n):
+            MO[:, pl.ds(pl.multiple_of(ch * 512 + n * 256, 256), 256)] = mlp_tile(c, n)
+
+    def received(i):
+        for ch in range(2):
+            twin_copy(i + ch, SND.at[ch], RCV.at[ch]).wait_recv()
+
+    def both_parts(r):
+        return MO[r, :] + jnp.concatenate([RCV[0, r, :], RCV[1, r, :]], axis=1)
+
+    received(4)
+    LOSS[...] = jnp.zeros_like(LOSS)
+    GLP[...] = jnp.zeros_like(GLP)
+
+    @pl.loop(0, TOK // 32)
+    def _(i):
+        r = rows_at(i, 32)
+        mlp_out = both_parts(r)
+        x1 = RSD[r, :] + mod_row(5) * mlp_out
+        hat, inv = normed(x1)
+        scale = 1.0 + mod_row(7)
+        final_in = (hat * scale + mod_row(6)).astype(BF)
+        w_lin = WLT[...].astype(BF)
+        error = dot_nt(final_in, w_lin) - pt[1, r, :]
+        LOSS[...] += fold(error * error)
+        d_pred = (2.0 * error / (TOK * PDIM)).astype(BF)
+        GLP[16:32, :] += dot_tn(d_pred, final_in)
+        d_final = dot_nn(d_pred, w_lin)
+        DACC[6] += fold(d_final)
+        DACC[7] += fold(d_final * hat)
+        d_x = normed_back(d_final * scale, hat, inv)
+        X1[r, :] = d_x
+        DACC[5] += fold(d_x * mlp_out)
+        DMO[c, r, :] = (d_x * mod_row(5)).astype(BF)
+
+    twin_copy(6, DMO.at[c], DMO.at[c]).start()
+
+    def r1_of(k, b):
+        return R1.at[k - 8, b] if k >= 8 else W.at[8 + k // 2, :, k % 2, b]
+
+    def r2_of(k):
+        return R2.at[k - 8] if k >= 8 else W.at[4 + k // 4, :, (k // 2) % 2, k % 2]
+
+    def r3_of(k):
+        return R3.at[k - 8] if k >= 8 else W.at[6 + k // 4, :, (k // 2) % 2, k % 2]
+
+    def s1_copy(k, b):
+        yy, xx = yx(1 - a_me, b)
+        return remote(G.at[k, :, yy, xx], r1_of(k, b), s1s.at[k * 2 + b], s1r.at[k * 2 + b], nb_a)
+
+    def s2_copy(k):
+        yy, xx = yx(a_me, 1 - b_me)
+        return remote(G.at[k, :, yy, xx], r2_of(k), s2s.at[k], s2r.at[k], nb_b)
+
+    def s3_copy(k, dz):
+        zt = (z + dz) % 4
+        return remote(G.at[k, zt, y, x], r3_of(k).at[z], s3s.at[k * 3 + dz - 1], s3r.at[k * 4 + z], dev(c, chip_of(zt, y, x)))
+
+    def s1(k):
+        for b in range(2):
+            s1_copy(k, b).start()
+
+    def s2(k):
+        for b in range(2):
+            s1_copy(k, b).wait_recv()
+        yy, xx = yx(a_me, 1 - b_me)
+
+        @pl.loop(0, 4)
+        def _(zz):
+            total = G[k, zz, yy, xx].astype(F32) + r1_of(k, 1 - b_me)[zz].astype(F32)
+            G[k, zz, yy, xx] = total.astype(BF)
+
+        s2_copy(k).start()
+
+    def s3(k):
+        s2_copy(k).wait_recv()
+
+        def total(zz):
+            return (
+                G[k, zz, y, x].astype(F32) + r1_of(k, b_me)[zz].astype(F32) + r2_of(k)[zz].astype(F32)
+            )
+
+        FIN[k] = total(z)
+
+        @pl.loop(1, 4)
+        def _(dz):
+            zt = (z + dz) % 4
+            G[k, zt, y, x] = total(zt).astype(BF)
+
+        for dz in range(1, 4):
+            s3_copy(k, dz).start()
+
+    def s4(k):
+        for dz in range(1, 4):
+            frm = (z + dz) % 4
+            remote(G.at[k, frm, y, x], r3_of(k).at[frm], s3s.at[k * 3 + dz - 1], s3r.at[k * 4 + frm], dev(c, chip_of(frm, y, x))).wait_recv()
+        total = FIN[k]
+        for dz in range(1, 4):
+            total += r3_of(k)[(z + dz) % 4].astype(F32)
+        FIN[k] = total
+        SQ[...] += fold(total * total)
+
+    def to_outputs(i, src, dst):
+        pltpu.make_async_copy(src, dst, f_l.at[i]).start()
+        remote(src, dst, f_s.at[i], f_r.at[i], twin).start()
+
+    def grad_tiles(k, left, right):
+        @pl.loop(0, 4)
+        def _(r):
+            G[k, r] = dot_tn(left(r), right).astype(BF).reshape(2, 2, 64, 512)
+
+    SQ[...] = jnp.zeros_like(SQ)
+    twin_copy(6, DMO.at[o], DMO.at[o]).wait_recv()
+    for ch in range(2):
+        for rh in range(2):
+            k = 8 + 2 * ch + rh
+            grad_tiles(
+                k,
+                lambda r: ACT[:, :, pl.ds(pl.multiple_of(rh * 1024 + r * 256, 256), 256)].reshape(512, 256),
+                DMO[:, :, ch * 512 : ch * 512 + 512].reshape(512, 512),
+            )
+            s1(k)
+
+    for k in range(CHUNKS):
+        for dz in range(1, 4):
+            z_copy(k, dz).wait_send()
+        b_copy(k).wait_send()
+        a_copy(k, 0).wait_send()
+        a_copy(k, 1).wait_send()
+
+    @pl.loop(0, 16)
+    def _(t):
+        lat, rh, r = t // 8, (t // 4) % 2, t % 4
+        total = 0.0
+        for ch in range(2):
+            total += dot_nt(DMO[lat, :, ch * 512 : ch * 512 + 512], W[8 + 2 * ch + rh, r].reshape(256, 512))
+        cols = pl.ds(pl.multiple_of(rh * 1024 + r * 256, 256), 256)
+        GD[lat, :, cols] = (total * GD[lat, :, cols].astype(F32)).astype(BF)
+
+    pl.semaphore_signal(cred_a, 1, device_id=nb_a, device_id_type=MESH)
+
+    def data_back(first_k, count, left, i):
+        for ch in range(2):
+            @pl.loop(0, 2)
+            def _(n):
+                total = 0.0
+                for j in range(count):
+                    total += dot_nt(left(j, o), W[first_k + j, 2 * ch + n].reshape(256, 512))
+                SND[ch, :, rows_at(n, 256)] = total
+
+            twin_copy(i + ch, SND.at[ch], RCV.at[ch]).start()
+
+        @pl.loop(0, 4)
+        def _(r):
+            total = 0.0
+            for j in range(count):
+                total += dot_nt(left(j, c), W[first_k + j, r].reshape(256, 512))
+            MO[:, rows_at(r, 256)] = total
+
+    for ch in range(2):
+        twin_copy(4 + ch, SND.at[ch], RCV.at[ch]).wait_send()
+    data_back(4, 4, lambda j, lat: GD[lat, :, j * 512 : j * 512 + 512], 7)
+    pl.semaphore_signal(cred_b, 1, device_id=nb_b, device_id_type=MESH)
+    for dz in range(1, 4):
+        pl.semaphore_signal(cred_z, 1, device_id=dev(c, chip_of((z + dz) % 4, y, x)), device_id_type=MESH)
+
+    pl.semaphore_wait(cred_a, 1)
+    for j in range(4):
+        grad_tiles(
+            4 + j,
+            lambda r: MLI[:, :, rows_at(r, 256)].reshape(512, 256),
+            GD[:, :, j * 512 : j * 512 + 512].reshape(512, 512),
+        )
+        s1(4 + j)
+    s2(8)
+    received(7)
+
+    @pl.loop(0, TOK // 32)
+    def _(i):
+        r = rows_at(i, 32)
+        d_in = both_parts(r)
+        hat, inv = normed(RSD[r, :])
+        DACC[3] += fold(d_in)
+        DACC[4] += fold(d_in * hat)
+        d_x = normed_back(d_in * (1.0 + mod_row(4)), hat, inv) + X1[r, :]
+        X1[r, :] = d_x
+        DACC[2] += fold(d_x * AO[r, :])
+        DAO[c, r, :] = (d_x * mod_row(2)).astype(BF)
+
+    dao_other = pl.ds(pl.multiple_of(o * 512, 512), 512)
+    dao_mine = pl.ds(pl.multiple_of(c * 512, 512), 512)
+    twin_copy(9, DAO.at[c, :, dao_other], DAO.at[c, :, dao_other]).start()
+
+    def mixed_back(hh, n):
+        w_mine = W[3, 2 * hh + n].reshape(256, 512)
+        w_other = WP[2 * hh + n].reshape(256, 512)
+        return (dot_nt(DAO[c, :, dao_mine], w_mine) + dot_nt(DAO[c, :, dao_other], w_other)).astype(BF)
+
+    @pl.loop(0, 2)
+    def _(n):
+        DMS[:, rows_at(n, 256)] = mixed_back(o, n)
+
+    twin_copy(10, DMS, DMX.at[c]).start()
+
+    @pl.loop(0, 2)
+    def _(n):
+        DMX[c, :, rows_at(n, 256)] = mixed_back(c, n)
+
+    s2(9)
+    s3(8)
+    twin_copy(9, DAO.at[o, :, dao_mine], DAO.at[o, :, dao_mine]).wait_recv()
+
+    @pl.loop(0, 4)
+    def _(r):
+        left = MIX[r // 2, :, :, rows_at(r % 2, 256)].reshape(512, 256)
+        G[3, r] = dot_tn(left, DAO[:, :, dao_mine].reshape(512, 512)).astype(BF).reshape(2, 2, 64, 512)
+
+    s1(3)
+    twin_copy(10, DMS, DMX.at[o]).wait_recv()
+
+    @pl.loop(0, 8)
+    def _(t):
+        lat, cols = t // 4, rows_at(t % 4, 128)
+        q, k, v = QKV[0, lat, :, cols], QKV[1, lat, :, cols], QKV[2, lat, :, cols]
+        dm = DMX[lat, :, cols]
+        res = []
+        for m in masks:
+            probs = probs_of(q * m, k)
+            d_probs = dot_nt(dm * m, v)
+            d_v = dot_tn(probs.astype(BF), dm)
+            d_s = probs * (d_probs - jnp.sum(d_probs * probs, axis=-1, keepdims=True))
+            d_s = (d_s * 0.125).astype(BF)
+            res.append((dot_nn(d_s, k), dot_tn(d_s, q), d_v))
+        for j in range(3):
+            QKV[j, lat, :, cols] = jnp.where(first, res[0][j], res[1][j]).astype(BF)
+
+    for j in range(3):
+        grad_tiles(
+            j,
+            lambda r: ATI[:, :, rows_at(r, 256)].reshape(512, 256),
+            QKV[j].reshape(512, 512),
+        )
+        s1(j)
+    s2(10)
+    s3(9)
+    for ch in range(2):
+        twin_copy(7 + ch, SND.at[ch], RCV.at[ch]).wait_send()
+    data_back(0, 3, lambda j, lat: QKV[j, lat], 11)
+    s2(11)
+    s3(10)
+    received(11)
+
+    @pl.loop(0, TOK // 32)
+    def _(i):
+        r = rows_at(i, 32)
+        d_in = both_parts(r)
+        hat, inv = normed(X0[r, :])
+        DACC[0] += fold(d_in)
+        DACC[1] += fold(d_in * hat)
+        d_x = normed_back(d_in * (1.0 + mod_row(1)), hat, inv) + X1[r, :]
+        GLP[0:16, :] += dot_tn(pt[0, r, :].astype(BF), d_x.astype(BF))
+
+    for k in range(8):
+        MODS[k : k + 1, :] = jnp.sum(DACC[k], axis=0, keepdims=True)
+    d_mods = MODS[...]
+    DMB[c, s] = jnp.concatenate([d_mods[:, :512], d_mods[:, 512:]], axis=0).astype(BF)
+    peers_send(3, lambda p: DMB.at[c, s], DMB.at[c])
+    for q in range(8):
+        B3S[q] = GLP[:, q * 128 : q * 128 + 128]
+    B3R[s] = B3S[s // 2]
+    peers_send(4, lambda p: B3S.at[p // 2], B3R)
+    pl.semaphore_wait(cred_b, 1)
+    pl.semaphore_wait(cred_z, 3)
+    s3(11)
+    s2(4)
+    s4(8)
+    peers_wait(3, lambda p: DMB.at[c, s], DMB.at[c])
+    twin_copy(13, DMB.at[c], DMB.at[c]).start()
+
+    def unpack(g):
+        @pl.loop(0, 16)
+        def _(l):
+            both = DMB[g, l].astype(F32)
+            DMF[g, :, l, 0:512] = both[0:8]
+            DMF[g, :, l, 512:1024] = both[8:16]
+
+    unpack(c)
+    d_cond_low = 0.0
+    for k in range(8):
+        w_k = WMOD[:, k * 1024 : k * 1024 + 1024] if k < 6 else EX[:, (k - 5) * 1024 : (k - 4) * 1024]
+        d_cond_low += dot_nt(DMF[c, k].astype(BF), w_k.astype(BF))
+    d_cond = d_cond_low * silu_slope(CND[1])
+    CP[c, 2, :, 0:64] = d_cond
+    d_temb = d_cond.astype(BF).astype(F32)
+    B2S[...] = jnp.concatenate([d_temb, d_temb], axis=1)
+    B2R[s] = B2S[...]
+    peers_send(5, lambda p: B2S, B2R)
+    s2(5)
+    s3(4)
+    s4(9)
+    peers_wait(4, lambda p: B3S.at[p // 2], B3R)
+    B3D[c] = jnp.sum(B3R[...], axis=0)
+    twin_copy(14, B3D.at[c], B3D.at[c]).start()
+    peers_wait(5, lambda p: B2S, B2R)
+    for q in range(8):
+        DTA[c, :, q * 128 : q * 128 + 128] = jnp.concatenate(
+            [B2R[2 * q, :, 0:64], B2R[2 * q + 1, :, 0:64]], axis=1
+        )
+    d_tact = dot_nt(DTA[c].astype(BF), EX[:, 0:1024].astype(BF))
+    CP[c, 3, :, 0:64] = (d_tact * silu_slope(CND[0])).astype(BF).astype(F32)
+    twin_copy(15, DTA.at[c], DTA.at[c]).start()
+    twin_copy(16, CP.at[c], CP.at[c]).start()
+    twin_copy(17, E1.at[c], E1.at[c]).start()
+    s2(6)
+    s3(5)
+    s4(10)
+    twin_copy(13, DMB.at[o], DMB.at[o]).wait_recv()
+    unpack(o)
+    twin_copy(14, B3D.at[o], B3D.at[o]).wait_recv()
+    twin_copy(15, DTA.at[o], DTA.at[o]).wait_recv()
+    twin_copy(16, CP.at[o], CP.at[o]).wait_recv()
+    twin_copy(17, E1.at[o], E1.at[o]).wait_recv()
+
+    def packed(i):
+        return jnp.concatenate([CP[0, i, :, 0:64], CP[1, i, :, 0:64]], axis=0)
+
+    def square_half(value):
+        part = 0.5 * value * value
+        return jnp.sum(jnp.sum(part, axis=0, keepdims=True), axis=1, keepdims=True)
+
+    cond_both = packed(0).astype(BF)
+    small = jnp.zeros((1, 1), F32)
+    for k in range(8):
+        grad = dot_tn(cond_both, jnp.concatenate([DMF[0, k], DMF[1, k]], axis=0).astype(BF))
+        small += square_half(grad)
+        if k < 6:
+            WMOD[:, k * 1024 : k * 1024 + 1024] = grad
+        else:
+            EX[:, (k - 5) * 1024 : (k - 4) * 1024] = grad
+    mod_out = pltpu.make_async_copy(WMOD, g_in.at[:, pl.ds(0, 6144)], st_sem.at[26])
+    mod_out.start()
+    s2(7)
+    s3(6)
+    s4(11)
+    grad = dot_tn(packed(1).astype(BF), jnp.concatenate([DTA[0], DTA[1]], axis=0).astype(BF))
+    small += square_half(grad)
+    EX[:, 0:1024] = grad
+    sums = B3D[0] + B3D[1]
+    sums = jnp.where(x == 0, sums[:, 0:64], sums[:, 64:128])
+    small += square_half(sums)
+    ENT[0:16, :] = sums[0:16]
+    wide = jnp.concatenate(
+        [jnp.concatenate([sums[16:32], jnp.zeros((16, 64), F32)], axis=1), jnp.zeros((112, 128), F32)], axis=0
+    )
+    EX[:, 3072:3088] = wide.T[0:64, 0:16]
+    labels = jnp.sum(E1[0, :, 3, :] + E1[1, :, 3, :], axis=0, keepdims=True).astype(jnp.int32)
+    d_cond_both = jnp.concatenate([packed(2), jnp.zeros((96, 64), F32)], axis=0)
+    for i in range(5):
+        rows = lax.broadcasted_iota(jnp.int32, (200, LANES), 0) + i * 200
+        hot = (rows == labels).astype(F32)
+        grad = lax.dot_general(
+            hot, d_cond_both, (((1,), (0,)), ((), ())), preferred_element_type=F32, precision=highest
+        )
+        small += square_half(grad)
+        ENT[16 + i * 200 : 216 + i * 200, :] = grad
+    d_thidden = packed(3).astype(BF)
+    for i in range(2):
+        femb = jnp.concatenate([E1[0, :, i, :], E1[1, :, i, :]], axis=0).astype(BF)
+        grad = dot_tn(femb, d_thidden)
+        small += square_half(grad)
+        ENT[1016 + i * 128 : 1144 + i * 128, :] = grad
+
+    s2(3)
+    s3(7)
+    s4(4)
+    s2(0)
+    s3(3)
+    s4(5)
+    s2(1)
+    s3(0)
+    s4(6)
+    s2(2)
+    s3(1)
+    s4(7)
+    for half in range(2):
+        for q in range(4):
+            cols = slice(q * 128, q * 128 + 128)
+            low, high = FIN[4 + half, :, cols], FIN[6 + half, :, cols]
+            FIN[4 + half, :, cols] = jnp.concatenate([low[:, 0:64], high[:, 0:64]], axis=1)
+            FIN[6 + half, :, cols] = jnp.concatenate([low[:, 64:128], high[:, 64:128]], axis=1)
+    outs = []
+    for ch in range(2):
+        for rh in range(2):
+            outs.append((
+                FIN.at[8 + 2 * ch + rh],
+                g_out.at[pl.ds(pl.multiple_of(c * 128 + rh * 64, 64), 64), pl.ds(ch * 512, 512)],
+            ))
+    for j in range(16):
+        outs.append((
+            FIN.at[4 + j // 8 + 2 * (j % 2), :, pl.ds(((j % 8) // 2) * 128, 128)],
+            g_in.at[:, pl.ds(pl.multiple_of(10240 + 256 * j + c * 128, 128), 128)],
+        ))
+    for j in (3, 0, 1, 2):
+        outs.append((FIN.at[j], g_in.at[:, pl.ds(pl.multiple_of(6144 + 1024 * j + c * 512, 512), 512)]))
+    for i in range(20):
+        to_outputs(i, *outs[i])
+    s3(2)
+    s4(3)
+    to_outputs(20, *outs[20])
+    s4(0)
+    to_outputs(21, *outs[21])
+    s4(1)
+    to_outputs(22, *outs[22])
+    s4(2)
+    to_outputs(23, *outs[23])
+
+    def total_of(value):
+        return jnp.sum(jnp.sum(value, axis=0, keepdims=True), axis=1, keepdims=True)
+
+    NSS[0:1, :] = jnp.broadcast_to(total_of(SQ[...]) + small, (1, 128))
+    NSS[1:2, :] = jnp.broadcast_to(total_of(LOSS[...]) / (TOK * PDIM), (1, 128))
+    NSS[2:8, :] = jnp.zeros((6, 128), F32)
+    NSR[s] = NSS[...]
+    peers_send(6, lambda p: NSS, NSR)
+    peers_wait(6, lambda p: NSS, NSR)
+    NSD[c] = jnp.sum(NSR[...], axis=0)
+    twin_copy(18, NSD.at[c], NSD.at[c]).start()
+    twin_copy(18, NSD.at[o], NSD.at[o]).wait_recv()
+    stats[...] = NSD[0] + NSD[1]
+
+    mod_out.wait()
+    for i, (src, dst) in enumerate(outs):
+        pltpu.make_async_copy(src, dst, f_l.at[i]).wait()
+        remote(src, dst, f_s.at[i], f_r.at[i], twin).wait()
+    for k in range(CHUNKS):
+        for b in range(2):
+            s1_copy(k, b).wait_send()
+        s2_copy(k).wait_send()
+        for dz in range(1, 4):
+            s3_copy(k, dz).wait_send()
+    twin_copy(0, ATI.at[c], ATI.at[c]).wait_send()
+    twin_copy(1, MIX.at[c], MIX.at[c]).wait_send()
+    twin_copy(2, W.at[3], WP).wait_send()
+    twin_copy(3, MLI.at[c], MLI.at[c]).wait_send()
+    twin_copy(6, DMO.at[c], DMO.at[c]).wait_send()
+    twin_copy(9, DAO.at[c, :, dao_other], DAO.at[c, :, dao_other]).wait_send()
+    twin_copy(10, DMS, DMX.at[c]).wait_send()
+    for ch in range(2):
+        twin_copy(11 + ch, SND.at[ch], RCV.at[ch]).wait_send()
+    twin_copy(13, DMB.at[c], DMB.at[c]).wait_send()
+    twin_copy(14, B3D.at[c], B3D.at[c]).wait_send()
+    twin_copy(15, DTA.at[c], DTA.at[c]).wait_send()
+    twin_copy(16, CP.at[c], CP.at[c]).wait_send()
+    twin_copy(17, E1.at[c], E1.at[c]).wait_send()
+    twin_copy(18, NSD.at[c], NSD.at[c]).wait_send()
+
+
+def fused_step(msg, pt, pos, block_in, block_out, entry, exit_):
+    vm = pltpu.VMEM
+    dma = pltpu.SemaphoreType.DMA
+    scratch = [
+        vm((12, 4, 2, 2, 64, 512), BF), vm((4, 2, 2, 64, 512), BF), vm((12, 4, 2, 2, 64, 512), BF),
+        vm((4, 2, 4, 64, 512), BF), vm((4, 4, 64, 512), BF), vm((4, 4, 64, 512), BF), vm((12, 64, 512), F32),
+        vm((2, TOK, 1024), BF), vm((3, 2, TOK, 512), BF), vm((2, 2, TOK, 512), BF), vm((2, TOK, 1024), BF),
+        vm((2, TOK, 2048), BF), vm((2, TOK, 2048), BF), vm((2, TOK, 1024), BF), vm((2, TOK, 1024), BF),
+        vm((2, TOK, 512), BF), vm((TOK, 512), BF),
+        *[vm((TOK, 1024), F32)] * 5, vm((2, TOK, 512), F32), vm((2, TOK, 512), F32),
+        vm((64, 6144), F32), vm((2, 16, 24, 128), F32), vm((8, 16, 128), F32), vm((16, 16, 128), F32),
+        vm((16, 8, 1024), F32), vm((16, 8, 1024), F32), vm((2, 16, 16, 512), BF), vm((2, 8, 16, 1024), F32),
+        vm((16, 128), F32), vm((16, 16, 128), F32), vm((2, 16, 1024), F32), vm((2, 4, 16, 128), F32), vm((2, 16, 64), F32),
+        vm((8, 32, 128), F32), vm((16, 32, 128), F32), vm((2, 32, 128), F32),
+        vm((8, 128), F32), vm((16, 8, 128), F32), vm((2, 8, 128), F32),
+        vm((8, 1024), F32), vm((8, 8, 1024), F32), vm((16, 1024), F32), vm((16, 1024), F32), vm((32, 1024), F32),
+        vm((8, 512), F32), vm((8, 16), F32),
+        dma((27,)), dma((7, 16)), dma((7, 16)), dma((36,)), dma((48,)), dma((12,)), dma((12,)), dma((24,)), dma((24,)),
+        dma((24,)), dma((24,)), dma((12,)), dma((12,)), dma((36,)), dma((48,)), dma((19,)), dma((19,)),
+        dma((24,)), dma((24,)), dma((24,)),
+        pltpu.SemaphoreType.REGULAR, pltpu.SemaphoreType.REGULAR, pltpu.SemaphoreType.REGULAR,
+    ]
+    any_ = pl.BlockSpec(memory_space=pl.ANY)
+    vmem = pl.BlockSpec(memory_space=pltpu.VMEM)
+    shape = jax.ShapeDtypeStruct
+    return pl.pallas_call(
+        step_kernel,
+        out_shape=(
+            shape(block_in.shape, F32), shape(block_out.shape, F32), shape(entry.shape, F32),
+            shape(exit_.shape, F32), shape((8, 128), F32),
+        ),
+        in_specs=[vmem, vmem, vmem, any_, any_, any_, any_],
+        out_specs=(any_, any_, vmem, vmem, vmem),
+        scratch_shapes=scratch,
+        compiler_params=pltpu.CompilerParams(
+            collective_id=0, has_side_effects=True, vmem_limit_bytes=62 * 2**20
+        ),
+        cost_estimate=pl.CostEstimate(flops=21 * 10**9, bytes_accessed=20 * 10**6, transcendentals=4 * 10**6),
+    )(msg, pt, pos, block_in, block_out, entry, exit_)
+
+
+def local_fused(
+    noisy, timesteps, labels, noise,
+    block_in, block_in_first, block_in_second,
+    block_out, block_out_first, block_out_second,
+    entry_table, entry_first, entry_second,
+    exit_proj, exit_first, exit_second,
+):
+    index = lax.axis_index("rep") * 16 + lax.axis_index("shard")
+    femb = lowered(time_features(timesteps, FREQ)).astype(F32).reshape(2, LANES)
+    label = labels.astype(F32)[0]
+    lane = jnp.arange(LANES)[None, :]
+    head = jnp.concatenate(
+        [femb, jnp.full((1, LANES), label), jnp.where(lane == index, label, 0.0), jnp.zeros((4, LANES), F32)], axis=0
+    )
+    edge = jnp.concatenate([entry_table[:PDIM], exit_proj[:, 3 * D :].T], axis=1)
+    msg = jnp.concatenate([head, edge], axis=0)
+    pt = patchify(jnp.concatenate([noisy, noise], axis=0), PATCH)
+    grid = noisy.shape[-1] // PATCH
+    pos = position_table(grid, D)[:grid, : D // 2]
+    g_in, g_out, g_entry, g_exit, stats = fused_step(
+        msg, pt, pos, block_in[0], block_out[0], entry_table, exit_proj
+    )
+    loss = stats[1, 0]
+    grad_norm = jnp.sqrt(stats[0, 0])
+    factor = clip_limit / jnp.maximum(grad_norm, clip_limit)
+    outs = [loss, grad_norm]
+    for weight, first, second, grad, rate in (
+        (block_in, block_in_first, block_in_second, g_in[None], rate_main),
+        (block_out, block_out_first, block_out_second, g_out[None], rate_main),
+        (entry_table, entry_first, entry_second, g_entry, rate_edge),
+        (exit_proj, exit_first, exit_second, g_exit, rate_main),
+    ):
+        outs.extend(adam_step(weight, first, second, grad, factor, rate))
+    return tuple(outs)
+
+
 def solution(mesh):
+    step = local_fused if dict(mesh.shape) == {"rep": 2, "shard": 16} else local
     in_specs = (
         P(("rep", "shard"), None, None, None),
         P(("rep", "shard")),
@@ -400,4 +1310,4 @@
         P("shard", None),
         P("shard", None),
     )
-    return jax.shard_map(local, mesh=mesh, in_specs=in_specs, out_specs=out_specs, check_vma=False)
+    return jax.shard_map(step, mesh=mesh, in_specs=in_specs, out_specs=out_specs, check_vma=False)

time: 2790 us -> 390 us (0.14)
  waiting for transfers between devices: 2420 us -> 0 us
  Pallas kernels: 0 us -> 351 us
  matrix products: 137 us -> 0 us
  other arithmetic: 106 us -> 21.3 us
  blocking collectives: 82 us -> 0 us
    reduce_scatter x4 -> x0, waiting for transfers between devices: 1850 us -> none  [the longest x1 1200 us: local(): lax.psum_scatter(g_in, 'shard', scatter_dimension=0, tiled=True)]
    all_gather x4 -> x0, waiting for transfers between devices: 543 us -> none  [the longest x1 308 us: local(): lax.all_gather(lowered(block_in[layer]), 'shard', axis=0, tiled=True)]
    pallas_call x0 -> x1, Pallas kernels: none -> 351 us  [fused_step(): pl.pallas_call(step_kernel, out_shape=(shape(block_in.shape, F32), shape(...]
    dot_general x30 -> x0, matrix products: 133 us -> none  [the longest x4 12.3 us: product(): return jnp.dot(left, right, preferred_element_type=jnp.float32)]
    psum x2 -> x0, blocking collectives: 82 us -> none  [the longest x1 41.5 us: local(): norm_sq = lax.psum(squares, 'shard')]
    concatenate x2 -> x3, other arithmetic: 43.7 us -> 1.58 us  [the longest x1 0.88 us: local_fused(): pt = patchify(jnp.concatenate([noisy, noise], axis=0), PATCH)]
    psum x1 -> x0, waiting for transfers between devices: 29.1 us -> none  [local(): lax.psum(jnp.stack(shards_in).astype(jnp.bfloat16), 'rep')]
  transfers between devices with their start and end apart: 9 -> 0, of which waited for: 9 -> 0; matrix products, arithmetic and copies ran while one was open for 5% -> 0% of each run, Pallas kernels for 0% -> 0%
where the time goes in v1:
time: 390 us
  Pallas kernels  351 us (90%)
  other arithmetic  21.3 us (5%)
  local copies, waits for them, and re-layouts  13.1 us (3%)
  between operations  4.01 us (1%)
    pallas_call x1, Pallas kernels, fused_step(): pl.pallas_call(step_kernel, out_shape=(shape(block_in.shape, F32), shape(...  351 us
    convert_element_type x4, other arithmetic, adam_step(): return (weight_new, first_new, second_new, weight_new.astype(jnp.bfloat16))  18.6 us

profile of v1, /device:TPU:0, one launch (start us, length us, event | category | flops | bytes accessed | tf_op | source)
XLA Modules:
  0.0 389.6 jit_solution(11766076594052817462)
XLA Ops:
  2.1 0.8 slice.16
  2.8 0.1 copy.60
  2.9 1.2 copy.46.ent_in
  4.1 0.1 pad_maximum_fusion.2
  4.2 1.3 concatenate.20.msg
  5.5 0.9 pad_maximum_fusion
  6.4 0.5 copy.48
  6.9 1.1 copy.49
  7.9 0.1 reshape.111
  8.1 0.8 copy.50.pt
  8.9 1.0 multiply_sine_fusion
  9.9 0.6 pad_maximum_fusion.1.pos
  10.5 351.2 %shard_map.295 = (f32[64,14336]{1,0:T(8,128)}, f32[256,1024]{1,0:T(8,128)}, f32[1272,64]{1,0:T(8,128)}, f32[64,3088]{1,0:T(8,128)}, f32[8,128]{1,0:T(8,128)}) custom-call(f32[24,128]{1,0:T(8,128)} %concatenate.20.msg, f32[2,256,16]{2,1,0:T(8,128)} %copy.50.pt, f32[16,512]{1,0:T(8,128)} %pad_maximum_fusion.1.pos, f32[64,14336]{1,0:T(8,128)} %bitcast.36, ...), custom_call_target="tpu_custom_call" | custom-call | flops 20999999488 | bytes 20000000 | tf_op jit(solution)/shard_map/pallas_call | solution.py:1221
  361.7 1.3 fusion.19
  363.8 10.0 %fusion.16 = (bf16[1,64,14336]{2,1,0:T(8,128)(2,1)}, f32[1,64,14336]{2,1,0:T(8,128)}, f32[1,64,14336]{2,1,0:T(8,128)}, f32[1,64,14336]{2,1,0:T(8,128)}) fusion(f32[1,64,14336]{2,1,0:T(8,128)} %param.20, f32[64,14336]{1,0:T(8,128)} %get-tuple-element.24, f32[]{:T(128)S(6)} %div.61, f32[1,64,14336]{2,1,0:T(8,128)} %param.21, f32[1,64,14336]{2,1,0:T(8,128)} %param.22), kind=kLoop, calls=%fused_computation.36 | loop fusion | flops 14680064 | bytes 27525124 | tf_op jit(solution)/shard_map/convert_element_type | solution.py:89
  373.8 2.5 fusion.13
  376.3 0.2 copy.52
  376.5 1.1 copy.53
  377.6 2.5 fusion.11
  380.2 0.9 copy.56
  381.1 0.9 copy.57
  382.0 0.9 copy.58
  383.0 1.8 copy.59
  384.8 3.7 fusion.9
  (26 shorter events, 0.1 us)
Async XLA Ops:
  4.1 6.4 %copy-start = (f32[1272,64]{1,0:T(8,128)}, f32[1272,64]{1,0:T(8,128)S(1)}, u32[]{:S(2)}) copy-start(f32[1272,64]{1,0:T(8,128)S(1)} %copy.46.ent_in) | copy-start | bytes 976900
  363.8 10.0 %copy-start.2 = (f32[1,256,1024]{2,1,0:T(8,128)S(1)}, f32[1,256,1024]{2,1,0:T(8,128)}, u32[]{:S(2)}) copy-start(f32[1,256,1024]{2,1,0:T(8,128)} %param.23) | copy-start | bytes 3145732
  363.8 10.0 %copy-start.3 = (f32[1,256,1024]{2,1,0:T(8,128)S(1)}, f32[1,256,1024]{2,1,0:T(8,128)}, u32[]{:S(2)}) copy-start(f32[1,256,1024]{2,1,0:T(8,128)} %param.24) | copy-start | bytes 3145732
  363.8 10.0 %copy-start.4 = (f32[1,256,1024]{2,1,0:T(8,128)S(1)}, f32[1,256,1024]{2,1,0:T(8,128)}, u32[]{:S(2)}) copy-start(f32[1,256,1024]{2,1,0:T(8,128)} %param.25) | copy-start | bytes 3145732
  363.8 10.0 %copy-start.5 = (f32[256,1024]{1,0:T(8,128)S(1)}, f32[256,1024]{1,0:T(8,128)}, u32[]{:S(2)}) copy-start(f32[256,1024]{1,0:T(8,128)} %get-tuple-element.25) | copy-start | bytes 3145732
  373.8 2.5 copy-start.7
  373.8 2.7 copy-start.8
  373.8 3.8 copy-start.1
  380.2 4.6 %copy-start.6 = (f32[64,3088]{1,0:T(8,128)S(1)}, f32[64,3088]{1,0:T(8,128)}, u32[]{:S(2)}) copy-start(f32[64,3088]{1,0:T(8,128)} %ex_in.1) | copy-start | bytes 2371588

commit v2 on v1

--- a/solution.py
+++ b/solution.py
@@ -12,6 +12,7 @@
 FREQ = 256
 STEP = 10
 PDIM = 16
+ENTRIES = PDIM + NCLS + FREQ
 
 
 clip_limit = 0.5
@@ -369,6 +370,12 @@
 TOK = 256
 LANES = 128
 CHUNKS = 12
+AHEAD = 2
+VIA_Z = ()
+LEAD = 3
+LAG3 = 1
+LAG4 = 2
+LAG_A = 1
 ORDER = (8, 9, 10, 11, 4, 5, 6, 7, 3, 0, 1, 2)
 
 
@@ -382,6 +389,12 @@
 
 def dot_tn(left, right):
     return lax.dot_general(left, right, (((0,), (0,)), ((), ())), preferred_element_type=F32)
+
+
+def dot_tn_exact(left, right):
+    return lax.dot_general(
+        left, right, (((0,), (0,)), ((), ())), preferred_element_type=F32, precision=highest
+    )
 
 
 def sigmoid(value):
@@ -421,7 +434,7 @@
     W, WP, G, R1, R2, R3, FIN,
     ATI, QKV, MIX, MLI, ACT, GD, DMO, DAO, DMX, DMS,
     X0, AO, RSD, MO, X1, SND, RCV,
-    WMOD, E1, E2S, E2R, E3S, E3R, DMB, DMF, B2S, B2R, DTA, CP, CND,
+    WMOD, E1, EDG, E2S, E2R, E3S, E3R, DMB, DMF, B2S, B2R, DTA, CP, CND,
     B3S, B3R, B3D, NSS, NSR, NSD, MODS, DACC, WPT, WLT, GLP, SQ, LOSS,
     st_sem, peer_s, peer_r, zs, zr, bs, br, as_, ar,
     s1s, s1r, s2s, s2r, s3s, s3r, d_s, d_r, f_l, f_s, f_r,
@@ -506,39 +519,86 @@
     def twin_copy(i, src, dst):
         return remote(src, dst, d_s.at[i], d_r.at[i], twin)
 
-    def z_copy(k, dz):
-        peer = (z + dz) % 4
-        return remote(W.at[k, z, y, x], W.at[k, z, y, x], zs.at[k * 3 + dz - 1], zr.at[k * 4 + z], dev(c, chip_of(peer, y, x)))
-
-    def z_wait(k):
+    def block(k, zz, far):
+        yy, xx = yx(a_me, 1 - b_me if far else b_me)
+        return W.at[k, zz, yy, xx]
+
+    def z_copy(k, dz, far=0):
+        at = block(k, z, far)
+        i = k * 8 + far * 4
+        return remote(at, at, zs.at[i + dz], zr.at[i + z], dev(c, chip_of((z + dz) % 4, y, x)))
+
+    def z_wait(k, dz, far=0):
+        frm = (z + dz) % 4
+        at = block(k, frm, far)
+        i = k * 8 + far * 4
+        remote(at, at, zs.at[i + dz], zr.at[i + frm], dev(c, chip_of(frm, y, x))).wait_recv()
+
+    def b_copy(k, zz):
+        at = block(k, zz, 0)
+        return remote(at, at, bs.at[k * 4 + zz], br.at[k * 4 + zz], nb_b)
+
+    def a_copy(k, zz, far=0):
+        at = block(k, zz, far)
+        i = k * 8 + far * 4 + zz
+        return remote(at, at, as_.at[i], ar.at[i], nb_a)
+
+    def own(k):
+        b_copy(k, z).start()
+        a_copy(k, z).start()
+        for dz in range(1, 4):
+            z_copy(k, dz).start()
+
+    def pump_b(k):
+        if k in VIA_Z:
+            b_copy(k, z).wait_recv()
+            for dz in range(1, 4):
+                z_copy(k, dz, 1).start()
+            a_copy(k, z, 1).start()
         for dz in range(1, 4):
             frm = (z + dz) % 4
-            remote(W.at[k, frm, y, x], W.at[k, frm, y, x], zs.at[k * 3 + dz - 1], zr.at[k * 4 + frm], dev(c, chip_of(frm, y, x))).wait_recv()
-
-    def b_copy(k):
-        return remote(W.at[k, :, y, x], W.at[k, :, y, x], bs.at[k], br.at[k], nb_b)
-
-    def a_copy(k, i):
-        yy, xx = yx(a_me, b_me if i == 0 else 1 - b_me)
-        return remote(W.at[k, :, yy, xx], W.at[k, :, yy, xx], as_.at[k * 2 + i], ar.at[k * 2 + i], nb_a)
-
-    def pump_b(k):
-        z_wait(k)
-        b_copy(k).start()
-        a_copy(k, 0).start()
+            z_wait(k, dz)
+            if k not in VIA_Z:
+                b_copy(k, frm).start()
+            a_copy(k, frm).start()
 
     def pump_a(k):
-        b_copy(k).wait_recv()
-        a_copy(k, 1).start()
+        if k in VIA_Z:
+            for dz in range(1, 4):
+                z_wait(k, dz, 1)
+                a_copy(k, (z + dz) % 4, 1).start()
+        else:
+            for dz in range(4):
+                b_copy(k, (z + dz) % 4).wait_recv()
+                a_copy(k, (z + dz) % 4, 1).start()
+
+    def sends_done(k):
+        for dz in range(1, 4):
+            z_copy(k, dz).wait_send()
+            if k in VIA_Z:
+                z_copy(k, dz, 1).wait_send()
+            else:
+                b_copy(k, (z + dz) % 4).wait_send()
+        b_copy(k, z).wait_send()
+        for far in range(2):
+            for zz in range(4):
+                a_copy(k, zz, far).wait_send()
+
+    def pump(k):
+        if k + AHEAD < CHUNKS:
+            cast(k + AHEAD)
+            own(k + AHEAD)
+        if k < CHUNKS:
+            pump_b(k)
+        if 0 <= k - LAG_A < CHUNKS:
+            pump_a(k - LAG_A)
 
     def need(k):
-        a_copy(k, 0).wait_recv()
-        a_copy(k, 1).wait_recv()
-
-    E1[c, s] = msg[...]
-    peers_send(0, lambda p: msg, E1.at[c])
-
-    for k in range(CHUNKS):
+        for far in range(2):
+            for dz in range(4):
+                a_copy(k, (z + dz) % 4, far).wait_recv()
+
+    def cast(k):
         if k < 4:
             local[k].wait()
             W[k, z, y, x] = FIN[k].astype(BF)
@@ -557,14 +617,18 @@
         else:
             local[20 + k - 8].wait()
             W[k, z, y, x] = FIN[k].astype(BF)
-        for dz in range(1, 4):
-            z_copy(k, dz).start()
+
+    E1[c, s] = msg[0:8, :]
+    peers_send(0, lambda p: msg.at[0:8, :], E1.at[c])
+    for k in range(AHEAD):
+        cast(k)
+        own(k)
 
     local[24].wait()
     local[25].wait()
-    peers_wait(0, lambda p: msg, E1.at[c])
-    t_hidden = dot_nn(E1[c, :, 0, :].astype(BF), ENT[1016:1144, :].astype(BF)) + dot_nn(
-        E1[c, :, 1, :].astype(BF), ENT[1144:1272, :].astype(BF)
+    peers_wait(0, lambda p: msg.at[0:8, :], E1.at[c])
+    t_hidden = dot_nt(E1[c, :, 0, :].astype(BF), ENT[:, 1016:1144].astype(BF)) + dot_nt(
+        E1[c, :, 1, :].astype(BF), ENT[:, 1144:1272].astype(BF)
     )
     CND[0] = t_hidden
     t_act = (t_hidden * sigmoid(t_hidden)).astype(BF)
@@ -573,31 +637,39 @@
         E2S[q] = dot_nn(t_act, EX[:, q * 128 : q * 128 + 128].astype(BF))
     E2R[s] = E2S[s // 2]
     peers_send(1, lambda p: E2S.at[p // 2], E2R)
-    for q in range(8):
-        even = E1[c, 2 * q, 8:24, :]
-        odd = E1[c, 2 * q + 1, 8:24, :]
-        WPT[:, q * 128 : q * 128 + 128] = jnp.concatenate([even[:, :64], odd[:, :64]], axis=1)
-        WLT[:, q * 128 : q * 128 + 128] = jnp.concatenate([even[:, 64:], odd[:, 64:]], axis=1)
-    pump_b(0)
+    pump(0)
     hot = (
-        E1[c, :, 2, 0:1].astype(jnp.int32) == lax.broadcasted_iota(jnp.int32, (16, 1024), 1)
+        E1[c, :, 2, 0:1].astype(jnp.int32) + PDIM == lax.broadcasted_iota(jnp.int32, (16, ENTRIES), 1)
     ).astype(F32).astype(BF)
-    w_class = dot_nn(hot, ENT[16:1040, :].astype(BF))
+    w_class = dot_nt(hot, ENT[...].astype(BF))
+    pump(1)
+    local[26].wait()
     peers_wait(1, lambda p: E2S.at[p // 2], E2R)
     temb = jnp.sum(E2R[...], axis=0)
     cond = jnp.where(x == 0, temb[:, :64], temb[:, 64:]) + w_class
     CND[1] = cond
     cond_low = (cond * sigmoid(cond)).astype(BF)
     CP[c, 0, :, 0:64] = cond_low.astype(F32)
-    local[26].wait()
     for k in range(8):
         w_k = WMOD[:, k * 1024 : k * 1024 + 1024] if k < 6 else EX[:, (k - 5) * 1024 : (k - 4) * 1024]
-        E3S[:, k, :] = dot_nn(cond_low, w_k.astype(BF))
+        DMF[0, k] = dot_nn(cond_low, w_k.astype(BF))
+
+    @pl.loop(0, 16)
+    def _(l):
+        part = DMF[0, :, l, :]
+        E3S[l] = jnp.concatenate([part[:, :512], part[:, 512:]], axis=0).astype(BF)
+
     E3R[s] = E3S[s]
     peers_send(2, lambda p: E3S.at[p], E3R)
-    pump_b(1)
-    pump_a(0)
-
+    EDG[s] = msg[8:24, :]
+    peers_send(7, lambda p: msg.at[8:24, :], EDG)
+    pump(2)
+
+    peers_wait(7, lambda p: msg.at[8:24, :], EDG)
+    for q in range(8):
+        even, odd = EDG[2 * q], EDG[2 * q + 1]
+        WPT[:, q * 128 : q * 128 + 128] = jnp.concatenate([even[:, :64], odd[:, :64]], axis=1)
+        WLT[:, q * 128 : q * 128 + 128] = jnp.concatenate([even[:, 64:], odd[:, 64:]], axis=1)
     for n in range(4):
         cols = slice(n * 256, n * 256 + 256)
         X0[:, cols] = dot_nn(pt[0].astype(BF), WPT[:, cols].astype(BF))
@@ -608,8 +680,12 @@
         X0[rows_at(i, 16), 512:1024] += jnp.broadcast_to(pos[pl.ds(i, 1), :], (16, 512))
 
     DACC[...] = jnp.zeros_like(DACC)
+    pump(3)
     peers_wait(2, lambda p: E3S.at[p], E3R)
-    MODS[...] = jnp.sum(E3R[...], axis=0)
+    parts = E3R[0].astype(F32)
+    for i in range(1, 16):
+        parts += E3R[i].astype(F32)
+    MODS[...] = jnp.concatenate([parts[0:8], parts[8:16]], axis=1)
 
     def mod_row(k):
         return MODS[k : k + 1, :]
@@ -623,10 +699,7 @@
 
     modulated(X0, ATI, 0, 1)
     twin_copy(0, ATI.at[c], ATI.at[c]).start()
-    pump_b(2)
-    pump_a(1)
-    pump_b(3)
-    pump_a(2)
+    pump(4)
     twin_copy(0, ATI.at[o], ATI.at[o]).wait_recv()
 
     def w_cols(k, n):
@@ -640,8 +713,7 @@
             lat, n = t // 2, t % 2
             QKV[j, lat, :, rows_at(n, 256)] = dot_nn(ATI[lat], w_cols(j, n)).astype(BF)
 
-        pump_b(4 + j)
-        pump_a(3 + j)
+        pump(5 + j)
 
     lane = lax.broadcasted_iota(jnp.int32, (1, LANES), 1)
     first = lane < 64
@@ -662,10 +734,7 @@
     twin_copy(1, MIX.at[c], MIX.at[c]).start()
     need(3)
     twin_copy(2, W.at[3], WP).start()
-    pump_b(7)
-    pump_a(6)
-    pump_b(8)
-    pump_a(7)
+    pump(8)
     twin_copy(1, MIX.at[o], MIX.at[o]).wait_recv()
     twin_copy(2, W.at[3], WP).wait_recv()
 
@@ -692,8 +761,7 @@
 
     modulated(RSD, MLI, 3, 4)
     twin_copy(3, MLI.at[c], MLI.at[c]).start()
-    pump_b(9)
-    pump_a(8)
+    pump(9)
     twin_copy(3, MLI.at[o], MLI.at[o]).wait_recv()
     for j in range(4):
         need(4 + j)
@@ -713,11 +781,8 @@
             )
             GD[lat, :, cols] = slope.astype(BF)
 
-        if j < 2:
-            pump_b(10 + j)
-            pump_a(9 + j)
-        if j == 2:
-            pump_a(11)
+        if j < 3:
+            pump(10 + j)
 
     for ch in range(2):
         need(8 + 2 * ch)
@@ -790,57 +855,143 @@
         yy, xx = yx(a_me, 1 - b_me)
         return remote(G.at[k, :, yy, xx], r2_of(k), s2s.at[k], s2r.at[k], nb_b)
 
-    def s3_copy(k, dz):
+    def s2_single(k):
+        yy, xx = yx(a_me, 1 - b_me)
+        return remote(G.at[k, z, yy, xx], r2_of(k).at[z], s2s.at[k], s2r.at[k], nb_b)
+
+    def s3_copy(k, dz, far=0):
         zt = (z + dz) % 4
-        return remote(G.at[k, zt, y, x], r3_of(k).at[z], s3s.at[k * 3 + dz - 1], s3r.at[k * 4 + z], dev(c, chip_of(zt, y, x)))
+        yy, xx = yx(a_me, 1 - b_me if far else b_me)
+        dst = (r2_of(k) if far else r3_of(k)).at[z]
+        i = k * 8 + far * 4
+        return remote(G.at[k, zt, yy, xx], dst, s3s.at[i + dz], s3r.at[i + z], dev(c, chip_of(zt, y, x)))
+
+    def s3_wait(k, dz, far=0):
+        frm = (z + dz) % 4
+        dst = (r2_of(k) if far else r3_of(k)).at[frm]
+        i = k * 8 + far * 4
+        remote(G.at[k, frm, y, x], dst, s3s.at[i + dz], s3r.at[i + frm], dev(c, chip_of(frm, y, x))).wait_recv()
 
     def s1(k):
         for b in range(2):
             s1_copy(k, b).start()
 
+    def sum_a(k, zz, far):
+        b = 1 - b_me if far else b_me
+        yy, xx = yx(a_me, b)
+        return G[k, zz, yy, xx].astype(F32) + r1_of(k, b)[zz].astype(F32)
+
+    def store(k, zz, far, value):
+        yy, xx = yx(a_me, 1 - b_me if far else b_me)
+        G[k, zz, yy, xx] = value.astype(BF)
+
     def s2(k):
         for b in range(2):
             s1_copy(k, b).wait_recv()
-        yy, xx = yx(a_me, 1 - b_me)
-
-        @pl.loop(0, 4)
-        def _(zz):
-            total = G[k, zz, yy, xx].astype(F32) + r1_of(k, 1 - b_me)[zz].astype(F32)
-            G[k, zz, yy, xx] = total.astype(BF)
-
-        s2_copy(k).start()
+        if k in VIA_Z:
+            for dz in range(1, 4):
+                for far in range(2):
+                    store(k, (z + dz) % 4, far, sum_a(k, (z + dz) % 4, far))
+                    s3_copy(k, dz, far).start()
+        else:
+            @pl.loop(0, 4)
+            def _(zz):
+                store(k, zz, 1, sum_a(k, zz, 1))
+
+            s2_copy(k).start()
 
     def s3(k):
-        s2_copy(k).wait_recv()
-
-        def total(zz):
-            return (
-                G[k, zz, y, x].astype(F32) + r1_of(k, b_me)[zz].astype(F32) + r2_of(k)[zz].astype(F32)
-            )
-
-        FIN[k] = total(z)
-
-        @pl.loop(1, 4)
-        def _(dz):
-            zt = (z + dz) % 4
-            G[k, zt, y, x] = total(zt).astype(BF)
-
-        for dz in range(1, 4):
-            s3_copy(k, dz).start()
+        if k in VIA_Z:
+            for far in (1, 0):
+                total = sum_a(k, z, far)
+                for dz in range(1, 4):
+                    s3_wait(k, dz, far)
+                    total += (r2_of(k) if far else r3_of(k))[(z + dz) % 4].astype(F32)
+                if far:
+                    store(k, z, 1, total)
+                    s2_single(k).start()
+                else:
+                    FIN[k] = total
+        else:
+            s2_copy(k).wait_recv()
+            for dz in range(1, 4):
+                zt = (z + dz) % 4
+                store(k, zt, 0, sum_a(k, zt, 0) + r2_of(k)[zt].astype(F32))
+                s3_copy(k, dz).start()
+            FIN[k] = sum_a(k, z, 0) + r2_of(k)[z].astype(F32)
 
     def s4(k):
-        for dz in range(1, 4):
-            frm = (z + dz) % 4
-            remote(G.at[k, frm, y, x], r3_of(k).at[frm], s3s.at[k * 3 + dz - 1], s3r.at[k * 4 + frm], dev(c, chip_of(frm, y, x))).wait_recv()
         total = FIN[k]
-        for dz in range(1, 4):
-            total += r3_of(k)[(z + dz) % 4].astype(F32)
+        if k in VIA_Z:
+            s2_single(k).wait_recv()
+            total += r2_of(k)[z].astype(F32)
+        else:
+            for dz in range(1, 4):
+                s3_wait(k, dz)
+                total += r3_of(k)[(z + dz) % 4].astype(F32)
         FIN[k] = total
         SQ[...] += fold(total * total)
 
-    def to_outputs(i, src, dst):
-        pltpu.make_async_copy(src, dst, f_l.at[i]).start()
-        remote(src, dst, f_s.at[i], f_r.at[i], twin).start()
+    def sums_done(k):
+        for b in range(2):
+            s1_copy(k, b).wait_send()
+        (s2_single if k in VIA_Z else s2_copy)(k).wait_send()
+        for dz in range(1, 4):
+            s3_copy(k, dz).wait_send()
+            if k in VIA_Z:
+                s3_copy(k, dz, 1).wait_send()
+
+    def result_copies(i):
+        if i < 4:
+            k = 8 + i
+            src = FIN.at[k]
+            dst = g_out.at[
+                pl.ds(pl.multiple_of(c * 128 + (i % 2) * 64, 64), 64), pl.ds((i // 2) * 512, 512)
+            ]
+        elif i < 20:
+            j = i - 4
+            src = FIN.at[4 + j // 8 + 2 * (j % 2), :, pl.ds(((j % 8) // 2) * 128, 128)]
+            dst = g_in.at[:, pl.ds(pl.multiple_of(10240 + 256 * j + c * 128, 128), 128)]
+        else:
+            j = i - 20
+            src = FIN.at[j]
+            dst = g_in.at[:, pl.ds(pl.multiple_of(6144 + 1024 * j + c * 512, 512), 512)]
+        return pltpu.make_async_copy(src, dst, f_l.at[i]), remote(src, dst, f_s.at[i], f_r.at[i], twin)
+
+    def send_result(k):
+        if k >= 8:
+            span = (k - 8,)
+        elif k == 7:
+            for half in range(2):
+                for q in range(4):
+                    cols = slice(q * 128, q * 128 + 128)
+                    low, high = FIN[4 + half, :, cols], FIN[6 + half, :, cols]
+                    FIN[4 + half, :, cols] = jnp.concatenate([low[:, 0:64], high[:, 0:64]], axis=1)
+                    FIN[6 + half, :, cols] = jnp.concatenate([low[:, 64:128], high[:, 64:128]], axis=1)
+            span = range(4, 20)
+        elif k >= 4:
+            span = ()
+        else:
+            span = (20 + k,)
+        for i in span:
+            for copy in result_copies(i):
+                copy.start()
+
+    def step(t):
+        if t + LEAD < CHUNKS:
+            if t + LEAD == 4:
+                pl.semaphore_wait(cred_a, 1)
+            s1(ORDER[t + LEAD])
+        if t == 4:
+            pl.semaphore_wait(cred_b, 1)
+            pl.semaphore_wait(cred_z, 3)
+        if t < CHUNKS:
+            s2(ORDER[t])
+        if 0 <= t - LAG3 < CHUNKS:
+            s3(ORDER[t - LAG3])
+        if 0 <= t - LAG4 < CHUNKS:
+            s4(ORDER[t - LAG4])
+            send_result(ORDER[t - LAG4])
 
     def grad_tiles(k, left, right):
         @pl.loop(0, 4)
@@ -857,14 +1008,11 @@
                 lambda r: ACT[:, :, pl.ds(pl.multiple_of(rh * 1024 + r * 256, 256), 256)].reshape(512, 256),
                 DMO[:, :, ch * 512 : ch * 512 + 512].reshape(512, 512),
             )
-            s1(k)
+            if 2 * ch + rh < LEAD:
+                s1(k)
 
     for k in range(CHUNKS):
-        for dz in range(1, 4):
-            z_copy(k, dz).wait_send()
-        b_copy(k).wait_send()
-        a_copy(k, 0).wait_send()
-        a_copy(k, 1).wait_send()
+        sends_done(k)
 
     @pl.loop(0, 16)
     def _(t):
@@ -902,15 +1050,13 @@
     for dz in range(1, 4):
         pl.semaphore_signal(cred_z, 1, device_id=dev(c, chip_of((z + dz) % 4, y, x)), device_id_type=MESH)
 
-    pl.semaphore_wait(cred_a, 1)
+    step(0)
     for j in range(4):
         grad_tiles(
             4 + j,
             lambda r: MLI[:, :, rows_at(r, 256)].reshape(512, 256),
             GD[:, :, j * 512 : j * 512 + 512].reshape(512, 512),
         )
-        s1(4 + j)
-    s2(8)
     received(7)
 
     @pl.loop(0, TOK // 32)
@@ -944,8 +1090,7 @@
     def _(n):
         DMX[c, :, rows_at(n, 256)] = mixed_back(c, n)
 
-    s2(9)
-    s3(8)
+    step(1)
     twin_copy(9, DAO.at[o, :, dao_mine], DAO.at[o, :, dao_mine]).wait_recv()
 
     @pl.loop(0, 4)
@@ -953,11 +1098,9 @@
         left = MIX[r // 2, :, :, rows_at(r % 2, 256)].reshape(512, 256)
         G[3, r] = dot_tn(left, DAO[:, :, dao_mine].reshape(512, 512)).astype(BF).reshape(2, 2, 64, 512)
 
-    s1(3)
     twin_copy(10, DMS, DMX.at[o]).wait_recv()
 
-    @pl.loop(0, 8)
-    def _(t):
+    def attention_back(t):
         lat, cols = t // 4, rows_at(t % 4, 128)
         q, k, v = QKV[0, lat, :, cols], QKV[1, lat, :, cols], QKV[2, lat, :, cols]
         dm = DMX[lat, :, cols]
@@ -972,20 +1115,18 @@
         for j in range(3):
             QKV[j, lat, :, cols] = jnp.where(first, res[0][j], res[1][j]).astype(BF)
 
+    for half in range(2):
+        pl.loop(4 * half, 4 * half + 4)(attention_back)
+        step(2 + half)
+    for ch in range(2):
+        twin_copy(7 + ch, SND.at[ch], RCV.at[ch]).wait_send()
+    data_back(0, 3, lambda j, lat: QKV[j, lat], 11)
     for j in range(3):
         grad_tiles(
             j,
             lambda r: ATI[:, :, rows_at(r, 256)].reshape(512, 256),
             QKV[j].reshape(512, 512),
         )
-        s1(j)
-    s2(10)
-    s3(9)
-    for ch in range(2):
-        twin_copy(7 + ch, SND.at[ch], RCV.at[ch]).wait_send()
-    data_back(0, 3, lambda j, lat: QKV[j, lat], 11)
-    s2(11)
-    s3(10)
     received(11)
 
     @pl.loop(0, TOK // 32)
@@ -1007,11 +1148,7 @@
         B3S[q] = GLP[:, q * 128 : q * 128 + 128]
     B3R[s] = B3S[s // 2]
     peers_send(4, lambda p: B3S.at[p // 2], B3R)
-    pl.semaphore_wait(cred_b, 1)
-    pl.semaphore_wait(cred_z, 3)
-    s3(11)
-    s2(4)
-    s4(8)
+    step(4)
     peers_wait(3, lambda p: DMB.at[c, s], DMB.at[c])
     twin_copy(13, DMB.at[c], DMB.at[c]).start()
 
@@ -1033,9 +1170,7 @@
     B2S[...] = jnp.concatenate([d_temb, d_temb], axis=1)
     B2R[s] = B2S[...]
     peers_send(5, lambda p: B2S, B2R)
-    s2(5)
-    s3(4)
-    s4(9)
+    step(5)
     peers_wait(4, lambda p: B3S.at[p // 2], B3R)
     B3D[c] = jnp.sum(B3R[...], axis=0)
     twin_copy(14, B3D.at[c], B3D.at[c]).start()
@@ -1049,9 +1184,7 @@
     twin_copy(15, DTA.at[c], DTA.at[c]).start()
     twin_copy(16, CP.at[c], CP.at[c]).start()
     twin_copy(17, E1.at[c], E1.at[c]).start()
-    s2(6)
-    s3(5)
-    s4(10)
+    step(6)
     twin_copy(13, DMB.at[o], DMB.at[o]).wait_recv()
     unpack(o)
     twin_copy(14, B3D.at[o], B3D.at[o]).wait_recv()
@@ -1077,80 +1210,32 @@
             EX[:, (k - 5) * 1024 : (k - 4) * 1024] = grad
     mod_out = pltpu.make_async_copy(WMOD, g_in.at[:, pl.ds(0, 6144)], st_sem.at[26])
     mod_out.start()
-    s2(7)
-    s3(6)
-    s4(11)
+    step(7)
     grad = dot_tn(packed(1).astype(BF), jnp.concatenate([DTA[0], DTA[1]], axis=0).astype(BF))
     small += square_half(grad)
     EX[:, 0:1024] = grad
     sums = B3D[0] + B3D[1]
     sums = jnp.where(x == 0, sums[:, 0:64], sums[:, 64:128])
-    small += square_half(sums)
-    ENT[0:16, :] = sums[0:16]
+    small += square_half(sums[16:32])
     wide = jnp.concatenate(
         [jnp.concatenate([sums[16:32], jnp.zeros((16, 64), F32)], axis=1), jnp.zeros((112, 128), F32)], axis=0
     )
     EX[:, 3072:3088] = wide.T[0:64, 0:16]
-    labels = jnp.sum(E1[0, :, 3, :] + E1[1, :, 3, :], axis=0, keepdims=True).astype(jnp.int32)
-    d_cond_both = jnp.concatenate([packed(2), jnp.zeros((96, 64), F32)], axis=0)
-    for i in range(5):
-        rows = lax.broadcasted_iota(jnp.int32, (200, LANES), 0) + i * 200
-        hot = (rows == labels).astype(F32)
-        grad = lax.dot_general(
-            hot, d_cond_both, (((1,), (0,)), ((), ())), preferred_element_type=F32, precision=highest
-        )
-        small += square_half(grad)
-        ENT[16 + i * 200 : 216 + i * 200, :] = grad
-    d_thidden = packed(3).astype(BF)
-    for i in range(2):
-        femb = jnp.concatenate([E1[0, :, i, :], E1[1, :, i, :]], axis=0).astype(BF)
-        grad = dot_tn(femb, d_thidden)
-        small += square_half(grad)
-        ENT[1016 + i * 128 : 1144 + i * 128, :] = grad
-
-    s2(3)
-    s3(7)
-    s4(4)
-    s2(0)
-    s3(3)
-    s4(5)
-    s2(1)
-    s3(0)
-    s4(6)
-    s2(2)
-    s3(1)
-    s4(7)
-    for half in range(2):
-        for q in range(4):
-            cols = slice(q * 128, q * 128 + 128)
-            low, high = FIN[4 + half, :, cols], FIN[6 + half, :, cols]
-            FIN[4 + half, :, cols] = jnp.concatenate([low[:, 0:64], high[:, 0:64]], axis=1)
-            FIN[6 + half, :, cols] = jnp.concatenate([low[:, 64:128], high[:, 64:128]], axis=1)
-    outs = []
-    for ch in range(2):
-        for rh in range(2):
-            outs.append((
-                FIN.at[8 + 2 * ch + rh],
-                g_out.at[pl.ds(pl.multiple_of(c * 128 + rh * 64, 64), 64), pl.ds(ch * 512, 512)],
-            ))
-    for j in range(16):
-        outs.append((
-            FIN.at[4 + j // 8 + 2 * (j % 2), :, pl.ds(((j % 8) // 2) * 128, 128)],
-            g_in.at[:, pl.ds(pl.multiple_of(10240 + 256 * j + c * 128, 128), 128)],
-        ))
-    for j in (3, 0, 1, 2):
-        outs.append((FIN.at[j], g_in.at[:, pl.ds(pl.multiple_of(6144 + 1024 * j + c * 512, 512), 512)]))
-    for i in range(20):
-        to_outputs(i, *outs[i])
-    s3(2)
-    s4(3)
-    to_outputs(20, *outs[20])
-    s4(0)
-    to_outputs(21, *outs[21])
-    s4(1)
-    to_outputs(22, *outs[22])
-    s4(2)
-    to_outputs(23, *outs[23])
+    def both(value):
+        return jnp.concatenate([value(0), value(1)], axis=0)
+
+    index = lax.broadcasted_iota(jnp.int32, (32, ENTRIES), 1)
+    hot = (both(lambda g: E1[g, :, 2, 0:1]).astype(jnp.int32) + PDIM == index).astype(F32)
+    grad = dot_tn_exact(packed(2), hot)
+    spot = lax.broadcasted_iota(jnp.int32, (16, ENTRIES), 0) == index[0:16]
+    grad += dot_tn_exact(sums[0:16], spot.astype(F32))
+    ENT[...] = grad
+    femb = both(lambda g: jnp.concatenate([E1[g, :, 0, :], E1[g, :, 1, :]], axis=1)).astype(BF)
+    ENT[:, PDIM + NCLS :] = dot_tn(packed(3).astype(BF), femb)
+    small += square_half(ENT[...])
+
+    for t in range(8, CHUNKS + LAG4):
+        step(t)
 
     def total_of(value):
         return jnp.sum(jnp.sum(value, axis=0, keepdims=True), axis=1, keepdims=True)
@@ -1167,15 +1252,11 @@
     stats[...] = NSD[0] + NSD[1]
 
     mod_out.wait()
-    for i, (src, dst) in enumerate(outs):
-        pltpu.make_async_copy(src, dst, f_l.at[i]).wait()
-        remote(src, dst, f_s.at[i], f_r.at[i], twin).wait()
+    for i in range(24):
+        for copy in result_copies(i):
+            copy.wait()
     for k in range(CHUNKS):
-        for b in range(2):
-            s1_copy(k, b).wait_send()
-        s2_copy(k).wait_send()
-        for dz in range(1, 4):
-            s3_copy(k, dz).wait_send()
+        sums_done(k)
     twin_copy(0, ATI.at[c], ATI.at[c]).wait_send()
     twin_copy(1, MIX.at[c], MIX.at[c]).wait_send()
     twin_copy(2, W.at[3], WP).wait_send()
@@ -1203,15 +1284,15 @@
         vm((2, TOK, 2048), BF), vm((2, TOK, 2048), BF), vm((2, TOK, 1024), BF), vm((2, TOK, 1024), BF),
         vm((2, TOK, 512), BF), vm((TOK, 512), BF),
         *[vm((TOK, 1024), F32)] * 5, vm((2, TOK, 512), F32), vm((2, TOK, 512), F32),
-        vm((64, 6144), F32), vm((2, 16, 24, 128), F32), vm((8, 16, 128), F32), vm((16, 16, 128), F32),
-        vm((16, 8, 1024), F32), vm((16, 8, 1024), F32), vm((2, 16, 16, 512), BF), vm((2, 8, 16, 1024), F32),
+        vm((64, 6144), F32), vm((2, 16, 8, 128), F32), vm((16, 16, 128), F32), vm((8, 16, 128), F32), vm((16, 16, 128), F32),
+        vm((16, 16, 512), BF), vm((16, 16, 512), BF), vm((2, 16, 16, 512), BF), vm((2, 8, 16, 1024), F32),
         vm((16, 128), F32), vm((16, 16, 128), F32), vm((2, 16, 1024), F32), vm((2, 4, 16, 128), F32), vm((2, 16, 64), F32),
         vm((8, 32, 128), F32), vm((16, 32, 128), F32), vm((2, 32, 128), F32),
         vm((8, 128), F32), vm((16, 8, 128), F32), vm((2, 8, 128), F32),
         vm((8, 1024), F32), vm((8, 8, 1024), F32), vm((16, 1024), F32), vm((16, 1024), F32), vm((32, 1024), F32),
         vm((8, 512), F32), vm((8, 16), F32),
-        dma((27,)), dma((7, 16)), dma((7, 16)), dma((36,)), dma((48,)), dma((12,)), dma((12,)), dma((24,)), dma((24,)),
-        dma((24,)), dma((24,)), dma((12,)), dma((12,)), dma((36,)), dma((48,)), dma((19,)), dma((19,)),
+        dma((27,)), dma((8, 16)), dma((8, 16)), dma((96,)), dma((96,)), dma((48,)), dma((48,)), dma((96,)), dma((96,)),
+        dma((24,)), dma((24,)), dma((12,)), dma((12,)), dma((96,)), dma((96,)), dma((19,)), dma((19,)),
         dma((24,)), dma((24,)), dma((24,)),
         pltpu.SemaphoreType.REGULAR, pltpu.SemaphoreType.REGULAR, pltpu.SemaphoreType.REGULAR,
     ]
@@ -1254,7 +1335,7 @@
     grid = noisy.shape[-1] // PATCH
     pos = position_table(grid, D)[:grid, : D // 2]
     g_in, g_out, g_entry, g_exit, stats = fused_step(
-        msg, pt, pos, block_in[0], block_out[0], entry_table, exit_proj
+        msg, pt, pos, block_in[0], block_out[0], entry_table.T, exit_proj
     )
     loss = stats[1, 0]
     grad_norm = jnp.sqrt(stats[0, 0])
@@ -1263,7 +1344,7 @@
     for weight, first, second, grad, rate in (
         (block_in, block_in_first, block_in_second, g_in[None], rate_main),
         (block_out, block_out_first, block_out_second, g_out[None], rate_main),
-        (entry_table, entry_first, entry_second, g_entry, rate_edge),
+        (entry_table, entry_first, entry_second, g_entry.T, rate_edge),
         (exit_proj, exit_first, exit_second, g_exit, rate_main),
     ):
         outs.extend(adam_step(weight, first, second, grad, factor, rate))

time: 390 us -> 304 us (0.78)
  Pallas kernels: 351 us -> 274 us
  local copies, waits for them, and re-layouts: 13.1 us -> 7.24 us
    pallas_call x1, Pallas kernels: 351 us -> 274 us  [fused_step(): pl.pallas_call(step_kernel, out_shape=(shape(block_in.shape, F32), shape(...]
    unnamed x26, local copies, waits for them, and re-layouts: 7.24 us -> 0.71 us
where the time goes in v2:
time: 304 us
  Pallas kernels  274 us (90%)
  other arithmetic  18.3 us (6%)
  local copies, waits for them, and re-layouts  7.24 us (2%)
  between operations  4.01 us (1%)
    pallas_call x1, Pallas kernels, fused_step(): pl.pallas_call(step_kernel, out_shape=(shape(block_in.shape, F32), shape(...  274 us
    convert_element_type x4, other arithmetic, adam_step(): return (weight_new, first_new, second_new, weight_new.astype(jnp.bfloat16))  15.7 us

profile of v2, /device:TPU:0, one launch (start us, length us, event | category | flops | bytes accessed | tf_op | source)
XLA Modules:
  0.0 303.8 jit_solution(13261912753717234658)
XLA Ops:
  2.0 0.1 sine_convert_fusion
  2.0 0.8 slice.16
  2.8 0.1 copy.43
  2.9 0.8 slice.15
  3.6 0.1 copy.42
  3.7 0.1 pad_maximum_fusion.2
  3.8 1.2 concatenate.20.msg
  5.0 1.0 multiply_sine_fusion
  6.0 0.6 pad_maximum_fusion.1.pos
  6.6 0.9 pad_maximum_fusion
  7.5 0.5 copy.39
  8.0 1.1 copy.40
  9.0 0.1 reshape.111
  9.2 0.8 copy.41.pt
  10.0 274.2 %shard_map.295 = (f32[64,14336]{1,0:T(8,128)}, f32[256,1024]{1,0:T(8,128)}, f32[64,1272]{1,0:T(8,128)}, f32[64,3088]{1,0:T(8,128)}, f32[8,128]{1,0:T(8,128)}) custom-call(f32[24,128]{1,0:T(8,128)} %concatenate.20.msg, f32[2,256,16]{2,1,0:T(8,128)} %copy.41.pt, f32[16,512]{1,0:T(8,128)} %pad_maximum_fusion.1.pos, f32[64,14336]{1,0:T(8,128)} %bitcast.42, ...), custom_call_target="tpu_custom_call" | custom-call | flops 20999999488 | bytes 20000000 | tf_op jit(solution)/shard_map/pallas_call | solution.py:1302
  284.2 1.3 fusion.19
  286.3 0.0 copy-start.1
  286.3 0.0 copy-start.2
  286.3 10.0 %fusion.16 = (bf16[1,64,14336]{2,1,0:T(8,128)(2,1)}, f32[1,64,14336]{2,1,0:T(8,128)}, f32[1,64,14336]{2,1,0:T(8,128)}, f32[1,64,14336]{2,1,0:T(8,128)}) fusion(f32[1,64,14336]{2,1,0:T(8,128)} %param.20, f32[64,14336]{1,0:T(8,128)} %get-tuple-element.24, f32[]{:T(128)S(6)} %div.61, f32[1,64,14336]{2,1,0:T(8,128)} %param.21, f32[1,64,14336]{2,1,0:T(8,128)} %param.22), kind=kLoop, calls=%fused_computation.36 | loop fusion | flops 14680064 | bytes 27525124 | tf_op jit(solution)/shard_map/convert_element_type | solution.py:90
  296.3 0.0 copy-start.6
  296.4 2.5 fusion.13
  298.9 0.5 copy-done.7
  299.4 2.0 fusion.9
  301.4 1.2 fusion.11
  (26 shorter events, 0.1 us)
Async XLA Ops:
  286.3 10.0 %copy-start = (f32[1,256,1024]{2,1,0:T(8,128)S(1)}, f32[1,256,1024]{2,1,0:T(8,128)}, u32[]{:S(2)}) copy-start(f32[1,256,1024]{2,1,0:T(8,128)} %param.23) | copy-start | bytes 3145732
  286.3 10.0 %copy-start.1 = (f32[1,256,1024]{2,1,0:T(8,128)S(1)}, f32[1,256,1024]{2,1,0:T(8,128)}, u32[]{:S(2)}) copy-start(f32[1,256,1024]{2,1,0:T(8,128)} %param.24) | copy-start | bytes 3145732
  286.3 10.0 %copy-start.2 = (f32[1,256,1024]{2,1,0:T(8,128)S(1)}, f32[1,256,1024]{2,1,0:T(8,128)}, u32[]{:S(2)}) copy-start(f32[1,256,1024]{2,1,0:T(8,128)} %param.25) | copy-start | bytes 3145732
  286.3 10.0 %copy-start.3 = (f32[256,1024]{1,0:T(8,128)S(1)}, f32[256,1024]{1,0:T(8,128)}, u32[]{:S(2)}) copy-start(f32[256,1024]{1,0:T(8,128)} %get-tuple-element.25) | copy-start | bytes 3145732
  296.3 2.5 copy-start.4
  296.3 2.5 copy-start.5
  296.3 2.5 copy-start.6
  296.3 3.0 %copy-start.7 = (f32[64,3088]{1,0:T(8,128)S(1)}, f32[64,3088]{1,0:T(8,128)}, u32[]{:S(2)}) copy-start(f32[64,3088]{1,0:T(8,128)} %get-tuple-element.27) | copy-start | bytes 2371588
  298.8 2.6 copy-start.8
  298.8 2.6 copy-start.9
  298.8 2.6 copy-start.10
  298.8 2.6 copy-start.11

commit v3 on v2

--- a/solution.py
+++ b/solution.py
@@ -368,15 +368,20 @@
 F32 = jnp.float32
 MESH = pl.DeviceIdType.MESH
 TOK = 256
+TILE = 128
 LANES = 128
 CHUNKS = 12
-AHEAD = 2
-VIA_Z = ()
+START = (4, 2)
+OWN_AT = ((), (4,), (5, 6), (7, 8), (9, 10), (11,))
+Z_AT = ((2,), (3,), (4,), (5,), (6, 7), (8,), (9,), (10,), (11,))
+VIA_Z = (1, 3, 5, 7, 9, 11)
+SUM_VIA_Z = (0, 3, 6)
 LEAD = 3
-LAG3 = 1
-LAG4 = 2
+LAGS = (0, 1, 2, 3)
 LAG_A = 1
-ORDER = (8, 9, 10, 11, 4, 5, 6, 7, 3, 0, 1, 2)
+UNITS = tuple((k, 0, 64) for k in (8, 9, 10, 11, 4, 5, 6, 7, 3, 0, 1)) + tuple((2, 16 * i, 16) for i in range(4))
+NU = len(UNITS)
+SMALL = 11
 
 
 def dot_nn(left, right):
@@ -395,6 +400,14 @@
     return lax.dot_general(
         left, right, (((0,), (0,)), ((), ())), preferred_element_type=F32, precision=highest
     )
+
+
+def to_tile(value):
+    return jnp.concatenate([value[0:8], value[8:16]], axis=1)
+
+
+def from_tile(value):
+    return jnp.concatenate([value[:, 0:64], value[:, 64:128]], axis=0)
 
 
 def sigmoid(value):
@@ -429,16 +442,16 @@
 
 
 def step_kernel(
-    msg, pt, pos, bi, bo, ent_in, ex_in,
+    msg, edge, pt, pos, bi, bo, ent_in, ex_in,
     g_in, g_out, ENT, EX, stats,
-    W, WP, G, R1, R2, R3, FIN,
+    W, WP, G, R1, R2, R3, PF, FIN,
     ATI, QKV, MIX, MLI, ACT, GD, DMO, DAO, DMX, DMS,
     X0, AO, RSD, MO, X1, SND, RCV,
     WMOD, E1, EDG, E2S, E2R, E3S, E3R, DMB, DMF, B2S, B2R, DTA, CP, CND,
-    B3S, B3R, B3D, NSS, NSR, NSD, MODS, DACC, WPT, WLT, GLP, SQ, LOSS,
+    B3S, B3R, B3D, NSS, NSR, MODS, DACC, WPT, WLT, GLP, SQ, LOSS,
     st_sem, peer_s, peer_r, zs, zr, bs, br, as_, ar,
-    s1s, s1r, s2s, s2r, s3s, s3r, d_s, d_r, f_l, f_s, f_r,
-    cred_a, cred_b, cred_z,
+    s1s, s1r, s2s, s2r, szs, szr, pss, psr, d_s, d_r, f_l, f_s, f_r,
+    far_s, far_r, cred_a, cred_b, cred_z,
 ):
     c = lax.axis_index("rep")
     s = lax.axis_index("shard")
@@ -494,8 +507,11 @@
     def _(k):
         pl.semaphore_signal(barrier, 1, device_id=dev(c, (s + k) % 16), device_id_type=MESH)
 
-    pl.semaphore_signal(barrier, 1, device_id=twin, device_id_type=MESH)
-    pl.semaphore_wait(barrier, 16)
+    @pl.loop(0, 16)
+    def _(k):
+        pl.semaphore_signal(barrier, 1, device_id=dev(o, k), device_id_type=MESH)
+
+    pl.semaphore_wait(barrier, 31)
 
     def peers_copy(e, k, src_of, dst):
         peer = (s + k) % 16
@@ -534,6 +550,29 @@
         i = k * 8 + far * 4
         remote(at, at, zs.at[i + dz], zr.at[i + frm], dev(c, chip_of(frm, y, x))).wait_recv()
 
+    inner = jnp.logical_or(z == 1, z == 2)
+
+    def z_pass(k, far=0):
+        at = block(k, (z + 2) % 4, far)
+        i = k * 8 + far * 4
+        return remote(at, at, zs.at[i], zr.at[i + (z + 2) % 4], dev(c, chip_of(3 * (z - 1), y, x)))
+
+    def z_start(k, far=0):
+        z_copy(k, 2, far).start()
+        pl.when(z != 3)(lambda: z_copy(k, 1, far).start())
+        pl.when(z != 0)(lambda: z_copy(k, 3, far).start())
+
+    def z_arrived(k, dz, far=0):
+        z_wait(k, dz, far)
+        if dz == 2:
+            pl.when(inner)(lambda: z_pass(k, far).start())
+
+    def z_sent(k, far=0):
+        z_copy(k, 2, far).wait_send()
+        pl.when(z != 3)(lambda: z_copy(k, 1, far).wait_send())
+        pl.when(z != 0)(lambda: z_copy(k, 3, far).wait_send())
+        pl.when(inner)(lambda: z_pass(k, far).wait_send())
+
     def b_copy(k, zz):
         at = block(k, zz, 0)
         return remote(at, at, bs.at[k * 4 + zz], br.at[k * 4 + zz], nb_b)
@@ -544,28 +583,27 @@
         return remote(at, at, as_.at[i], ar.at[i], nb_a)
 
     def own(k):
+        cast(k)
         b_copy(k, z).start()
         a_copy(k, z).start()
-        for dz in range(1, 4):
-            z_copy(k, dz).start()
+
+    def far_start(k):
+        b_copy(k, z).wait_recv()
+        z_start(k, 1)
+        a_copy(k, z, 1).start()
 
     def pump_b(k):
-        if k in VIA_Z:
-            b_copy(k, z).wait_recv()
-            for dz in range(1, 4):
-                z_copy(k, dz, 1).start()
-            a_copy(k, z, 1).start()
-        for dz in range(1, 4):
+        for dz in (2, 1, 3):
             frm = (z + dz) % 4
-            z_wait(k, dz)
+            z_arrived(k, dz)
             if k not in VIA_Z:
                 b_copy(k, frm).start()
             a_copy(k, frm).start()
 
     def pump_a(k):
         if k in VIA_Z:
-            for dz in range(1, 4):
-                z_wait(k, dz, 1)
+            for dz in (2, 1, 3):
+                z_arrived(k, dz, 1)
                 a_copy(k, (z + dz) % 4, 1).start()
         else:
             for dz in range(4):
@@ -573,11 +611,11 @@
                 a_copy(k, (z + dz) % 4, 1).start()
 
     def sends_done(k):
-        for dz in range(1, 4):
-            z_copy(k, dz).wait_send()
-            if k in VIA_Z:
-                z_copy(k, dz, 1).wait_send()
-            else:
+        z_sent(k)
+        if k in VIA_Z:
+            z_sent(k, 1)
+        else:
+            for dz in range(1, 4):
                 b_copy(k, (z + dz) % 4).wait_send()
         b_copy(k, z).wait_send()
         for far in range(2):
@@ -585,9 +623,12 @@
                 a_copy(k, zz, far).wait_send()
 
     def pump(k):
-        if k + AHEAD < CHUNKS:
-            cast(k + AHEAD)
-            own(k + AHEAD)
+        for i in OWN_AT[k] if k < len(OWN_AT) else ():
+            own(i)
+        for i in Z_AT[k] if k < len(Z_AT) else ():
+            z_start(i)
+        if k + 1 in VIA_Z:
+            far_start(k + 1)
         if k < CHUNKS:
             pump_b(k)
         if 0 <= k - LAG_A < CHUNKS:
@@ -618,15 +659,16 @@
             local[20 + k - 8].wait()
             W[k, z, y, x] = FIN[k].astype(BF)
 
-    E1[c, s] = msg[0:8, :]
-    peers_send(0, lambda p: msg.at[0:8, :], E1.at[c])
-    for k in range(AHEAD):
-        cast(k)
+    E1[c, s] = msg[...]
+    peers_send(0, lambda p: msg, E1.at[c])
+    for k in range(START[0]):
         own(k)
+        if k < START[1]:
+            z_start(k)
 
     local[24].wait()
     local[25].wait()
-    peers_wait(0, lambda p: msg.at[0:8, :], E1.at[c])
+    peers_wait(0, lambda p: msg, E1.at[c])
     t_hidden = dot_nt(E1[c, :, 0, :].astype(BF), ENT[:, 1016:1144].astype(BF)) + dot_nt(
         E1[c, :, 1, :].astype(BF), ENT[:, 1144:1272].astype(BF)
     )
@@ -634,9 +676,11 @@
     t_act = (t_hidden * sigmoid(t_hidden)).astype(BF)
     CP[c, 1, :, 0:64] = t_act.astype(F32)
     for q in range(8):
-        E2S[q] = dot_nn(t_act, EX[:, q * 128 : q * 128 + 128].astype(BF))
-    E2R[s] = E2S[s // 2]
-    peers_send(1, lambda p: E2S.at[p // 2], E2R)
+        part = dot_nn(t_act, EX[:, q * 128 : q * 128 + 128].astype(BF))
+        for h in range(2):
+            E2S[2 * q + h] = to_tile(part[:, 64 * h : 64 * h + 64])
+    E2R[s] = E2S[s]
+    peers_send(1, lambda p: E2S.at[p], E2R)
     pump(0)
     hot = (
         E1[c, :, 2, 0:1].astype(jnp.int32) + PDIM == lax.broadcasted_iota(jnp.int32, (16, ENTRIES), 1)
@@ -644,9 +688,8 @@
     w_class = dot_nt(hot, ENT[...].astype(BF))
     pump(1)
     local[26].wait()
-    peers_wait(1, lambda p: E2S.at[p // 2], E2R)
-    temb = jnp.sum(E2R[...], axis=0)
-    cond = jnp.where(x == 0, temb[:, :64], temb[:, 64:]) + w_class
+    peers_wait(1, lambda p: E2S.at[p], E2R)
+    cond = from_tile(jnp.sum(E2R[...], axis=0)) + w_class
     CND[1] = cond
     cond_low = (cond * sigmoid(cond)).astype(BF)
     CP[c, 0, :, 0:64] = cond_low.astype(F32)
@@ -661,18 +704,18 @@
 
     E3R[s] = E3S[s]
     peers_send(2, lambda p: E3S.at[p], E3R)
-    EDG[s] = msg[8:24, :]
-    peers_send(7, lambda p: msg.at[8:24, :], EDG)
+    EDG[s] = edge[...]
+    peers_send(7, lambda p: edge, EDG)
     pump(2)
 
-    peers_wait(7, lambda p: msg.at[8:24, :], EDG)
+    peers_wait(7, lambda p: edge, EDG)
     for q in range(8):
         even, odd = EDG[2 * q], EDG[2 * q + 1]
         WPT[:, q * 128 : q * 128 + 128] = jnp.concatenate([even[:, :64], odd[:, :64]], axis=1)
         WLT[:, q * 128 : q * 128 + 128] = jnp.concatenate([even[:, 64:], odd[:, 64:]], axis=1)
     for n in range(4):
         cols = slice(n * 256, n * 256 + 256)
-        X0[:, cols] = dot_nn(pt[0].astype(BF), WPT[:, cols].astype(BF))
+        X0[:, cols] = dot_nn(pt[0].astype(BF), WPT[:, cols])
 
     @pl.loop(0, 16)
     def _(i):
@@ -691,9 +734,9 @@
         return MODS[k : k + 1, :]
 
     def modulated(src, dst, shift, scale):
-        @pl.loop(0, TOK // 32)
+        @pl.loop(0, TOK // TILE)
         def _(i):
-            r = rows_at(i, 32)
+            r = rows_at(i, TILE)
             hat, _ = normed(src[r, :])
             dst[c, r, :] = (hat * (1.0 + mod_row(scale)) + mod_row(shift)).astype(BF)
 
@@ -724,17 +767,20 @@
         e = jnp.exp(score - jnp.max(score, axis=-1, keepdims=True))
         return e / jnp.sum(e, axis=-1, keepdims=True)
 
-    @pl.loop(0, 8)
-    def _(t):
+    def attention(t):
         lat, cols = t // 4, rows_at(t % 4, 128)
         q, k, v = QKV[0, lat, :, cols], QKV[1, lat, :, cols], QKV[2, lat, :, cols]
         outs = [dot_nn(probs_of(q * m, k).astype(BF), v) for m in masks]
         MIX[c, lat, :, cols] = jnp.where(first, outs[0], outs[1]).astype(BF)
 
+    pl.loop(0, 4)(attention)
+    pump(8)
+    pl.loop(4, 8)(attention)
+
     twin_copy(1, MIX.at[c], MIX.at[c]).start()
     need(3)
     twin_copy(2, W.at[3], WP).start()
-    pump(8)
+    pump(9)
     twin_copy(1, MIX.at[o], MIX.at[o]).wait_recv()
     twin_copy(2, W.at[3], WP).wait_recv()
 
@@ -754,14 +800,14 @@
     proj(True)
     proj(False)
 
-    @pl.loop(0, TOK // 32)
+    @pl.loop(0, TOK // TILE)
     def _(i):
-        r = rows_at(i, 32)
+        r = rows_at(i, TILE)
         RSD[r, :] = X0[r, :] + mod_row(2) * AO[r, :]
 
     modulated(RSD, MLI, 3, 4)
     twin_copy(3, MLI.at[c], MLI.at[c]).start()
-    pump(9)
+    pump(10)
     twin_copy(3, MLI.at[o], MLI.at[o]).wait_recv()
     for j in range(4):
         need(4 + j)
@@ -781,8 +827,8 @@
             )
             GD[lat, :, cols] = slope.astype(BF)
 
-        if j < 3:
-            pump(10 + j)
+        if j < 2:
+            pump(11 + j)
 
     for ch in range(2):
         need(8 + 2 * ch)
@@ -815,15 +861,15 @@
     LOSS[...] = jnp.zeros_like(LOSS)
     GLP[...] = jnp.zeros_like(GLP)
 
-    @pl.loop(0, TOK // 32)
+    @pl.loop(0, TOK // TILE)
     def _(i):
-        r = rows_at(i, 32)
+        r = rows_at(i, TILE)
         mlp_out = both_parts(r)
         x1 = RSD[r, :] + mod_row(5) * mlp_out
         hat, inv = normed(x1)
         scale = 1.0 + mod_row(7)
         final_in = (hat * scale + mod_row(6)).astype(BF)
-        w_lin = WLT[...].astype(BF)
+        w_lin = WLT[...]
         error = dot_nt(final_in, w_lin) - pt[1, r, :]
         LOSS[...] += fold(error * error)
         d_pred = (2.0 * error / (TOK * PDIM)).astype(BF)
@@ -847,99 +893,165 @@
     def r3_of(k):
         return R3.at[k - 8] if k >= 8 else W.at[6 + k // 4, :, (k // 2) % 2, k % 2]
 
-    def s1_copy(k, b):
+    def rows_of(u):
+        return pl.ds(UNITS[u][1], UNITS[u][2])
+
+    def g_at(u, zz, a, b):
+        yy, xx = yx(a, b)
+        return G.at[UNITS[u][0], zz, yy, xx, rows_of(u)]
+
+    def b_of(far):
+        return 1 - b_me if far else b_me
+
+    def z_slot(u, i, far):
+        return (r2_of if far else r3_of)(UNITS[u][0]).at[i, rows_of(u)]
+
+    def pass_slot(u, i, far):
+        return PF.at[SUM_VIA_Z.index(u)] if far else z_slot(u, i, 0)
+
+    def s1_copy(u, b):
+        k, r = UNITS[u][0], rows_of(u)
         yy, xx = yx(1 - a_me, b)
-        return remote(G.at[k, :, yy, xx], r1_of(k, b), s1s.at[k * 2 + b], s1r.at[k * 2 + b], nb_a)
-
-    def s2_copy(k):
+        return remote(G.at[k, :, yy, xx, r], r1_of(k, b).at[:, r], s1s.at[u * 2 + b], s1r.at[u * 2 + b], nb_a)
+
+    def s2_copy(u):
+        if u in SUM_VIA_Z:
+            return remote(g_at(u, z, a_me, 1 - b_me), z_slot(u, z, 1), s2s.at[u], s2r.at[u], nb_b)
+        k, r = UNITS[u][0], rows_of(u)
         yy, xx = yx(a_me, 1 - b_me)
-        return remote(G.at[k, :, yy, xx], r2_of(k), s2s.at[k], s2r.at[k], nb_b)
-
-    def s2_single(k):
-        yy, xx = yx(a_me, 1 - b_me)
-        return remote(G.at[k, z, yy, xx], r2_of(k).at[z], s2s.at[k], s2r.at[k], nb_b)
-
-    def s3_copy(k, dz, far=0):
+        return remote(G.at[k, :, yy, xx, r], r2_of(k).at[:, r], s2s.at[u], s2r.at[u], nb_b)
+
+    def line(zz):
+        return dev(c, chip_of(zz, y, x))
+
+    def sz_copy(u, dz, far):
         zt = (z + dz) % 4
-        yy, xx = yx(a_me, 1 - b_me if far else b_me)
-        dst = (r2_of(k) if far else r3_of(k)).at[z]
-        i = k * 8 + far * 4
-        return remote(G.at[k, zt, yy, xx], dst, s3s.at[i + dz], s3r.at[i + z], dev(c, chip_of(zt, y, x)))
-
-    def s3_wait(k, dz, far=0):
+        i = u * 8 + far * 4
+        return remote(g_at(u, zt, a_me, b_of(far)), z_slot(u, z, far), szs.at[i + dz], szr.at[i + z], line(zt))
+
+    def sz_wait(u, dz, far):
         frm = (z + dz) % 4
-        dst = (r2_of(k) if far else r3_of(k)).at[frm]
-        i = k * 8 + far * 4
-        remote(G.at[k, frm, y, x], dst, s3s.at[i + dz], s3r.at[i + frm], dev(c, chip_of(frm, y, x))).wait_recv()
-
-    def s1(k):
+        i = u * 8 + far * 4
+        remote(g_at(u, frm, a_me, b_of(far)), z_slot(u, frm, far), szs.at[i + dz], szr.at[i + frm], line(frm)).wait_recv()
+
+    near_end = jnp.where(z < 2, 1, 2)
+
+    def pass_copy(u, far):
+        i = u * 2 + far
+        return remote(g_at(u, 3 - z, a_me, b_of(far)), pass_slot(u, near_end, far), pss.at[i], psr.at[i], line(near_end))
+
+    def sum_a(u, zz, far):
+        k, r = UNITS[u][0], rows_of(u)
+        b = b_of(far)
+        yy, xx = yx(a_me, b)
+        return G[k, zz, yy, xx, r].astype(F32) + r1_of(k, b)[zz, r].astype(F32)
+
+    def store(u, zz, far, value):
+        g_at(u, zz, a_me, b_of(far))[...] = value.astype(BF)
+
+    def sz_start(u, far):
+        for dz in (1, 3):
+            alone = z != (3 if dz == 1 else 0)
+            if u >= SMALL:
+                sz_copy(u, dz, far).start()
+            else:
+                pl.when(alone)(lambda: sz_copy(u, dz, far).start())
+                pl.when(jnp.logical_not(alone))(lambda: pass_copy(u, far).start())
+        if u >= SMALL:
+            sz_copy(u, 2, far).start()
+        else:
+            pl.when(jnp.logical_not(inner))(lambda: sz_copy(u, 2, far).start())
+
+    def sz_pass(u, far):
+        @pl.when(inner)
+        def _():
+            i = u * 2 + far
+            slot = pass_slot(u, z, far)
+            remote(g_at(u, z, a_me, b_of(far)), slot, pss.at[i], psr.at[i], line(z)).wait_recv()
+            zt = (z + 2) % 4
+            store(u, zt, far, g_at(u, zt, a_me, b_of(far))[...].astype(F32) + slot[...].astype(F32))
+            sz_copy(u, 2, far).start()
+
+    def sz_sum(u, far):
+        into = FIN.at[UNITS[u][0], rows_of(u)]
+
+        def add(dz):
+            sz_wait(u, dz, far)
+            into[...] += z_slot(u, (z + dz) % 4, far)[...].astype(F32)
+
+        for dz in (1, 3, 2):
+            if u >= SMALL or dz == 2:
+                add(dz)
+            else:
+                pl.when(z != (3 if dz == 1 else 0))(lambda: add(dz))
+
+    def s1(u):
         for b in range(2):
-            s1_copy(k, b).start()
-
-    def sum_a(k, zz, far):
-        b = 1 - b_me if far else b_me
-        yy, xx = yx(a_me, b)
-        return G[k, zz, yy, xx].astype(F32) + r1_of(k, b)[zz].astype(F32)
-
-    def store(k, zz, far, value):
-        yy, xx = yx(a_me, 1 - b_me if far else b_me)
-        G[k, zz, yy, xx] = value.astype(BF)
-
-    def s2(k):
+            s1_copy(u, b).start()
+
+    def stage_1(u):
         for b in range(2):
-            s1_copy(k, b).wait_recv()
-        if k in VIA_Z:
-            for dz in range(1, 4):
-                for far in range(2):
-                    store(k, (z + dz) % 4, far, sum_a(k, (z + dz) % 4, far))
-                    s3_copy(k, dz, far).start()
+            s1_copy(u, b).wait_recv()
+        if u in SUM_VIA_Z:
+            for far in (1, 0):
+                for dz in (1, 3, 2):
+                    store(u, (z + dz) % 4, far, sum_a(u, (z + dz) % 4, far))
+                sz_start(u, far)
         else:
             @pl.loop(0, 4)
             def _(zz):
-                store(k, zz, 1, sum_a(k, zz, 1))
-
-            s2_copy(k).start()
-
-    def s3(k):
-        if k in VIA_Z:
+                store(u, zz, 1, sum_a(u, zz, 1))
+
+            s2_copy(u).start()
+
+    def stage_2(u):
+        if u in SUM_VIA_Z:
             for far in (1, 0):
-                total = sum_a(k, z, far)
-                for dz in range(1, 4):
-                    s3_wait(k, dz, far)
-                    total += (r2_of(k) if far else r3_of(k))[(z + dz) % 4].astype(F32)
-                if far:
-                    store(k, z, 1, total)
-                    s2_single(k).start()
+                sz_pass(u, far)
+        else:
+            k, r = UNITS[u][0], rows_of(u)
+            s2_copy(u).wait_recv()
+            for dz in (1, 3, 2):
+                zt = (z + dz) % 4
+                store(u, zt, 0, sum_a(u, zt, 0) + r2_of(k)[zt, r].astype(F32))
+            sz_start(u, 0)
+            FIN[k, r] = sum_a(u, z, 0) + r2_of(k)[z, r].astype(F32)
+
+    def stage_3(u):
+        k, r = UNITS[u][0], rows_of(u)
+        if u in SUM_VIA_Z:
+            FIN[k, r] = sum_a(u, z, 1)
+            sz_sum(u, 1)
+            store(u, z, 1, FIN[k, r])
+            s2_copy(u).start()
+            FIN[k, r] = sum_a(u, z, 0)
+            sz_sum(u, 0)
+        elif u < SMALL:
+            sz_pass(u, 0)
+
+    def stage_4(u):
+        k, r = UNITS[u][0], rows_of(u)
+        if u in SUM_VIA_Z:
+            s2_copy(u).wait_recv()
+            FIN[k, r] += z_slot(u, z, 1)[...].astype(F32)
+        else:
+            sz_sum(u, 0)
+        total = FIN[k, r]
+        SQ[...] += fold(total * total)
+
+    def sums_done(u):
+        for b in range(2):
+            s1_copy(u, b).wait_send()
+        s2_copy(u).wait_send()
+        for far in range(2 if u in SUM_VIA_Z else 1):
+            sz_copy(u, 2, far).wait_send()
+            for dz in (1, 3):
+                if u >= SMALL:
+                    sz_copy(u, dz, far).wait_send()
                 else:
-                    FIN[k] = total
-        else:
-            s2_copy(k).wait_recv()
-            for dz in range(1, 4):
-                zt = (z + dz) % 4
-                store(k, zt, 0, sum_a(k, zt, 0) + r2_of(k)[zt].astype(F32))
-                s3_copy(k, dz).start()
-            FIN[k] = sum_a(k, z, 0) + r2_of(k)[z].astype(F32)
-
-    def s4(k):
-        total = FIN[k]
-        if k in VIA_Z:
-            s2_single(k).wait_recv()
-            total += r2_of(k)[z].astype(F32)
-        else:
-            for dz in range(1, 4):
-                s3_wait(k, dz)
-                total += r3_of(k)[(z + dz) % 4].astype(F32)
-        FIN[k] = total
-        SQ[...] += fold(total * total)
-
-    def sums_done(k):
-        for b in range(2):
-            s1_copy(k, b).wait_send()
-        (s2_single if k in VIA_Z else s2_copy)(k).wait_send()
-        for dz in range(1, 4):
-            s3_copy(k, dz).wait_send()
-            if k in VIA_Z:
-                s3_copy(k, dz, 1).wait_send()
+                    alone = z != (3 if dz == 1 else 0)
+                    pl.when(alone)(lambda: sz_copy(u, dz, far).wait_send())
+                    pl.when(jnp.logical_not(alone))(lambda: pass_copy(u, far).wait_send())
 
     def result_copies(i):
         if i < 4:
@@ -953,12 +1065,13 @@
             src = FIN.at[4 + j // 8 + 2 * (j % 2), :, pl.ds(((j % 8) // 2) * 128, 128)]
             dst = g_in.at[:, pl.ds(pl.multiple_of(10240 + 256 * j + c * 128, 128), 128)]
         else:
-            j = i - 20
-            src = FIN.at[j]
-            dst = g_in.at[:, pl.ds(pl.multiple_of(6144 + 1024 * j + c * 512, 512), 512)]
+            k, r0, size = ((3, 0, 64), *UNITS[9:])[i - 20]
+            src = FIN.at[k, pl.ds(r0, size)]
+            dst = g_in.at[pl.ds(r0, size), pl.ds(pl.multiple_of(6144 + 1024 * k + c * 512, 512), 512)]
         return pltpu.make_async_copy(src, dst, f_l.at[i]), remote(src, dst, f_s.at[i], f_r.at[i], twin)
 
-    def send_result(k):
+    def send_result(u):
+        k = UNITS[u][0]
         if k >= 8:
             span = (k - 8,)
         elif k == 7:
@@ -972,26 +1085,25 @@
         elif k >= 4:
             span = ()
         else:
-            span = (20 + k,)
+            span = (20 + u - 8,)
         for i in span:
             for copy in result_copies(i):
                 copy.start()
 
     def step(t):
-        if t + LEAD < CHUNKS:
-            if t + LEAD == 4:
-                pl.semaphore_wait(cred_a, 1)
-            s1(ORDER[t + LEAD])
+        for u in range(t + LEAD, NU):
+            if u == t + LEAD and u <= 11 or t + LEAD == 11:
+                if u == 4:
+                    pl.semaphore_wait(cred_a, 1)
+                s1(u)
         if t == 4:
             pl.semaphore_wait(cred_b, 1)
             pl.semaphore_wait(cred_z, 3)
-        if t < CHUNKS:
-            s2(ORDER[t])
-        if 0 <= t - LAG3 < CHUNKS:
-            s3(ORDER[t - LAG3])
-        if 0 <= t - LAG4 < CHUNKS:
-            s4(ORDER[t - LAG4])
-            send_result(ORDER[t - LAG4])
+        for stage, lag in zip((stage_1, stage_2, stage_3, stage_4), LAGS):
+            if 0 <= t - lag < NU:
+                stage(t - lag)
+                if stage is stage_4:
+                    send_result(t - lag)
 
     def grad_tiles(k, left, right):
         @pl.loop(0, 4)
@@ -1009,7 +1121,7 @@
                 DMO[:, :, ch * 512 : ch * 512 + 512].reshape(512, 512),
             )
             if 2 * ch + rh < LEAD:
-                s1(k)
+                s1(2 * ch + rh)
 
     for k in range(CHUNKS):
         sends_done(k)
@@ -1059,9 +1171,9 @@
         )
     received(7)
 
-    @pl.loop(0, TOK // 32)
+    @pl.loop(0, TOK // TILE)
     def _(i):
-        r = rows_at(i, 32)
+        r = rows_at(i, TILE)
         d_in = both_parts(r)
         hat, inv = normed(RSD[r, :])
         DACC[3] += fold(d_in)
@@ -1129,9 +1241,9 @@
         )
     received(11)
 
-    @pl.loop(0, TOK // 32)
+    @pl.loop(0, TOK // TILE)
     def _(i):
-        r = rows_at(i, 32)
+        r = rows_at(i, TILE)
         d_in = both_parts(r)
         hat, inv = normed(X0[r, :])
         DACC[0] += fold(d_in)
@@ -1144,11 +1256,14 @@
     d_mods = MODS[...]
     DMB[c, s] = jnp.concatenate([d_mods[:, :512], d_mods[:, 512:]], axis=0).astype(BF)
     peers_send(3, lambda p: DMB.at[c, s], DMB.at[c])
-    for q in range(8):
-        B3S[q] = GLP[:, q * 128 : q * 128 + 128]
-    B3R[s] = B3S[s // 2]
-    peers_send(4, lambda p: B3S.at[p // 2], B3R)
+    for q in range(16):
+        cols = slice(q * 64, q * 64 + 64)
+        B3S[q] = jnp.concatenate([GLP[0:16, cols], GLP[16:32, cols]], axis=1).astype(BF)
+    B3R[s] = B3S[s]
+    peers_send(4, lambda p: B3S.at[p], B3R)
     step(4)
+    step(5)
+    step(6)
     peers_wait(3, lambda p: DMB.at[c, s], DMB.at[c])
     twin_copy(13, DMB.at[c], DMB.at[c]).start()
 
@@ -1167,24 +1282,27 @@
     d_cond = d_cond_low * silu_slope(CND[1])
     CP[c, 2, :, 0:64] = d_cond
     d_temb = d_cond.astype(BF).astype(F32)
-    B2S[...] = jnp.concatenate([d_temb, d_temb], axis=1)
+    B2S[...] = to_tile(d_temb)
     B2R[s] = B2S[...]
     peers_send(5, lambda p: B2S, B2R)
-    step(5)
-    peers_wait(4, lambda p: B3S.at[p // 2], B3R)
-    B3D[c] = jnp.sum(B3R[...], axis=0)
+    step(7)
+    peers_wait(4, lambda p: B3S.at[p], B3R)
+    sums = B3R[0].astype(F32)
+    for i in range(1, 16):
+        sums += B3R[i].astype(F32)
+    B3D[c] = sums
     twin_copy(14, B3D.at[c], B3D.at[c]).start()
     peers_wait(5, lambda p: B2S, B2R)
     for q in range(8):
         DTA[c, :, q * 128 : q * 128 + 128] = jnp.concatenate(
-            [B2R[2 * q, :, 0:64], B2R[2 * q + 1, :, 0:64]], axis=1
+            [from_tile(B2R[2 * q]), from_tile(B2R[2 * q + 1])], axis=1
         )
     d_tact = dot_nt(DTA[c].astype(BF), EX[:, 0:1024].astype(BF))
     CP[c, 3, :, 0:64] = (d_tact * silu_slope(CND[0])).astype(BF).astype(F32)
     twin_copy(15, DTA.at[c], DTA.at[c]).start()
     twin_copy(16, CP.at[c], CP.at[c]).start()
     twin_copy(17, E1.at[c], E1.at[c]).start()
-    step(6)
+    step(8)
     twin_copy(13, DMB.at[o], DMB.at[o]).wait_recv()
     unpack(o)
     twin_copy(14, B3D.at[o], B3D.at[o]).wait_recv()
@@ -1210,17 +1328,16 @@
             EX[:, (k - 5) * 1024 : (k - 4) * 1024] = grad
     mod_out = pltpu.make_async_copy(WMOD, g_in.at[:, pl.ds(0, 6144)], st_sem.at[26])
     mod_out.start()
-    step(7)
+    step(9)
     grad = dot_tn(packed(1).astype(BF), jnp.concatenate([DTA[0], DTA[1]], axis=0).astype(BF))
     small += square_half(grad)
     EX[:, 0:1024] = grad
     sums = B3D[0] + B3D[1]
-    sums = jnp.where(x == 0, sums[:, 0:64], sums[:, 64:128])
-    small += square_half(sums[16:32])
+    small += square_half(sums[:, 64:128])
     wide = jnp.concatenate(
-        [jnp.concatenate([sums[16:32], jnp.zeros((16, 64), F32)], axis=1), jnp.zeros((112, 128), F32)], axis=0
-    )
-    EX[:, 3072:3088] = wide.T[0:64, 0:16]
+        [sums, jnp.zeros((112, 128), F32)], axis=0
+    )
+    EX[:, 3072:3088] = wide.T[64:128, 0:16]
     def both(value):
         return jnp.concatenate([value(0), value(1)], axis=0)
 
@@ -1228,13 +1345,13 @@
     hot = (both(lambda g: E1[g, :, 2, 0:1]).astype(jnp.int32) + PDIM == index).astype(F32)
     grad = dot_tn_exact(packed(2), hot)
     spot = lax.broadcasted_iota(jnp.int32, (16, ENTRIES), 0) == index[0:16]
-    grad += dot_tn_exact(sums[0:16], spot.astype(F32))
+    grad += dot_tn_exact(sums[:, 0:64], spot.astype(F32))
     ENT[...] = grad
     femb = both(lambda g: jnp.concatenate([E1[g, :, 0, :], E1[g, :, 1, :]], axis=1)).astype(BF)
     ENT[:, PDIM + NCLS :] = dot_tn(packed(3).astype(BF), femb)
     small += square_half(ENT[...])
 
-    for t in range(8, CHUNKS + LAG4):
+    for t in range(10, NU + LAGS[3]):
         step(t)
 
     def total_of(value):
@@ -1243,20 +1360,31 @@
     NSS[0:1, :] = jnp.broadcast_to(total_of(SQ[...]) + small, (1, 128))
     NSS[1:2, :] = jnp.broadcast_to(total_of(LOSS[...]) / (TOK * PDIM), (1, 128))
     NSS[2:8, :] = jnp.zeros((6, 128), F32)
-    NSR[s] = NSS[...]
-    peers_send(6, lambda p: NSS, NSR)
-    peers_wait(6, lambda p: NSS, NSR)
-    NSD[c] = jnp.sum(NSR[...], axis=0)
-    twin_copy(18, NSD.at[c], NSD.at[c]).start()
-    twin_copy(18, NSD.at[o], NSD.at[o]).wait_recv()
-    stats[...] = NSD[0] + NSD[1]
+    NSR[c * 16 + s] = NSS[...]
+
+    def far_copy(k, frm):
+        return remote(NSS, NSR.at[frm], far_s.at[k], far_r.at[frm % 16], dev(o, k))
+
+    @pl.loop(0, 16)
+    def _(k):
+        far_copy(k, c * 16 + s).start()
+
+    mine = NSR.at[pl.ds(c * 16, 16)]
+    peers_send(6, lambda p: NSS, mine)
+    peers_wait(6, lambda p: NSS, mine)
+
+    @pl.loop(0, 16)
+    def _(k):
+        far_copy(k, o * 16 + k).wait()
+
+    stats[...] = jnp.sum(NSR[...], axis=0)
 
     mod_out.wait()
-    for i in range(24):
+    for i in range(27):
         for copy in result_copies(i):
             copy.wait()
-    for k in range(CHUNKS):
-        sums_done(k)
+    for u in range(NU):
+        sums_done(u)
     twin_copy(0, ATI.at[c], ATI.at[c]).wait_send()
     twin_copy(1, MIX.at[c], MIX.at[c]).wait_send()
     twin_copy(2, W.at[3], WP).wait_send()
@@ -1271,29 +1399,29 @@
     twin_copy(15, DTA.at[c], DTA.at[c]).wait_send()
     twin_copy(16, CP.at[c], CP.at[c]).wait_send()
     twin_copy(17, E1.at[c], E1.at[c]).wait_send()
-    twin_copy(18, NSD.at[c], NSD.at[c]).wait_send()
-
-
-def fused_step(msg, pt, pos, block_in, block_out, entry, exit_):
+
+
+def fused_step(msg, edge, pt, pos, block_in, block_out, entry, exit_):
     vm = pltpu.VMEM
     dma = pltpu.SemaphoreType.DMA
     scratch = [
         vm((12, 4, 2, 2, 64, 512), BF), vm((4, 2, 2, 64, 512), BF), vm((12, 4, 2, 2, 64, 512), BF),
-        vm((4, 2, 4, 64, 512), BF), vm((4, 4, 64, 512), BF), vm((4, 4, 64, 512), BF), vm((12, 64, 512), F32),
+        vm((4, 2, 4, 64, 512), BF), vm((4, 4, 64, 512), BF), vm((4, 4, 64, 512), BF),
+        vm((len(SUM_VIA_Z), 64, 512), BF), vm((12, 64, 512), F32),
         vm((2, TOK, 1024), BF), vm((3, 2, TOK, 512), BF), vm((2, 2, TOK, 512), BF), vm((2, TOK, 1024), BF),
         vm((2, TOK, 2048), BF), vm((2, TOK, 2048), BF), vm((2, TOK, 1024), BF), vm((2, TOK, 1024), BF),
         vm((2, TOK, 512), BF), vm((TOK, 512), BF),
         *[vm((TOK, 1024), F32)] * 5, vm((2, TOK, 512), F32), vm((2, TOK, 512), F32),
-        vm((64, 6144), F32), vm((2, 16, 8, 128), F32), vm((16, 16, 128), F32), vm((8, 16, 128), F32), vm((16, 16, 128), F32),
+        vm((64, 6144), F32), vm((2, 16, 8, 128), F32), vm((16, 16, 128), BF), vm((16, 8, 128), F32), vm((16, 8, 128), F32),
         vm((16, 16, 512), BF), vm((16, 16, 512), BF), vm((2, 16, 16, 512), BF), vm((2, 8, 16, 1024), F32),
-        vm((16, 128), F32), vm((16, 16, 128), F32), vm((2, 16, 1024), F32), vm((2, 4, 16, 128), F32), vm((2, 16, 64), F32),
-        vm((8, 32, 128), F32), vm((16, 32, 128), F32), vm((2, 32, 128), F32),
-        vm((8, 128), F32), vm((16, 8, 128), F32), vm((2, 8, 128), F32),
-        vm((8, 1024), F32), vm((8, 8, 1024), F32), vm((16, 1024), F32), vm((16, 1024), F32), vm((32, 1024), F32),
+        vm((8, 128), F32), vm((16, 8, 128), F32), vm((2, 16, 1024), F32), vm((2, 4, 16, 128), F32), vm((2, 16, 64), F32),
+        vm((16, 16, 128), BF), vm((16, 16, 128), BF), vm((2, 16, 128), F32),
+        vm((8, 128), F32), vm((32, 8, 128), F32),
+        vm((8, 1024), F32), vm((8, 8, 1024), F32), vm((16, 1024), BF), vm((16, 1024), BF), vm((32, 1024), F32),
         vm((8, 512), F32), vm((8, 16), F32),
         dma((27,)), dma((8, 16)), dma((8, 16)), dma((96,)), dma((96,)), dma((48,)), dma((48,)), dma((96,)), dma((96,)),
-        dma((24,)), dma((24,)), dma((12,)), dma((12,)), dma((96,)), dma((96,)), dma((19,)), dma((19,)),
-        dma((24,)), dma((24,)), dma((24,)),
+        dma((30,)), dma((30,)), dma((15,)), dma((15,)), dma((120,)), dma((120,)), dma((30,)), dma((30,)), dma((19,)), dma((19,)),
+        dma((27,)), dma((27,)), dma((27,)), dma((16,)), dma((16,)),
         pltpu.SemaphoreType.REGULAR, pltpu.SemaphoreType.REGULAR, pltpu.SemaphoreType.REGULAR,
     ]
     any_ = pl.BlockSpec(memory_space=pl.ANY)
@@ -1305,14 +1433,14 @@
             shape(block_in.shape, F32), shape(block_out.shape, F32), shape(entry.shape, F32),
             shape(exit_.shape, F32), shape((8, 128), F32),
         ),
-        in_specs=[vmem, vmem, vmem, any_, any_, any_, any_],
+        in_specs=[vmem, vmem, vmem, vmem, any_, any_, any_, any_],
         out_specs=(any_, any_, vmem, vmem, vmem),
         scratch_shapes=scratch,
         compiler_params=pltpu.CompilerParams(
             collective_id=0, has_side_effects=True, vmem_limit_bytes=62 * 2**20
         ),
         cost_estimate=pl.CostEstimate(flops=21 * 10**9, bytes_accessed=20 * 10**6, transcendentals=4 * 10**6),
-    )(msg, pt, pos, block_in, block_out, entry, exit_)
+    )(msg, edge, pt, pos, block_in, block_out, entry, exit_)
 
 
 def local_fused(
@@ -1330,12 +1458,11 @@
         [femb, jnp.full((1, LANES), label), jnp.where(lane == index, label, 0.0), jnp.zeros((4, LANES), F32)], axis=0
     )
     edge = jnp.concatenate([entry_table[:PDIM], exit_proj[:, 3 * D :].T], axis=1)
-    msg = jnp.concatenate([head, edge], axis=0)
     pt = patchify(jnp.concatenate([noisy, noise], axis=0), PATCH)
     grid = noisy.shape[-1] // PATCH
     pos = position_table(grid, D)[:grid, : D // 2]
     g_in, g_out, g_entry, g_exit, stats = fused_step(
-        msg, pt, pos, block_in[0], block_out[0], entry_table.T, exit_proj
+        head, lowered(edge), pt, pos, block_in[0], block_out[0], entry_table.T, exit_proj
     )
     loss = stats[1, 0]
     grad_norm = jnp.sqrt(stats[0, 0])

time: 304 us -> 284 us (0.934)
  Pallas kernels: 274 us -> 254 us
    pallas_call x1, Pallas kernels: 274 us -> 254 us  [fused_step(): pl.pallas_call(step_kernel, out_shape=(shape(block_in.shape, F32), shape(...]
where the time goes in v3:
time: 284 us
  Pallas kernels  254 us (89%)
  other arithmetic  19.6 us (7%)
  local copies, waits for them, and re-layouts  6.12 us (2%)
  between operations  4.02 us (1%)
    pallas_call x1, Pallas kernels, fused_step(): pl.pallas_call(step_kernel, out_shape=(shape(block_in.shape, F32), shape(...  254 us
    convert_element_type x4, other arithmetic, adam_step(): return (weight_new, first_new, second_new, weight_new.astype(jnp.bfloat16))  15.7 us

profile of v3, /device:TPU:0, one launch (start us, length us, event | category | flops | bytes accessed | tf_op | source)
XLA Modules:
  0.0 284.0 jit_solution(218351677467011608)
XLA Ops:
  2.0 0.1 sine_convert_fusion
  2.1 0.1 pad.9.clone
  2.1 0.7 maximum_maximum_fusion.msg
  2.8 1.0 multiply_sine_fusion
  3.8 0.6 pad_maximum_fusion.1.pos
  4.4 0.9 pad_maximum_fusion
  5.3 0.5 copy.44
  5.8 1.1 copy.45
  6.8 0.1 reshape.111
  7.0 0.8 copy.46.pt
  7.8 0.8 slice.26
  8.6 0.1 copy.48
  8.7 0.8 slice.27
  9.4 0.1 copy.47
  9.5 0.7 pad_maximum_fusion.2.edge
  10.2 254.3 %shard_map.295 = (f32[64,14336]{1,0:T(8,128)}, f32[256,1024]{1,0:T(8,128)}, f32[64,1272]{1,0:T(8,128)}, f32[64,3088]{1,0:T(8,128)}, f32[8,128]{1,0:T(8,128)}) custom-call(f32[8,128]{1,0:T(8,128)} %maximum_maximum_fusion.msg, bf16[16,128]{1,0:T(8,128)(2,1)} %pad_maximum_fusion.2.edge, f32[2,256,16]{2,1,0:T(8,128)} %copy.46.pt, ...), custom_call_target="tpu_custom_call" | custom-call | flops 20999999488 | bytes 20000000 | tf_op jit(solution)/shard_map/pallas_call | solution.py:1430
  264.5 1.3 fusion.19
  266.5 0.0 copy-start.2
  266.5 10.0 %fusion.16 = (bf16[1,64,14336]{2,1,0:T(8,128)(2,1)}, f32[1,64,14336]{2,1,0:T(8,128)}, f32[1,64,14336]{2,1,0:T(8,128)}, f32[1,64,14336]{2,1,0:T(8,128)}) fusion(f32[1,64,14336]{2,1,0:T(8,128)} %param.20, f32[64,14336]{1,0:T(8,128)} %get-tuple-element.24, f32[]{:T(128)S(6)} %div.61, f32[1,64,14336]{2,1,0:T(8,128)} %param.21, f32[1,64,14336]{2,1,0:T(8,128)} %param.22), kind=kLoop, calls=%fused_computation.39 | loop fusion | flops 14680064 | bytes 27525124 | tf_op jit(solution)/shard_map/convert_element_type | solution.py:90
  276.5 0.0 copy-start.4
  276.6 2.5 fusion.13
  279.1 0.5 copy-done.7
  279.6 2.0 fusion.9
  281.7 1.2 fusion.11
  (27 shorter events, 0.1 us)
Async XLA Ops:
  266.5 10.0 %copy-start = (f32[1,256,1024]{2,1,0:T(8,128)S(1)}, f32[1,256,1024]{2,1,0:T(8,128)}, u32[]{:S(2)}) copy-start(f32[1,256,1024]{2,1,0:T(8,128)} %param.23) | copy-start | bytes 3145732
  266.5 10.0 %copy-start.1 = (f32[1,256,1024]{2,1,0:T(8,128)S(1)}, f32[1,256,1024]{2,1,0:T(8,128)}, u32[]{:S(2)}) copy-start(f32[1,256,1024]{2,1,0:T(8,128)} %param.24) | copy-start | bytes 3145732
  266.5 10.0 %copy-start.2 = (f32[1,256,1024]{2,1,0:T(8,128)S(1)}, f32[1,256,1024]{2,1,0:T(8,128)}, u32[]{:S(2)}) copy-start(f32[1,256,1024]{2,1,0:T(8,128)} %param.25) | copy-start | bytes 3145732
  266.5 10.0 %copy-start.3 = (f32[256,1024]{1,0:T(8,128)S(1)}, f32[256,1024]{1,0:T(8,128)}, u32[]{:S(2)}) copy-start(f32[256,1024]{1,0:T(8,128)} %get-tuple-element.25) | copy-start | bytes 3145732
  276.5 2.5 copy-start.4
  276.6 2.5 copy-start.5
  276.6 2.5 copy-start.6
  276.6 3.0 %copy-start.7 = (f32[64,3088]{1,0:T(8,128)S(1)}, f32[64,3088]{1,0:T(8,128)}, u32[]{:S(2)}) copy-start(f32[64,3088]{1,0:T(8,128)} %get-tuple-element.27) | copy-start | bytes 2371588
  279.1 2.6 copy-start.8
  279.1 2.6 copy-start.9
  279.1 2.6 copy-start.10
  279.1 2.6 copy-start.11

commit v4 on v3

--- a/solution.py
+++ b/solution.py
@@ -1,5 +1,6 @@
 import jax
 import jax.numpy as jnp
+import numpy as np
 from jax import lax
 from jax.experimental import pallas as pl
 from jax.experimental.pallas import tpu as pltpu
@@ -375,9 +376,9 @@
 OWN_AT = ((), (4,), (5, 6), (7, 8), (9, 10), (11,))
 Z_AT = ((2,), (3,), (4,), (5,), (6, 7), (8,), (9,), (10,), (11,))
 VIA_Z = (1, 3, 5, 7, 9, 11)
-SUM_VIA_Z = (0, 3, 6)
+SUM_VIA_Z = (0, 2, 4, 6, 8)
 LEAD = 3
-LAGS = (0, 1, 2, 3)
+LAGS = (0, 2, 3, 4)
 LAG_A = 1
 UNITS = tuple((k, 0, 64) for k in (8, 9, 10, 11, 4, 5, 6, 7, 3, 0, 1)) + tuple((2, 16 * i, 16) for i in range(4))
 NU = len(UNITS)
@@ -400,6 +401,30 @@
     return lax.dot_general(
         left, right, (((0,), (0,)), ((), ())), preferred_element_type=F32, precision=highest
     )
+
+
+def patches_of(image):
+    how = highest if image.dtype == F32 else None
+
+    def product_of(left, right, dims):
+        return lax.dot_general(
+            left.astype(image.dtype), right.astype(image.dtype), (dims, ((), ())),
+            preferred_element_type=F32, precision=how,
+        )
+
+    def iota(shape, dim):
+        return lax.broadcasted_iota(jnp.int32, shape, dim)
+
+    total = 0.0
+    mine = iota((TOK, 128), 0) >> 4 == (iota((TOK, 128), 1) & 31) >> 1
+    for pc in range(2):
+        pick = (2 * iota((16, 32), 0) + pc == iota((16, 32), 1)).astype(F32)
+        cols = product_of(pick, image, ((1,), (1,)))
+        spread = jnp.where(mine, jnp.concatenate([cols] * 16, axis=0), 0.0)
+        row = iota((128, PDIM), 0)
+        place = (row & 1) * 8 + pc * 4 + (row >> 5) == iota((128, PDIM), 1)
+        total += product_of(spread, place.astype(F32), ((1,), (0,)))
+    return total
 
 
 def to_tile(value):
@@ -442,12 +467,12 @@
 
 
 def step_kernel(
-    msg, edge, pt, pos, bi, bo, ent_in, ex_in,
+    msg, noisy, noise, pos, bi, bo, ent_in, ex_in,
     g_in, g_out, ENT, EX, stats,
     W, WP, G, R1, R2, R3, PF, FIN,
     ATI, QKV, MIX, MLI, ACT, GD, DMO, DAO, DMX, DMS,
     X0, AO, RSD, MO, X1, SND, RCV,
-    WMOD, E1, EDG, E2S, E2R, E3S, E3R, DMB, DMF, B2S, B2R, DTA, CP, CND,
+    WMOD, PAT, TGT, EDS, E1, EDG, E2S, E2R, E3S, E3R, DMB, DMF, B2S, B2R, DTA, CP, CND,
     B3S, B3R, B3D, NSS, NSR, MODS, DACC, WPT, WLT, GLP, SQ, LOSS,
     st_sem, peer_s, peer_r, zs, zr, bs, br, as_, ar,
     s1s, s1r, s2s, s2r, szs, szr, pss, psr, d_s, d_r, f_l, f_s, f_r,
@@ -704,18 +729,25 @@
 
     E3R[s] = E3S[s]
     peers_send(2, lambda p: E3S.at[p], E3R)
-    EDG[s] = edge[...]
-    peers_send(7, lambda p: edge, EDG)
+    edges = jnp.concatenate(
+        [ENT[:, 0:128], jnp.concatenate([EX[:, 3072:3088], jnp.zeros((64, 112), F32)], axis=1)], axis=0
+    )
+    edges = edges.T[0:16].astype(BF)
+    EDS[...] = edges
+    EDG[s] = edges
+    peers_send(7, lambda p: EDS, EDG)
     pump(2)
 
-    peers_wait(7, lambda p: edge, EDG)
+    PAT[...] = patches_of(noisy[...].astype(BF)).astype(BF)
+    TGT[...] = patches_of(noise[...])
+    peers_wait(7, lambda p: EDS, EDG)
     for q in range(8):
         even, odd = EDG[2 * q], EDG[2 * q + 1]
         WPT[:, q * 128 : q * 128 + 128] = jnp.concatenate([even[:, :64], odd[:, :64]], axis=1)
         WLT[:, q * 128 : q * 128 + 128] = jnp.concatenate([even[:, 64:], odd[:, 64:]], axis=1)
     for n in range(4):
         cols = slice(n * 256, n * 256 + 256)
-        X0[:, cols] = dot_nn(pt[0].astype(BF), WPT[:, cols])
+        X0[:, cols] = dot_nn(PAT[...], WPT[:, cols])
 
     @pl.loop(0, 16)
     def _(i):
@@ -870,7 +902,7 @@
         scale = 1.0 + mod_row(7)
         final_in = (hat * scale + mod_row(6)).astype(BF)
         w_lin = WLT[...]
-        error = dot_nt(final_in, w_lin) - pt[1, r, :]
+        error = dot_nt(final_in, w_lin) - TGT[r, :]
         LOSS[...] += fold(error * error)
         d_pred = (2.0 * error / (TOK * PDIM)).astype(BF)
         GLP[16:32, :] += dot_tn(d_pred, final_in)
@@ -1249,7 +1281,7 @@
         DACC[0] += fold(d_in)
         DACC[1] += fold(d_in * hat)
         d_x = normed_back(d_in * (1.0 + mod_row(1)), hat, inv) + X1[r, :]
-        GLP[0:16, :] += dot_tn(pt[0, r, :].astype(BF), d_x.astype(BF))
+        GLP[0:16, :] += dot_tn(PAT[r, :], d_x.astype(BF))
 
     for k in range(8):
         MODS[k : k + 1, :] = jnp.sum(DACC[k], axis=0, keepdims=True)
@@ -1377,7 +1409,11 @@
     def _(k):
         far_copy(k, o * 16 + k).wait()
 
-    stats[...] = jnp.sum(NSR[...], axis=0)
+    totals = jnp.sum(NSR[...], axis=0)
+    norm = jnp.sqrt(totals[0:1])
+    stats[...] = totals
+    stats[0:1, :] = norm
+    stats[2:3, :] = clip_limit / jnp.maximum(norm, clip_limit)
 
     mod_out.wait()
     for i in range(27):
@@ -1401,7 +1437,7 @@
     twin_copy(17, E1.at[c], E1.at[c]).wait_send()
 
 
-def fused_step(msg, edge, pt, pos, block_in, block_out, entry, exit_):
+def fused_step(msg, noisy, noise, pos, block_in, block_out, entry, exit_):
     vm = pltpu.VMEM
     dma = pltpu.SemaphoreType.DMA
     scratch = [
@@ -1412,7 +1448,7 @@
         vm((2, TOK, 2048), BF), vm((2, TOK, 2048), BF), vm((2, TOK, 1024), BF), vm((2, TOK, 1024), BF),
         vm((2, TOK, 512), BF), vm((TOK, 512), BF),
         *[vm((TOK, 1024), F32)] * 5, vm((2, TOK, 512), F32), vm((2, TOK, 512), F32),
-        vm((64, 6144), F32), vm((2, 16, 8, 128), F32), vm((16, 16, 128), BF), vm((16, 8, 128), F32), vm((16, 8, 128), F32),
+        vm((64, 6144), F32), vm((TOK, PDIM), BF), vm((TOK, PDIM), F32), vm((16, 128), BF), vm((2, 16, 8, 128), F32), vm((16, 16, 128), BF), vm((16, 8, 128), F32), vm((16, 8, 128), F32),
         vm((16, 16, 512), BF), vm((16, 16, 512), BF), vm((2, 16, 16, 512), BF), vm((2, 8, 16, 1024), F32),
         vm((8, 128), F32), vm((16, 8, 128), F32), vm((2, 16, 1024), F32), vm((2, 4, 16, 128), F32), vm((2, 16, 64), F32),
         vm((16, 16, 128), BF), vm((16, 16, 128), BF), vm((2, 16, 128), F32),
@@ -1440,7 +1476,7 @@
             collective_id=0, has_side_effects=True, vmem_limit_bytes=62 * 2**20
         ),
         cost_estimate=pl.CostEstimate(flops=21 * 10**9, bytes_accessed=20 * 10**6, transcendentals=4 * 10**6),
-    )(msg, edge, pt, pos, block_in, block_out, entry, exit_)
+    )(msg, noisy, noise, pos, block_in, block_out, entry, exit_)
 
 
 def local_fused(
@@ -1457,16 +1493,15 @@
     head = jnp.concatenate(
         [femb, jnp.full((1, LANES), label), jnp.where(lane == index, label, 0.0), jnp.zeros((4, LANES), F32)], axis=0
     )
-    edge = jnp.concatenate([entry_table[:PDIM], exit_proj[:, 3 * D :].T], axis=1)
-    pt = patchify(jnp.concatenate([noisy, noise], axis=0), PATCH)
-    grid = noisy.shape[-1] // PATCH
-    pos = position_table(grid, D)[:grid, : D // 2]
+    side = noisy.shape[-1]
+    grid, quarter = side // PATCH, D // 4
+    angle = np.arange(grid)[:, None] / 10000.0 ** (np.arange(quarter)[None, :] / quarter)
+    pos = jnp.asarray(np.concatenate([np.sin(angle), np.cos(angle)], axis=1), F32)
     g_in, g_out, g_entry, g_exit, stats = fused_step(
-        head, lowered(edge), pt, pos, block_in[0], block_out[0], entry_table.T, exit_proj
+        head, noisy.reshape(-1, side), noise.reshape(-1, side), pos, block_in[0], block_out[0], entry_table.T, exit_proj
     )
     loss = stats[1, 0]
-    grad_norm = jnp.sqrt(stats[0, 0])
-    factor = clip_limit / jnp.maximum(grad_norm, clip_limit)
+    grad_norm, factor = stats[0, 0], stats[2, 0]
     outs = [loss, grad_norm]
     for weight, first, second, grad, rate in (
         (block_in, block_in_first, block_in_second, g_in[None], rate_main),

time: 284 us -> 271 us (0.954)
  Pallas kernels: 254 us -> 248 us
  local copies, waits for them, and re-layouts: 6.12 us -> 1.45 us
    pallas_call x1, Pallas kernels: 254 us -> 248 us  [fused_step(): pl.pallas_call(step_kernel, out_shape=(shape(block_in.shape, F32), shape(...]
where the time goes in v4:
time: 271 us
  Pallas kernels  248 us (92%)
  other arithmetic  19.1 us (7%)
    pallas_call x1, Pallas kernels, fused_step(): pl.pallas_call(step_kernel, out_shape=(shape(block_in.shape, F32), shape(...  248 us
    convert_element_type x4, other arithmetic, adam_step(): return (weight_new, first_new, second_new, weight_new.astype(jnp.bfloat16))  18.4 us

profile of v4, /device:TPU:0, one launch (start us, length us, event | category | flops | bytes accessed | tf_op | source)
XLA Modules:
  0.0 270.8 jit_solution(11463936696034754019)
XLA Ops:
  2.0 0.1 sine_convert_fusion
  2.1 0.1 pad.3.clone
  2.1 0.7 maximum_maximum_fusion.msg
  2.8 248.1 %shard_map.304 = (f32[64,14336]{1,0:T(8,128)}, f32[256,1024]{1,0:T(8,128)}, f32[64,1272]{1,0:T(8,128)}, f32[64,3088]{1,0:T(8,128)}, f32[8,128]{1,0:T(8,128)}) custom-call(f32[8,128]{1,0:T(8,128)} %maximum_maximum_fusion.msg, f32[128,32]{1,0:T(8,128)} %bitcast.40, f32[128,32]{1,0:T(8,128)} %bitcast.41, f32[16,512]{1,0:T(8,128)} %constant.27.clone.pos, ...), custom_call_target="tpu_custom_call" | custom-call | flops 20999999488 | bytes 20000000 | tf_op jit(solution)/shard_map/pallas_call | solution.py:1466
  250.9 1.3 fusion.18
  252.2 10.9 %fusion.15 = (bf16[1,64,14336]{2,1,0:T(8,128)(2,1)}, f32[1,64,14336]{2,1,0:T(8,128)}, f32[1,64,14336]{2,1,0:T(8,128)}, f32[1,64,14336]{2,1,0:T(8,128)}) fusion(f32[1,64,14336]{2,1,0:T(8,128)} %param.21, f32[64,14336]{1,0:T(8,128)} %get-tuple-element.24, f32[]{:T(128)} %bitcast.10, f32[1,64,14336]{2,1,0:T(8,128)} %param.22, f32[1,64,14336]{2,1,0:T(8,128)} %param.23), kind=kLoop, calls=%fused_computation.29 | loop fusion | flops 14680064 | bytes 27525124 | tf_op jit(solution)/shard_map/convert_element_type | solution.py:91
  263.1 0.0 copy-done
  263.1 0.0 copy-done.1
  263.1 0.0 copy-done.2
  263.1 0.0 copy-done.3
  263.1 0.0 copy-start.4
  263.1 0.0 copy-start.5
  263.2 0.0 copy-start.6
  263.2 0.0 copy-start.7
  263.2 3.2 %fusion.12 = (bf16[1,256,1024]{2,1,0:T(8,128)(2,1)}, f32[1,256,1024]{2,1,0:T(8,128)}, f32[1,256,1024]{2,1,0:T(8,128)}, f32[1,256,1024]{2,1,0:T(8,128)}) fusion(f32[1,256,1024]{2,1,0:T(8,128)S(1)} %copy-done, f32[256,1024]{1,0:T(8,128)S(1)} %copy-done.3, f32[]{:T(128)} %bitcast.10, f32[1,256,1024]{2,1,0:T(8,128)S(1)} %copy-done.1, ...), kind=kLoop, calls=%fused_computation.28 | loop fusion | flops 4194304 | bytes 7864324 | tf_op jit(solution)/shard_map/convert_element_type | solution.py:91
  266.4 0.0 copy-done.4
  266.4 0.0 copy-done.5
  266.4 0.0 copy-done.6
  266.4 0.0 copy-done.7
  266.4 2.7 fusion.8
  269.1 0.0 copy-done.8
  269.1 0.0 copy-done.9
  269.1 0.0 copy-done.10
  269.1 1.7 fusion.10
  (13 shorter events, 0.0 us)
Async XLA Ops:
  252.2 10.9 %copy-start = (f32[1,256,1024]{2,1,0:T(8,128)S(1)}, f32[1,256,1024]{2,1,0:T(8,128)}, u32[]{:S(2)}) copy-start(f32[1,256,1024]{2,1,0:T(8,128)} %param.24) | copy-start | bytes 3145732
  252.2 10.9 %copy-start.1 = (f32[1,256,1024]{2,1,0:T(8,128)S(1)}, f32[1,256,1024]{2,1,0:T(8,128)}, u32[]{:S(2)}) copy-start(f32[1,256,1024]{2,1,0:T(8,128)} %param.25) | copy-start | bytes 3145732
  252.2 10.9 %copy-start.2 = (f32[1,256,1024]{2,1,0:T(8,128)S(1)}, f32[1,256,1024]{2,1,0:T(8,128)}, u32[]{:S(2)}) copy-start(f32[1,256,1024]{2,1,0:T(8,128)} %param.26) | copy-start | bytes 3145732
  252.2 10.9 %copy-start.3 = (f32[256,1024]{1,0:T(8,128)S(1)}, f32[256,1024]{1,0:T(8,128)}, u32[]{:S(2)}) copy-start(f32[256,1024]{1,0:T(8,128)} %get-tuple-element.25) | copy-start | bytes 3145732
  263.1 3.2 %copy-start.4 = (f32[64,3088]{1,0:T(8,128)S(1)}, f32[64,3088]{1,0:T(8,128)}, u32[]{:S(2)}) copy-start(f32[64,3088]{1,0:T(8,128)} %ex_in.1) | copy-start | bytes 2371588
  263.1 3.2 %copy-start.5 = (f32[64,3088]{1,0:T(8,128)S(1)}, f32[64,3088]{1,0:T(8,128)}, u32[]{:S(2)}) copy-start(f32[64,3088]{1,0:T(8,128)} %param.31) | copy-start | bytes 2371588
  263.2 3.2 %copy-start.6 = (f32[64,3088]{1,0:T(8,128)S(1)}, f32[64,3088]{1,0:T(8,128)}, u32[]{:S(2)}) copy-start(f32[64,3088]{1,0:T(8,128)} %param.32) | copy-start | bytes 2371588
  263.2 3.2 %copy-start.7 = (f32[64,3088]{1,0:T(8,128)S(1)}, f32[64,3088]{1,0:T(8,128)}, u32[]{:S(2)}) copy-start(f32[64,3088]{1,0:T(8,128)} %get-tuple-element.27) | copy-start | bytes 2371588
  266.3 2.7 %copy-start.8 = (f32[1272,64]{0,1:T(8,128)S(1)}, f32[1272,64]{0,1:T(8,128)}, u32[]{:S(2)}) copy-start(f32[1272,64]{0,1:T(8,128)} %param.27) | copy-start | bytes 976900
  266.3 2.7 %copy-start.9 = (f32[1272,64]{0,1:T(8,128)S(1)}, f32[1272,64]{0,1:T(8,128)}, u32[]{:S(2)}) copy-start(f32[1272,64]{0,1:T(8,128)} %param.28) | copy-start | bytes 976900
  266.3 2.7 %copy-start.10 = (f32[1272,64]{0,1:T(8,128)S(1)}, f32[1272,64]{0,1:T(8,128)}, u32[]{:S(2)}) copy-start(f32[1272,64]{0,1:T(8,128)} %param.29) | copy-start | bytes 976900
  266.3 2.7 %copy-start.11 = (f32[64,1272]{1,0:T(8,128)S(1)}, f32[64,1272]{1,0:T(8,128)}, u32[]{:S(2)}) copy-start(f32[64,1272]{1,0:T(8,128)} %get-tuple-element.26) | copy-start | bytes 976900

commit v5 on v4

--- a/solution.py
+++ b/solution.py
@@ -862,6 +862,8 @@
         if j < 2:
             pump(11 + j)
 
+    for k in range(8):
+        sends_done(k)
     for ch in range(2):
         need(8 + 2 * ch)
         need(9 + 2 * ch)
@@ -1136,6 +1138,8 @@
                 stage(t - lag)
                 if stage is stage_4:
                     send_result(t - lag)
+                    if 2 <= t - lag < 11:
+                        sums_done(t - lag - 2)
 
     def grad_tiles(k, left, right):
         @pl.loop(0, 4)
@@ -1155,7 +1159,7 @@
             if 2 * ch + rh < LEAD:
                 s1(2 * ch + rh)
 
-    for k in range(CHUNKS):
+    for k in range(8, CHUNKS):
         sends_done(k)
 
     @pl.loop(0, 16)
@@ -1403,23 +1407,11 @@
 
     mine = NSR.at[pl.ds(c * 16, 16)]
     peers_send(6, lambda p: NSS, mine)
-    peers_wait(6, lambda p: NSS, mine)
-
-    @pl.loop(0, 16)
-    def _(k):
-        far_copy(k, o * 16 + k).wait()
-
-    totals = jnp.sum(NSR[...], axis=0)
-    norm = jnp.sqrt(totals[0:1])
-    stats[...] = totals
-    stats[0:1, :] = norm
-    stats[2:3, :] = clip_limit / jnp.maximum(norm, clip_limit)
-
     mod_out.wait()
     for i in range(27):
         for copy in result_copies(i):
             copy.wait()
-    for u in range(NU):
+    for u in range(9, NU):
         sums_done(u)
     twin_copy(0, ATI.at[c], ATI.at[c]).wait_send()
     twin_copy(1, MIX.at[c], MIX.at[c]).wait_send()
@@ -1435,6 +1427,18 @@
     twin_copy(15, DTA.at[c], DTA.at[c]).wait_send()
     twin_copy(16, CP.at[c], CP.at[c]).wait_send()
     twin_copy(17, E1.at[c], E1.at[c]).wait_send()
+
+    peers_wait(6, lambda p: NSS, mine)
+
+    @pl.loop(0, 16)
+    def _(k):
+        far_copy(k, o * 16 + k).wait()
+
+    totals = jnp.sum(NSR[...], axis=0)
+    norm = jnp.sqrt(totals[0:1])
+    stats[...] = totals
+    stats[0:1, :] = norm
+    stats[2:3, :] = clip_limit / jnp.maximum(norm, clip_limit)
 
 
 def fused_step(msg, noisy, noise, pos, block_in, block_out, entry, exit_):
@@ -1479,6 +1483,57 @@
     )(msg, noisy, noise, pos, block_in, block_out, entry, exit_)
 
 
+def adam_kernel(stats, *refs):
+    ins, (loss, grad_norm), outs = refs[:16], refs[16:18], refs[18:]
+    factor = stats[2, 0]
+    loss[0, 0] = stats[1, 0]
+    grad_norm[0, 0] = stats[0, 0]
+    corr = 1.0 - 0.5**STEP
+
+    def update(i, rate):
+        weight, first, second, grad = (r[...] for r in ins[4 * i : 4 * i + 4])
+        clipped = grad * factor
+        first_new = 0.5 * first + 0.5 * clipped
+        second_new = 0.5 * second + 0.5 * clipped * clipped
+        change = first_new * (1.0 / corr) / (jnp.sqrt(second_new * (1.0 / corr)) + adam_eps)
+        weight_new = weight - rate * (change + decay_rate * weight)
+        for ref, value in zip(outs[4 * i : 4 * i + 4], (weight_new, first_new, second_new, weight_new)):
+            ref[...] = value.astype(ref.dtype)
+
+    update(0, rate_main)
+    update(1, rate_main)
+    update(2, rate_edge)
+    update(3, rate_main)
+
+
+def adam_all(stats, *groups):
+    steps = 4
+    specs = []
+    for i, group in enumerate(groups):
+        rows, cols = group[0].shape
+        if i == 0:
+            specs.append(pl.BlockSpec((rows, cols // steps), lambda t: (0, t)))
+        elif i == 1:
+            specs.append(pl.BlockSpec((rows // steps, cols), lambda t: (t, 0)))
+        else:
+            specs.append(pl.BlockSpec((rows // steps, cols), lambda t: (t, 0)))
+    scalar = pl.BlockSpec(memory_space=pltpu.SMEM)
+    shape = jax.ShapeDtypeStruct
+    count = sum(group[0].size for group in groups)
+    return pl.pallas_call(
+        adam_kernel,
+        grid=(steps,),
+        out_shape=(
+            shape((1, 1), F32), shape((1, 1), F32),
+            *(shape(group[0].shape, d) for group in groups for d in (F32, F32, F32, BF)),
+        ),
+        in_specs=[scalar, *(spec for spec in specs for _ in range(4))],
+        out_specs=(scalar, scalar, *(spec for spec in specs for _ in range(4))),
+        compiler_params=pltpu.CompilerParams(vmem_limit_bytes=62 * 2**20),
+        cost_estimate=pl.CostEstimate(flops=20 * count, bytes_accessed=30 * count, transcendentals=2 * count),
+    )(stats, *(a for group in groups for a in group))
+
+
 def local_fused(
     noisy, timesteps, labels, noise,
     block_in, block_in_first, block_in_second,
@@ -1500,17 +1555,16 @@
     g_in, g_out, g_entry, g_exit, stats = fused_step(
         head, noisy.reshape(-1, side), noise.reshape(-1, side), pos, block_in[0], block_out[0], entry_table.T, exit_proj
     )
-    loss = stats[1, 0]
-    grad_norm, factor = stats[0, 0], stats[2, 0]
-    outs = [loss, grad_norm]
-    for weight, first, second, grad, rate in (
-        (block_in, block_in_first, block_in_second, g_in[None], rate_main),
-        (block_out, block_out_first, block_out_second, g_out[None], rate_main),
-        (entry_table, entry_first, entry_second, g_entry.T, rate_edge),
-        (exit_proj, exit_first, exit_second, g_exit, rate_main),
-    ):
-        outs.extend(adam_step(weight, first, second, grad, factor, rate))
-    return tuple(outs)
+    loss, grad_norm, *new = adam_all(
+        stats,
+        (block_in[0], block_in_first[0], block_in_second[0], g_in),
+        (block_out[0], block_out_first[0], block_out_second[0], g_out),
+        (entry_table.T, entry_first.T, entry_second.T, g_entry),
+        (exit_proj, exit_first, exit_second, g_exit),
+    )
+    return (
+        loss[0, 0], grad_norm[0, 0], *(a[None] for a in new[:8]), *(a.T for a in new[8:12]), *new[12:]
+    )
 
 
 def solution(mesh):

time: 271 us -> 266 us (0.982)
  other arithmetic: 19.1 us -> 0.72 us
  Pallas kernels: 248 us -> 263 us
    convert_element_type x4 -> x0, other arithmetic: 18.4 us -> none  [adam_step(): return (weight_new, first_new, second_new, weight_new.astype(jnp.bfloat16))]
    pallas_call x0 -> x1, Pallas kernels: none -> 15.2 us  [adam_all(): pl.pallas_call(adam_kernel, grid=(steps,), out_shape=(shape((1, 1), F32),...]
where the time goes in v5:
time: 266 us
  Pallas kernels  263 us (99%)
    pallas_call x1, Pallas kernels, fused_step(): pl.pallas_call(step_kernel, out_shape=(shape(block_in.shape, F32), shape(...  247 us
    pallas_call x1, Pallas kernels, adam_all(): pl.pallas_call(adam_kernel, grid=(steps,), out_shape=(shape((1, 1), F32),...  15.2 us

profile of v5, /device:TPU:0, one launch (start us, length us, event | category | flops | bytes accessed | tf_op | source)
XLA Modules:
  0.0 265.6 jit_solution(8984781767244560583)
XLA Ops:
  2.0 0.1 pad.3.clone
  2.1 0.1 sine_convert_fusion
  2.1 0.7 maximum_maximum_fusion.msg
  2.8 247.5 %shard_map.304 = (f32[64,14336]{1,0:T(8,128)}, f32[256,1024]{1,0:T(8,128)}, f32[64,1272]{1,0:T(8,128)}, f32[64,3088]{1,0:T(8,128)}, f32[8,128]{1,0:T(8,128)}) custom-call(f32[8,128]{1,0:T(8,128)} %maximum_maximum_fusion.msg, f32[128,32]{1,0:T(8,128)} %bitcast.53, f32[128,32]{1,0:T(8,128)} %bitcast.54, f32[16,512]{1,0:T(8,128)} %constant.22.clone.pos, ...), custom_call_target="tpu_custom_call" | custom-call | flops 20999999488 | bytes 20000000 | tf_op jit(solution)/shard_map/pallas_call | solution.py:1470
  250.3 15.2 %shard_map.305 = (f32[1,1]{1,0:T(1,128)}, f32[1,1]{1,0:T(1,128)}, f32[64,14336]{1,0:T(8,128)}, f32[64,14336]{1,0:T(8,128)}, f32[64,14336]{1,0:T(8,128)}, /*index...) custom-call(f32[8,128]{1,0:T(8,128)} %get-tuple-element.41.stats, ...), custom_call_target="tpu_custom_call" | custom-call | flops 29173760 | bytes 43760640 | tf_op jit(solution)/shard_map/pallas_call | solution.py:1523
  (4 shorter events, 0.0 us)

commit v6 on v5

--- a/solution.py
+++ b/solution.py
@@ -369,7 +369,7 @@
 F32 = jnp.float32
 MESH = pl.DeviceIdType.MESH
 TOK = 256
-TILE = 128
+TILE = 256
 LANES = 128
 CHUNKS = 12
 START = (4, 2)
@@ -378,7 +378,7 @@
 VIA_Z = (1, 3, 5, 7, 9, 11)
 SUM_VIA_Z = (0, 2, 4, 6, 8)
 LEAD = 3
-LAGS = (0, 2, 3, 4)
+LAGS = (0, 2, 4, 5)
 LAG_A = 1
 UNITS = tuple((k, 0, 64) for k in (8, 9, 10, 11, 4, 5, 6, 7, 3, 0, 1)) + tuple((2, 16 * i, 16) for i in range(4))
 NU = len(UNITS)
@@ -523,7 +523,7 @@
     pieces.append((ex_in, EX))
     pieces.append((bi.at[:, pl.ds(0, 6144)], WMOD))
     local = [pltpu.make_async_copy(p, q, st_sem.at[i]) for i, (p, q) in enumerate(pieces)]
-    for i in (24, 25, 0, 1, 2, 3, *range(4, 24), 26):
+    for i in (0, 1, 2, 3, 24, 25, *range(4, 24), 26):
         local[i].start()
 
     barrier = pltpu.get_barrier_semaphore()
@@ -535,6 +535,10 @@
     @pl.loop(0, 16)
     def _(k):
         pl.semaphore_signal(barrier, 1, device_id=dev(o, k), device_id_type=MESH)
+
+    for k in range(START[0]):
+        local[k].wait()
+        W[k, z, y, x] = FIN[k].astype(BF)
 
     pl.semaphore_wait(barrier, 31)
 
@@ -665,10 +669,9 @@
                 a_copy(k, (z + dz) % 4, far).wait_recv()
 
     def cast(k):
-        if k < 4:
-            local[k].wait()
-            W[k, z, y, x] = FIN[k].astype(BF)
-        elif k < 8:
+        if k < START[0]:
+            return
+        if k < 8:
             if k == 4:
                 for i in range(4, 20):
                     local[i].wait()
@@ -1172,6 +1175,7 @@
         GD[lat, :, cols] = (total * GD[lat, :, cols].astype(F32)).astype(BF)
 
     pl.semaphore_signal(cred_a, 1, device_id=nb_a, device_id_type=MESH)
+    step(0)
 
     def data_back(first_k, count, left, i):
         for ch in range(2):
@@ -1198,13 +1202,13 @@
     for dz in range(1, 4):
         pl.semaphore_signal(cred_z, 1, device_id=dev(c, chip_of((z + dz) % 4, y, x)), device_id_type=MESH)
 
-    step(0)
     for j in range(4):
         grad_tiles(
             4 + j,
             lambda r: MLI[:, :, rows_at(r, 256)].reshape(512, 256),
             GD[:, :, j * 512 : j * 512 + 512].reshape(512, 512),
         )
+    step(1)
     received(7)
 
     @pl.loop(0, TOK // TILE)
@@ -1238,7 +1242,7 @@
     def _(n):
         DMX[c, :, rows_at(n, 256)] = mixed_back(c, n)
 
-    step(1)
+    step(2)
     twin_copy(9, DAO.at[o, :, dao_mine], DAO.at[o, :, dao_mine]).wait_recv()
 
     @pl.loop(0, 4)
@@ -1265,7 +1269,7 @@
 
     for half in range(2):
         pl.loop(4 * half, 4 * half + 4)(attention_back)
-        step(2 + half)
+        step(3 + half)
     for ch in range(2):
         twin_copy(7 + ch, SND.at[ch], RCV.at[ch]).wait_send()
     data_back(0, 3, lambda j, lat: QKV[j, lat], 11)
@@ -1297,7 +1301,6 @@
         B3S[q] = jnp.concatenate([GLP[0:16, cols], GLP[16:32, cols]], axis=1).astype(BF)
     B3R[s] = B3S[s]
     peers_send(4, lambda p: B3S.at[p], B3R)
-    step(4)
     step(5)
     step(6)
     peers_wait(3, lambda p: DMB.at[c, s], DMB.at[c])
@@ -1507,7 +1510,7 @@
 
 
 def adam_all(stats, *groups):
-    steps = 4
+    steps = 2
     specs = []
     for i, group in enumerate(groups):
         rows, cols = group[0].shape

time: 266 us -> 263 us (0.989)
  Pallas kernels: 263 us -> 260 us
where the time goes in v6:
time: 263 us
  Pallas kernels  260 us (99%)
    pallas_call x1, Pallas kernels, fused_step(): pl.pallas_call(step_kernel, out_shape=(shape(block_in.shape, F32), shape(...  245 us
    pallas_call x1, Pallas kernels, adam_all(): pl.pallas_call(adam_kernel, grid=(steps,), out_shape=(shape((1, 1), F32),...  14.4 us

profile of v6, /device:TPU:0, one launch (start us, length us, event | category | flops | bytes accessed | tf_op | source)
XLA Modules:
  0.0 262.5 jit_solution(9438666868543651310)
XLA Ops:
  2.0 0.1 pad.3.clone
  2.1 0.1 sine_convert_fusion
  2.1 0.7 maximum_maximum_fusion.msg
  2.8 245.1 %shard_map.304 = (f32[64,14336]{1,0:T(8,128)}, f32[256,1024]{1,0:T(8,128)}, f32[64,1272]{1,0:T(8,128)}, f32[64,3088]{1,0:T(8,128)}, f32[8,128]{1,0:T(8,128)}) custom-call(f32[8,128]{1,0:T(8,128)} %maximum_maximum_fusion.msg, f32[128,32]{1,0:T(8,128)} %bitcast.53, f32[128,32]{1,0:T(8,128)} %bitcast.54, f32[16,512]{1,0:T(8,128)} %constant.22.clone.pos, ...), custom_call_target="tpu_custom_call" | custom-call | flops 20999999488 | bytes 20000000 | tf_op jit(solution)/shard_map/pallas_call | solution.py:1473
  248.0 14.4 %shard_map.305 = (f32[1,1]{1,0:T(1,128)}, f32[1,1]{1,0:T(1,128)}, f32[64,14336]{1,0:T(8,128)}, f32[64,14336]{1,0:T(8,128)}, f32[64,14336]{1,0:T(8,128)}, /*index...) custom-call(f32[8,128]{1,0:T(8,128)} %get-tuple-element.41.stats, ...), custom_call_target="tpu_custom_call" | custom-call | flops 29173760 | bytes 43760640 | tf_op jit(solution)/shard_map/pallas_call | solution.py:1526
  (4 shorter events, 0.0 us)
